TPU v7x, 32 devices: a whole 2x2x4 slice. The times are simulated.
32 devices in a mesh: dp: 8 (over y, x, core), ctx: 4 (over z).
Axes of the slice: x: 2, y: 2, z: 4, core: 2. Of those that a mesh axis runs over, the one named last changes fastest.
Arguments:
- layer_in: bfloat16 [8, 1024, 1536], P('dp', 'ctx'), may hold values from -6 to 6
- seg_ids: int32 [8, 1024], P('dp'), may hold values from 0 to 1, as said below
- route_ids: int32 [8, 1024, 6], P('dp', 'ctx'), may hold values from 0 to 31, all different within a row; in each aligned block of 256 rows (0 to 255, 256 to 511, ..., all dimensions but the last counted through in order) at most 60 rows name the same one
- out_grad: bfloat16 [8, 1024, 1536], P('dp', 'ctx'), may hold values from -6 to 6
- norm_in: bfloat16 [1536], P(('dp', 'ctx')), may hold values from 0.5 to 1.5
- w_in: bfloat16 [1536, 6448], P(('dp', 'ctx')), may hold values from -0.15625 to 0.15625
- conv_w: bfloat16 [4, 3328], P(None, ('dp', 'ctx')), may hold values from -3 to 3
- conv_b: bfloat16 [3328], P(('dp', 'ctx')), may hold values from -2 to 2
- dt_bias: float32 [48], replicated, may hold values from -1 to 1
- a_log: float32 [48], replicated, may hold values from -7 to -2
- d_skip: float32 [48], replicated, may hold values from 0.5 to 1.5
- norm_gate: bfloat16 [3072], P(('dp', 'ctx')), may hold values from 0.5 to 1.5
- w_out: bfloat16 [3072, 1536], P(('dp', 'ctx')), may hold values from -0.109375 to 0.109375
- norm_mid: bfloat16 [1536], P(('dp', 'ctx')), may hold values from 0.5 to 1.5
- w_router: bfloat16 [1536, 32], P(('dp', 'ctx')), may hold values from -0.078125 to 0.078125
- w_sgate: bfloat16 [1536, 1024], P(('dp', 'ctx')), may hold values from -0.15625 to 0.15625
- w_sup: bfloat16 [1536, 1024], P(('dp', 'ctx')), may hold values from -0.15625 to 0.15625
- w_sdown: bfloat16 [1024, 1536], P(('dp', 'ctx')), may hold values from -0.1875 to 0.1875
- e_gate: bfloat16 [32, 1536, 512], P('dp', 'ctx'), may hold values from -0.15625 to 0.15625
- e_up: bfloat16 [32, 1536, 512], P('dp', 'ctx'), may hold values from -0.15625 to 0.15625
- e_down: bfloat16 [32, 512, 1536], P('dp', None, 'ctx'), may hold values from -0.25 to 0.25
Outputs:
- layer_out: bfloat16 [8, 1024, 1536], P('dp', 'ctx')
- grad_in: float32 [8, 1024, 1536], P('dp', 'ctx')
- grad_norm_in: float32 [1536], P(('dp', 'ctx'))
- grad_w_in: float32 [1536, 6448], P(('dp', 'ctx'))
- grad_conv_w: float32 [4, 3328], P(None, ('dp', 'ctx'))
- grad_conv_b: float32 [3328], P(('dp', 'ctx'))
- grad_dt_bias: float32 [48], replicated
- grad_a_log: float32 [48], replicated
- grad_d_skip: float32 [48], replicated
- grad_norm_gate: float32 [3072], P(('dp', 'ctx'))
- grad_w_out: float32 [3072, 1536], P(('dp', 'ctx'))
- grad_norm_mid: float32 [1536], P(('dp', 'ctx'))
- grad_w_router: float32 [1536, 32], P(('dp', 'ctx'))
- grad_w_sgate: float32 [1536, 1024], P(('dp', 'ctx'))
- grad_w_sup: float32 [1536, 1024], P(('dp', 'ctx'))
- grad_w_sdown: float32 [1024, 1536], P(('dp', 'ctx'))
- grad_e_gate: float32 [32, 1536, 512], P('dp', 'ctx')
- grad_e_up: float32 [32, 1536, 512], P('dp', 'ctx')
- grad_e_down: float32 [32, 512, 1536], P('dp', None, 'ctx')
Inputs may be any that keep to these rules, and one draw needn't show every extreme that they name: `seg_ids`: within a sequence the numbers start at 0 and rise by one at the first token of each further document; at most one document starts in each aligned span of 64 tokens, and none in the first span. In every group of 1 sequence that one index of dp holds, one sequence has exactly two documents, the second starting in its last aligned span of 64 tokens and after the first of its last 256 tokens; if 1 > 1 another sequence starts a document in every span after the first. `route_ids`: the 6 routes of a token differ. In each aligned block of 256 tokens (one sequence's tokens on one index of ctx), no expert is named by more than 60 routes, a bound that some block reaches.
All inputs are finite; a program needn't handle non-finite values.
Results may differ from a plain program's by a relative error of at most 0.015.
Values may be sent and summed in bfloat16 or wider, within the bound.
A program may use at most 320 MiB of HBM per device.

v0:
```python
from functools import partial

import jax
import jax.numpy as jnp
from jax import lax
from jax.sharding import PartitionSpec as P

HEADS = 48
HEAD = 64
STATE = 128
TOP = 6
EXP_DEV = 4
DI = 3072
CONV = 3328
PROJ = 6448


def from_behind(value, axis, steps):
    count = lax.axis_size(axis)
    leading, last = (max(0, -steps), min(count, count - steps))
    return lax.ppermute(value, axis, [(source, source + steps) for source in range(leading, last)])


def carried_in_2(x, axis, combine, identity):
    count, mine = (lax.axis_size(axis), lax.axis_index(axis))
    everything = jax.tree.map(
        lambda part, kind: lax.all_gather(part.astype(kind), axis), x, (jnp.bfloat16, jnp.bfloat16)
    )
    start = jax.tree.map(
        lambda part, zero: jnp.broadcast_to(jnp.asarray(zero, part.dtype), part.shape), x, identity
    )

    def lap(k, before):
        reached = k < mine
        new = combine(
            before, jax.tree.map(lambda part, own: part[k].astype(own.dtype), everything, x)
        )
        return jax.tree.map(lambda a, b: jnp.where(reached, a, b), new, before)

    return lax.fori_loop(0, count, lap, start)


def carried_in_3(x, axis, combine, identity):
    count, mine = (lax.axis_size(axis), lax.axis_index(axis))
    everything = jax.tree.map(
        lambda part, kind: lax.all_gather(part.astype(kind), axis),
        x,
        jax.tree.map(lambda a: jnp.bfloat16 if a.dtype == jnp.float32 else a.dtype, x),
    )
    start = jax.tree.map(
        lambda part, zero: jnp.broadcast_to(jnp.asarray(zero, part.dtype), part.shape), x, identity
    )

    def lap(k, before):
        at = count - 1 - k
        reached = at > mine
        new = combine(
            before, jax.tree.map(lambda part, own: part[at].astype(own.dtype), everything, x)
        )
        return jax.tree.map(lambda a, b: jnp.where(reached, a, b), new, before)

    return lax.fori_loop(0, count, lap, start)


def for_sending(x):
    return jax.tree.map(lambda a: a.astype(jnp.bfloat16) if a.dtype == jnp.float32 else a, x)


def normalize(value):
    return value * lax.rsqrt(jnp.mean(value * value, axis=-1, keepdims=True) + 1e-05)


def scaled_norm(value, gain):
    return normalize(value) * gain


def gate_norm(y_heads, z_part, gain):
    joined = y_heads.reshape(z_part.shape) * jax.nn.silu(z_part)
    return normalize(joined) * gain


def silu_slope(value):
    squashed = jax.nn.sigmoid(value)
    return squashed * (1.0 + value * (1.0 - squashed))


def conv_apply(padded, weight, bias, seg_pad):
    tap_count = weight.shape[0]
    length = padded.shape[1] - tap_count + 1
    current = seg_pad[:, tap_count - 1 :]
    summed = bias + jnp.zeros(padded[:, tap_count - 1 :].shape, jnp.float32)
    for offset in range(tap_count):
        matches = (seg_pad[:, offset : offset + length] == current).astype(jnp.float32)
        summed = summed + weight[offset] * padded[:, offset : offset + length] * matches[..., None]
    return jax.nn.silu(summed)


def split_blocks(value, count):
    shaped = value.reshape((value.shape[0], count, value.shape[1] // count) + value.shape[2:])
    return jnp.moveaxis(shaped, 1, 0)


def block_step(carried_in, pieces):
    memory, previous = carried_in
    x_heads, b_mat, c_mat, dt_pos, decay, segment_ids = pieces
    cumul = jnp.cumsum(decay, axis=1)
    places = jnp.arange(segment_ids.shape[1])
    causal = places[:, None] >= places[None, :]
    linked = ((segment_ids[:, :, None] == segment_ids[:, None, :]) & causal[None])[..., None]
    spread = cumul[:, :, None, :] - cumul[:, None, :, :]
    weights = jnp.where(linked, jnp.exp(jnp.where(linked, spread, 0.0)), 0.0)
    inner = jnp.einsum("gtn,gsn->gts", c_mat, b_mat, precision=lax.Precision.HIGHEST)
    weights = weights * inner[..., None] * dt_pos[:, None, :, :]
    output = jnp.einsum("gtsh,gshp->gthp", weights, x_heads, precision=lax.Precision.HIGHEST)
    keeps = (segment_ids == previous[:, None]).astype(jnp.float32)
    reach = jnp.exp(cumul) * keeps[..., None]
    output = (
        output
        + jnp.einsum("gtn,ghpn->gthp", c_mat, memory, precision=lax.Precision.HIGHEST)
        * reach[..., None]
    )
    latest = segment_ids[:, -1]
    tails = (
        jnp.exp(cumul[:, -1:, :] - cumul)
        * (segment_ids == latest[:, None]).astype(jnp.float32)[..., None]
        * dt_pos
    )
    through = jnp.exp(cumul[:, -1, :]) * (latest == previous).astype(jnp.float32)[:, None]
    memory = memory * through[..., None, None] + jnp.einsum(
        "gsh,gshp,gsn->ghpn", tails, x_heads, b_mat, precision=lax.Precision.HIGHEST
    )
    return ((memory, latest), output)


def scan_blocks(x_heads, b_mat, c_mat, dt_pos, decay, segment_ids, memory, previous):
    length = segment_ids.shape[1]
    count = length // min(128, length)
    inputs = tuple(
        (
            split_blocks(value, count)
            for value in (x_heads, b_mat, c_mat, dt_pos, decay, segment_ids)
        )
    )
    (memory, latest), outputs = lax.scan(jax.checkpoint(block_step), (memory, previous), inputs)
    return (jnp.moveaxis(outputs, 0, 1).reshape(x_heads.shape), memory)


def part_local(x_heads, b_mat, c_mat, dt_raw, dt_bias, a_log, d_skip, segment_ids, previous):
    dt_pos = jax.nn.softplus(dt_raw + dt_bias)
    decay = -jnp.exp(a_log) * dt_pos
    zero_state = jnp.zeros((x_heads.shape[0], HEADS, HEAD, STATE), jnp.float32)
    mixed_heads, final_state = scan_blocks(
        x_heads, b_mat, c_mat, dt_pos, decay, segment_ids, zero_state, previous
    )
    y_local = mixed_heads + d_skip[:, None] * x_heads
    through = (
        jnp.exp(jnp.sum(decay, axis=1))
        * (segment_ids[:, -1] == previous).astype(jnp.float32)[:, None]
    )
    return (y_local, final_state, through)


def part_carry(c_mat, dt_raw, dt_bias, a_log, state_in, segment_ids, previous):
    dt_pos = jax.nn.softplus(dt_raw + dt_bias)
    cumul = jnp.cumsum(-jnp.exp(a_log) * dt_pos, axis=1)
    keeps = (segment_ids == previous[:, None]).astype(jnp.float32)
    reach = jnp.exp(cumul) * keeps[..., None]
    return (
        jnp.einsum("gtn,ghpn->gthp", c_mat, state_in, precision=lax.Precision.HIGHEST)
        * reach[..., None]
    )


def carry_forward(earlier, later):
    return (earlier[0] * later[0], later[0][..., None, None] * earlier[1] + later[1])


def carry_backward(earlier, later):
    return (earlier[0] * later[0], later[1] + later[0][..., None, None] * earlier[1])


def route_slots(flat_routes, expert_count, capacity):
    blocks = flat_routes.shape[0]
    onehot = (flat_routes[..., None] == jnp.arange(expert_count, dtype=jnp.int32)).astype(jnp.int32)
    ranks = jnp.sum((jnp.cumsum(onehot, axis=1) - onehot) * onehot, axis=-1)
    spots = (
        flat_routes * (blocks * capacity)
        + jnp.arange(blocks, dtype=jnp.int32)[:, None] * capacity
        + ranks
    )
    return spots


def times_rows(left, right):
    return lax.dot_general(
        left, right, (((0,), (0,)), ((), ())), preferred_element_type=jnp.float32
    )


def times_back(left, right):
    return lax.dot_general(
        left, right, (((1,), (1,)), ((), ())), preferred_element_type=jnp.float32
    )


def on_device(
    layer_in,
    seg_ids,
    route_ids,
    out_grad,
    norm_in,
    w_in,
    conv_w,
    conv_b,
    dt_bias,
    a_log,
    d_skip,
    norm_gate,
    w_out,
    norm_mid,
    w_router,
    w_sgate,
    w_sup,
    w_sdown,
    e_gate,
    e_up,
    e_down,
):
    seq_count, row_count, d_model = layer_in.shape
    token_count = seq_count * row_count
    tap_count = conv_w.shape[0]
    ctx_place = lax.axis_index("ctx")
    expert_count = EXP_DEV * lax.axis_size("dp")
    capacity = row_count * TOP * 5 // (expert_count * 4)
    dense_set = (
        lax.all_gather(norm_in, ("dp", "ctx"), axis=0, tiled=True),
        lax.all_gather(w_in, ("dp", "ctx"), axis=0, tiled=True),
        lax.all_gather(conv_w, ("dp", "ctx"), axis=1, tiled=True),
        lax.all_gather(conv_b, ("dp", "ctx"), axis=0, tiled=True),
        lax.all_gather(norm_gate, ("dp", "ctx"), axis=0, tiled=True),
        lax.all_gather(w_out, ("dp", "ctx"), axis=0, tiled=True),
        lax.all_gather(norm_mid, ("dp", "ctx"), axis=0, tiled=True),
        lax.all_gather(w_router, ("dp", "ctx"), axis=0, tiled=True),
        lax.all_gather(w_sgate, ("dp", "ctx"), axis=0, tiled=True),
        lax.all_gather(w_sup, ("dp", "ctx"), axis=0, tiled=True),
        lax.all_gather(w_sdown, ("dp", "ctx"), axis=0, tiled=True),
    )
    (
        gain_in,
        weight_in,
        conv_weight,
        conv_bias,
        gain_gate,
        weight_out,
        gain_mid,
        router_weight,
        sgate_weight,
        sup_weight,
        sdown_weight,
    ) = dense_set
    expert_gate, expert_up, expert_down = (
        lax.all_gather(e_gate, "ctx", axis=1, tiled=True),
        lax.all_gather(e_up, "ctx", axis=1, tiled=True),
        lax.all_gather(e_down, "ctx", axis=2, tiled=True),
    )
    input_f = layer_in.astype(jnp.float32)
    normed_f, pull_in = jax.vjp(scaled_norm, input_f, gain_in.astype(jnp.float32))
    normed = normed_f.astype(jnp.bfloat16).reshape(token_count, d_model)
    projected = jnp.dot(normed, weight_in, preferred_element_type=jnp.float32).reshape(
        seq_count, row_count, PROJ
    )
    z_part = projected[..., :DI]
    xbc_part = projected[..., DI : DI + CONV]
    dt_raw = projected[..., DI + CONV :]
    edge_rows = from_behind(
        xbc_part[:, row_count - tap_count + 1 :, :].astype(jnp.bfloat16), "ctx", 1
    ).astype(jnp.float32)
    seg_pad = jnp.concatenate(
        [jnp.full((seq_count, tap_count - 1), -1, jnp.int32), seg_ids], axis=1
    )
    seg_window = lax.dynamic_slice_in_dim(
        seg_pad, ctx_place * row_count, row_count + tap_count - 1, 1
    )
    seg_now = seg_window[:, tap_count - 1 :]
    seg_before = seg_window[:, tap_count - 2]
    padded = jnp.concatenate([edge_rows, xbc_part], axis=1)
    conv_out, pull_conv = jax.vjp(
        partial(conv_apply, seg_pad=seg_window),
        padded,
        conv_weight.astype(jnp.float32),
        conv_bias.astype(jnp.float32),
    )
    x_heads = conv_out[..., :DI].reshape(seq_count, row_count, HEADS, HEAD)
    b_mat = conv_out[..., DI : DI + STATE]
    c_mat = conv_out[..., DI + STATE :]
    local_piece = partial(part_local, segment_ids=seg_now, previous=seg_before)
    (y_local, state_out, through), pull_local = jax.vjp(
        local_piece, x_heads, b_mat, c_mat, dt_raw, dt_bias, a_log, d_skip
    )
    carried = carried_in_2(
        (through, state_out),
        "ctx",
        carry_forward,
        (jnp.ones_like(through), jnp.zeros_like(state_out)),
    )
    state_in = carried[1]
    carry_piece = partial(part_carry, segment_ids=seg_now, previous=seg_before)
    y_carry, pull_carry = jax.vjp(carry_piece, c_mat, dt_raw, dt_bias, a_log, state_in)
    gated_f, pull_gate = jax.vjp(
        gate_norm, y_local + y_carry, z_part, gain_gate.astype(jnp.float32)
    )
    gated = gated_f.astype(jnp.bfloat16).reshape(token_count, DI)
    mixed = jnp.dot(gated, weight_out, preferred_element_type=jnp.float32)
    resid_mid = input_f.reshape(token_count, d_model) + mixed
    normed_mid_f, pull_mid = jax.vjp(scaled_norm, resid_mid, gain_mid.astype(jnp.float32))
    normed_mid = normed_mid_f.astype(jnp.bfloat16)
    logits = jnp.dot(normed_mid, router_weight, preferred_element_type=jnp.float32)
    route_flat = route_ids.reshape(token_count, TOP)
    gates = jax.nn.softmax(jnp.take_along_axis(logits, route_flat, axis=1), axis=-1)
    shared_gate = jnp.dot(normed_mid, sgate_weight, preferred_element_type=jnp.float32)
    shared_up = jnp.dot(normed_mid, sup_weight, preferred_element_type=jnp.float32)
    shared_act = (jax.nn.silu(shared_gate) * shared_up).astype(jnp.bfloat16)
    shared_out = jnp.dot(shared_act, sdown_weight, preferred_element_type=jnp.float32)
    slot_ids = route_slots(route_ids.reshape(seq_count, row_count * TOP), expert_count, capacity)
    assigned = jnp.arange(token_count * TOP, dtype=jnp.int32)
    owners = (
        jnp.full((expert_count * seq_count * capacity,), token_count * TOP, jnp.int32)
        .at[slot_ids.reshape(-1)]
        .set(assigned)
    )
    token_of = owners // TOP
    rows_pad = jnp.concatenate([normed_mid, jnp.zeros((1, d_model), jnp.bfloat16)], axis=0)
    outgoing = rows_pad[token_of].reshape(expert_count, seq_count * capacity, d_model)
    incoming = lax.all_to_all(outgoing, "dp", split_axis=0, concat_axis=1, tiled=True)
    hidden_gate = jnp.einsum(
        "erd,edf->erf", incoming, expert_gate, preferred_element_type=jnp.float32
    )
    hidden_up = jnp.einsum("erd,edf->erf", incoming, expert_up, preferred_element_type=jnp.float32)
    hidden_act = (jax.nn.silu(hidden_gate) * hidden_up).astype(jnp.bfloat16)
    expert_out = jnp.einsum(
        "erf,efd->erd", hidden_act, expert_down, preferred_element_type=jnp.float32
    ).astype(jnp.bfloat16)
    returned = lax.all_to_all(expert_out, "dp", split_axis=1, concat_axis=0, tiled=True)
    slot_flat = slot_ids.reshape(token_count, TOP)
    picked = returned.reshape(-1, d_model)[slot_flat]
    routed = jnp.sum(gates[..., None] * picked, axis=1)
    layer_out = (
        (resid_mid + shared_out + routed)
        .astype(jnp.bfloat16)
        .reshape(seq_count, row_count, d_model)
    )
    grad_top = out_grad.astype(jnp.float32).reshape(token_count, d_model)
    grad_gates = jnp.sum(picked * grad_top[:, None, :], axis=-1)
    grad_pick = gates * (grad_gates - jnp.sum(gates * grad_gates, axis=-1, keepdims=True))
    expert_ids = jnp.arange(expert_count, dtype=jnp.int32)
    grad_logits = jnp.sum(
        grad_pick[..., None] * (route_flat[..., None] == expert_ids).astype(jnp.float32), axis=1
    ).astype(jnp.bfloat16)
    gates_pad = jnp.concatenate([gates.reshape(-1), jnp.zeros((1,), jnp.float32)])
    grad_pad = jnp.concatenate([grad_top, jnp.zeros((1, d_model), jnp.float32)], axis=0)
    grad_slots = (
        (gates_pad[owners][:, None] * grad_pad[token_of])
        .astype(jnp.bfloat16)
        .reshape(expert_count, seq_count * capacity, d_model)
    )
    grad_arrived = lax.all_to_all(grad_slots, "dp", split_axis=0, concat_axis=1, tiled=True)
    grad_act = jnp.einsum(
        "erd,efd->erf", grad_arrived, expert_down, preferred_element_type=jnp.float32
    )
    grad_e_down = jnp.einsum(
        "erf,erd->efd", hidden_act, grad_arrived, preferred_element_type=jnp.float32
    )
    grad_hgate = (grad_act * hidden_up * silu_slope(hidden_gate)).astype(jnp.bfloat16)
    grad_hup = (grad_act * jax.nn.silu(hidden_gate)).astype(jnp.bfloat16)
    grad_e_gate = jnp.einsum(
        "erd,erf->edf", incoming, grad_hgate, preferred_element_type=jnp.float32
    )
    grad_e_up = jnp.einsum("erd,erf->edf", incoming, grad_hup, preferred_element_type=jnp.float32)
    grad_incoming = jnp.einsum(
        "erf,edf->erd", grad_hgate, expert_gate, preferred_element_type=jnp.float32
    )
    grad_incoming = (
        grad_incoming
        + jnp.einsum("erf,edf->erd", grad_hup, expert_up, preferred_element_type=jnp.float32)
    ).astype(jnp.bfloat16)
    grad_returned = lax.all_to_all(grad_incoming, "dp", split_axis=1, concat_axis=0, tiled=True)
    grad_routed = jnp.sum(grad_returned.reshape(-1, d_model)[slot_flat], axis=1, dtype=jnp.float32)
    dense_set = (
        lax.all_gather(norm_in, ("dp", "ctx"), axis=0, tiled=True),
        lax.all_gather(w_in, ("dp", "ctx"), axis=0, tiled=True),
        lax.all_gather(conv_w, ("dp", "ctx"), axis=1, tiled=True),
        lax.all_gather(conv_b, ("dp", "ctx"), axis=0, tiled=True),
        lax.all_gather(norm_gate, ("dp", "ctx"), axis=0, tiled=True),
        lax.all_gather(w_out, ("dp", "ctx"), axis=0, tiled=True),
        lax.all_gather(norm_mid, ("dp", "ctx"), axis=0, tiled=True),
        lax.all_gather(w_router, ("dp", "ctx"), axis=0, tiled=True),
        lax.all_gather(w_sgate, ("dp", "ctx"), axis=0, tiled=True),
        lax.all_gather(w_sup, ("dp", "ctx"), axis=0, tiled=True),
        lax.all_gather(w_sdown, ("dp", "ctx"), axis=0, tiled=True),
    )
    (
        gain_in,
        weight_in,
        conv_weight,
        conv_bias,
        gain_gate,
        weight_out,
        gain_mid,
        router_weight,
        sgate_weight,
        sup_weight,
        sdown_weight,
    ) = dense_set
    grad_w_router = times_rows(normed_mid, grad_logits)
    grad_shared_out = grad_top.astype(jnp.bfloat16)
    grad_w_sdown = times_rows(shared_act, grad_shared_out)
    grad_shared_act = times_back(grad_shared_out, sdown_weight)
    grad_sgate = (grad_shared_act * shared_up * silu_slope(shared_gate)).astype(jnp.bfloat16)
    grad_sup = (grad_shared_act * jax.nn.silu(shared_gate)).astype(jnp.bfloat16)
    grad_w_sgate = times_rows(normed_mid, grad_sgate)
    grad_w_sup = times_rows(normed_mid, grad_sup)
    grad_mid = (
        grad_routed
        + times_back(grad_logits, router_weight)
        + times_back(grad_sgate, sgate_weight)
        + times_back(grad_sup, sup_weight)
    )
    grad_resid_part, grad_gain_mid = pull_mid(grad_mid)
    grad_resid = grad_top + grad_resid_part
    grad_mixed = grad_resid.astype(jnp.bfloat16)
    grad_w_out = times_rows(gated, grad_mixed)
    grad_gated = times_back(grad_mixed, weight_out).reshape(seq_count, row_count, DI)
    grad_y, grad_z, grad_gain_gate = pull_gate(grad_gated)
    grad_cmat_carry, grad_dt_carry, grad_bias_carry, grad_alog_carry, grad_state_in = pull_carry(
        grad_y
    )
    back_scan = carried_in_3(
        (through, grad_state_in),
        "ctx",
        carry_backward,
        (jnp.ones_like(through), jnp.zeros_like(grad_state_in)),
    )
    grad_state_out = back_scan[1]
    grad_through = jnp.sum(state_in * grad_state_out, axis=(2, 3))
    (
        grad_xheads,
        grad_bmat,
        grad_cmat,
        grad_dt_local,
        grad_bias_local,
        grad_alog_local,
        grad_dskip,
    ) = pull_local((grad_y, grad_state_out, grad_through))
    grad_conv_out = jnp.concatenate(
        [grad_xheads.reshape(seq_count, row_count, DI), grad_bmat, grad_cmat + grad_cmat_carry],
        axis=-1,
    )
    grad_padded, grad_conv_w, grad_conv_b = pull_conv(grad_conv_out)
    edge_grad = from_behind(for_sending(grad_padded[:, : tap_count - 1, :]), "ctx", -1)
    grad_xbc = grad_padded[:, tap_count - 1 :, :]
    grad_xbc = jnp.concatenate(
        [
            grad_xbc[:, : row_count - tap_count + 1],
            grad_xbc[:, row_count - tap_count + 1 :] + edge_grad,
        ],
        axis=1,
    )
    grad_proj = (
        jnp.concatenate([grad_z, grad_xbc, grad_dt_local + grad_dt_carry], axis=-1)
        .astype(jnp.bfloat16)
        .reshape(token_count, PROJ)
    )
    grad_w_in = times_rows(normed, grad_proj)
    grad_normed = times_back(grad_proj, weight_in).reshape(seq_count, row_count, d_model)
    grad_input_part, grad_gain_in = pull_in(grad_normed)
    grad_in = grad_resid.reshape(seq_count, row_count, d_model) + grad_input_part
    dense_grads = (
        lax.psum_scatter(grad_gain_in, ("dp", "ctx"), scatter_dimension=0, tiled=True),
        lax.psum_scatter(grad_w_in, ("dp", "ctx"), scatter_dimension=0, tiled=True),
        lax.psum_scatter(grad_conv_w, ("dp", "ctx"), scatter_dimension=1, tiled=True),
        lax.psum_scatter(grad_conv_b, ("dp", "ctx"), scatter_dimension=0, tiled=True),
        lax.psum_scatter(grad_gain_gate, ("dp", "ctx"), scatter_dimension=0, tiled=True),
        lax.psum_scatter(grad_w_out, ("dp", "ctx"), scatter_dimension=0, tiled=True),
        lax.psum_scatter(grad_gain_mid, ("dp", "ctx"), scatter_dimension=0, tiled=True),
        lax.psum_scatter(grad_w_router, ("dp", "ctx"), scatter_dimension=0, tiled=True),
        lax.psum_scatter(grad_w_sgate, ("dp", "ctx"), scatter_dimension=0, tiled=True),
        lax.psum_scatter(grad_w_sup, ("dp", "ctx"), scatter_dimension=0, tiled=True),
        lax.psum_scatter(grad_w_sdown, ("dp", "ctx"), scatter_dimension=0, tiled=True),
    )
    expert_grads = (
        lax.psum_scatter(
            grad_e_gate.astype(jnp.bfloat16), "ctx", scatter_dimension=1, tiled=True
        ).astype(jnp.float32),
        lax.psum_scatter(
            grad_e_up.astype(jnp.bfloat16), "ctx", scatter_dimension=1, tiled=True
        ).astype(jnp.float32),
        lax.psum_scatter(
            grad_e_down.astype(jnp.bfloat16), "ctx", scatter_dimension=2, tiled=True
        ).astype(jnp.float32),
    )
    head_grads = lax.psum(
        (grad_bias_local + grad_bias_carry, grad_alog_local + grad_alog_carry, grad_dskip),
        ("dp", "ctx"),
    )
    return (
        layer_out,
        grad_in,
        dense_grads[0],
        dense_grads[1],
        dense_grads[2],
        dense_grads[3],
        head_grads[0],
        head_grads[1],
        head_grads[2],
        dense_grads[4],
        dense_grads[5],
        dense_grads[6],
        dense_grads[7],
        dense_grads[8],
        dense_grads[9],
        dense_grads[10],
        expert_grads[0],
        expert_grads[1],
        expert_grads[2],
    )


def solution(mesh):
    in_specs = (
        P("dp", "ctx", None),
        P("dp", None),
        P("dp", "ctx", None),
        P("dp", "ctx", None),
        P(("dp", "ctx")),
        P(("dp", "ctx"), None),
        P(None, ("dp", "ctx")),
        P(("dp", "ctx")),
        P(),
        P(),
        P(),
        P(("dp", "ctx")),
        P(("dp", "ctx"), None),
        P(("dp", "ctx")),
        P(("dp", "ctx"), None),
        P(("dp", "ctx"), None),
        P(("dp", "ctx"), None),
        P(("dp", "ctx"), None),
        P("dp", "ctx", None),
        P("dp", "ctx", None),
        P("dp", None, "ctx"),
    )
    out_specs = (
        P("dp", "ctx", None),
        P("dp", "ctx", None),
        P(("dp", "ctx")),
        P(("dp", "ctx"), None),
        P(None, ("dp", "ctx")),
        P(("dp", "ctx")),
        P(),
        P(),
        P(),
        P(("dp", "ctx")),
        P(("dp", "ctx"), None),
        P(("dp", "ctx")),
        P(("dp", "ctx"), None),
        P(("dp", "ctx"), None),
        P(("dp", "ctx"), None),
        P(("dp", "ctx"), None),
        P("dp", "ctx", None),
        P("dp", "ctx", None),
        P("dp", None, "ctx"),
    )
    return jax.shard_map(
        on_device, mesh=mesh, in_specs=in_specs, out_specs=out_specs, check_vma=False
    )
```

profile of v0, /device:TPU:0, one launch (start us, length us, event | category | flops | bytes accessed | tf_op | source)
XLA Modules:
  0.0 3179.7 jit_solution(8354905883581156220)
XLA Ops:
  11.4 43.7 %all-reduce.24 = (bf16[1536]{0:T(1024)(128)(2,1)S(1)}, bf16[3328]{0:T(1024)(128)(2,1)S(1)}, bf16[3072]{0:T(1024)(128)(2,1)S(1)}, bf16[1536]{0:T(1024)(128)(2,1)}) all-reduce(bf16[1536]{0:T(1024)(128)(2,1)S(1)} %dynamic-update-slice, bf16[3328]{0:T(1024)(128)(2,1)S(1)} %dynamic-update-slice.1, ...), channel_id=1, replica_groups=mesh['dp'=8,'ctx'=4] {'dp','ctx'}, use_global_device_ids=true, to_apply=%add.13 | all-reduce | flops 9472 | bytes 37888
  55.1 66.5 %all-gather.3 = bf16[32,104,4]{1,2,0:T(4,128)(2,1)S(1)} all-gather(bf16[1,104,4]{1,2,0:T(4,128)(2,1)} %bitcast.787), channel_id=1, replica_groups=mesh['dp'=8,'ctx'=4] {'dp','ctx'}, dimensions={0}, use_global_device_ids=true | all-gather | bytes 27456 | tf_op jit(solution)/shard_map/all_gather | solution.py:238
  128.4 16.9 all-gather.16.cloned.1.call-done
  145.3 14.2 convolution_bitcast_fusion.1
  178.5 26.0 fusion.225
  210.2 10.6 copy.576
  224.8 117.7 %while.76 = (s32[]{:T(128)}, f32[1,48,64,128]{3,2,1,0:T(8,128)S(1)}, s32[1]{0:T(128)}, f32[2,1,128,48,64]{2,0,4,3,1:T(2,128)}, f32[2,1,48,64,128]{4,3,2,1,0:T(8,...) while((s32[]{:T(128)}, ...), condition=%wide.region_3.5_spmd.clone, body=%wide.region_1.4_spmd.clone.sunk | while | flops 1845037568 | bytes 32827252 | solution.py:144
  240.7 36.7 %dynamic_update_slice.88 = f32[2,1,128,48,64]{2,0,4,3,1:T(2,128)} dynamic-update-slice(f32[2,1,128,48,64]{2,0,4,3,1:T(2,128)} %get-tuple-element.1599, f32[1,1,128,48,64]{2,0,4,3,1:T(1,128)S(1)} %bitcast.721, s32[]{:T(128)} %get-tuple-element.1596, s32[]{:T(128)} %constant.255.clone.1..sunk.1, s32[]{:T(128)} %constant.255.clone.1..sunk.1, s32[]{:T(128)} %constant.255.clone.1..sunk.1, ...) | dynamic-update-slice | bytes 3145732 | tf_op jit(solution)/shard_map/jvp()/while/body/jit(dynamic_update_index_in_dim)/dynamic_update_slice | solution.py:144
  299.3 36.7 %dynamic_update_slice.88 = f32[2,1,128,48,64]{2,0,4,3,1:T(2,128)} dynamic-update-slice(f32[2,1,128,48,64]{2,0,4,3,1:T(2,128)} %get-tuple-element.1599, f32[1,1,128,48,64]{2,0,4,3,1:T(1,128)S(1)} %bitcast.721, s32[]{:T(128)} %get-tuple-element.1596, s32[]{:T(128)} %constant.255.clone.1..sunk.1, s32[]{:T(128)} %constant.255.clone.1..sunk.1, s32[]{:T(128)} %constant.255.clone.1..sunk.1, ...) | dynamic-update-slice | bytes 3145732 | tf_op jit(solution)/shard_map/jvp()/while/body/jit(dynamic_update_index_in_dim)/dynamic_update_slice | solution.py:144
  370.5 10.7 all-reduce.15
  427.7 20.0 multiply_reduce_fusion.11
  453.2 36.7 %all-gather.18.cloned.1.call-done = bf16[3072,1536]{1,0:T(8,128)(2,1)} async-done(((bf16[96,1536]{1,0:T(8,128)(2,1)}), bf16[3072,1536]{1,0:T(8,128)(2,1)}) %all-gather.18.cloned.1.call-update) | async-done | bytes 9437200 | tf_op jit(solution)/shard_map/all_gather | solution.py:241
  519.7 75.3 %all-gather.4 = bf16[32,48,32]{1,2,0:T(8,128)(2,1)S(1)} all-gather(bf16[1,48,32]{1,2,0:T(8,128)(2,1)S(1)} %bitcast.784), channel_id=1, replica_groups=mesh['dp'=8,'ctx'=4] {'dp','ctx'}, dimensions={0}, use_global_device_ids=true | all-gather | bytes 101376 | tf_op jit(solution)/shard_map/all_gather | solution.py:243
  606.0 11.2 gather.29
  617.5 12.7 gather_fusion.5
  631.3 10.4 gather_fusion.2
  674.8 51.4 %all-to-all-done.2 = bf16[32,60,1536]{2,1,0:T(8,128)(2,1)} async-done(((bf16[32,60,1536]{2,1,0:T(8,128)(2,1)}), bf16[32,60,1536]{2,1,0:T(8,128)(2,1)}, u32[]{:S(2)}, u32[]{:S(2)}) %all-to-all-start.2) | async-done | bytes 5898272 | tf_op jit(solution)/shard_map/all_to_all | solution.py:366
  746.0 94.5 %all-gather.30.cloned.1.call-done = bf16[4,512,1536]{2,1,0:T(8,128)(2,1)} async-done(((bf16[4,512,384]{2,1,0:T(8,128)(2,1)}), bf16[4,512,1536]{2,1,0:T(8,128)(2,1)}) %all-gather.30.cloned.1.call-update) | async-done | bytes 6291472 | tf_op jit(solution)/shard_map/all_gather | solution.py:264
  840.5 13.9 multiply_convert_fusion.1
  874.0 11.0 fusion.230
  885.0 12.6 add_convert_fusion
  907.4 39.5 %all-to-all-done.1 = bf16[4,480,1536]{2,0,1:T(4,128)(2,1)} async-done(((bf16[4,480,1536]{2,0,1:T(4,128)(2,1)}), bf16[4,480,1536]{2,0,1:T(4,128)(2,1)}, u32[]{:S(2)}, u32[]{:S(2)}) %all-to-all-start.1) | async-done | bytes 5898272 | tf_op jit(solution)/shard_map/all_to_all | solution.py:343
  964.8 36.6 %all-gather.22.cloned.1.call-done = bf16[1536,1024]{1,0:T(8,128)(2,1)} async-done(((bf16[48,1024]{1,0:T(8,128)(2,1)}), bf16[1536,1024]{1,0:T(8,128)(2,1)}) %all-gather.22.cloned.1.call-update) | async-done | bytes 3145744 | tf_op jit(solution)/shard_map/all_gather | solution.py:245
  1005.3 56.0 %all-gather.24.cloned.1.call-done = bf16[1024,1536]{1,0:T(8,128)(2,1)} async-done(((bf16[32,1536]{1,0:T(8,128)(2,1)}), bf16[1024,1536]{1,0:T(8,128)(2,1)}) %all-gather.24.cloned.1.call-update) | async-done | bytes 3145744 | tf_op jit(solution)/shard_map/all_gather | solution.py:246
  1080.7 13.8 gather_fusion.1
  1103.5 10.2 multiply_reduce_fusion.2
  1129.0 14.2 gather_fusion.4
  1177.2 14.1 multiply_reduce_fusion.9
  1213.7 10.8 copy.617
  1251.3 24.0 all-gather.34.cloned.1.call-done
  1291.1 212.5 %while.75 = (s32[]{:T(128)}, f32[1,48,64,128]{3,2,1,0:T(8,128)S(1)}, f32[2,1,128,48,64]{2,0,1,4,3:T(2,128)}, f32[2,1,128,128]{3,2,0,1:T(8,128)}, f32[2,1,128,128...) while((s32[]{:T(128)}, ...), condition=%wide.region_36.38_spmd, body=%wide.region_26.37_spmd.sunk | while | flops 4325945856 | bytes 86226888 | solution.py:144
  1360.9 36.8 %dynamic_update_slice.86 = f32[2,1,128,48,64]{2,0,1,4,3:T(2,128)} dynamic-update-slice(f32[2,1,128,48,64]{2,0,1,4,3:T(2,128)} %get-tuple-element.1695, f32[1,1,128,48,64]{2,0,1,4,3:T(1,128)} %bitcast.723, s32[]{:T(128)S(6)} %sub.382, s32[]{:T(128)} %constant.255.clone.1..sunk, s32[]{:T(128)} %constant.255.clone.1..sunk, s32[]{:T(128)} %constant.255.clone.1..sunk, s32[]{:T(128)} %constant.255.clone.1..sunk) | dynamic-update-slice | bytes 3145732 | tf_op jit(solution)/shard_map/transpose(jvp())/while/body/jit(dynamic_update_index_in_dim)/dynamic_update_slice | solution.py:144
  1459.1 36.8 %dynamic_update_slice.86 = f32[2,1,128,48,64]{2,0,1,4,3:T(2,128)} dynamic-update-slice(f32[2,1,128,48,64]{2,0,1,4,3:T(2,128)} %get-tuple-element.1695, f32[1,1,128,48,64]{2,0,1,4,3:T(1,128)} %bitcast.723, s32[]{:T(128)S(6)} %sub.382, s32[]{:T(128)} %constant.255.clone.1..sunk, s32[]{:T(128)} %constant.255.clone.1..sunk, s32[]{:T(128)} %constant.255.clone.1..sunk, s32[]{:T(128)} %constant.255.clone.1..sunk) | dynamic-update-slice | bytes 3145732 | tf_op jit(solution)/shard_map/transpose(jvp())/while/body/jit(dynamic_update_index_in_dim)/dynamic_update_slice | solution.py:144
  1503.6 10.6 copy.626
  1528.5 34.4 %multiply_reduce_fusion.6 = (f32[3328]{0:T(1024)}, f32[3328]{0:T(1024)}, f32[3328]{0:T(1024)}, f32[3328]{0:T(1024)}, f32[3328]{0:T(1024)}, /*index=5*/f32[1,256,3328]{2,0,1:T(1,128)S(1)}) fusion(f32[256]{0:T(256)S(1)} %bitcast.780, f32[1,256,3328]{2,0,1:T(1,128)S(1)} %copy-done.13, f32[1,3,3328]{2,0,1:T(1,128)S(1)} %copy-done.72, f32[256]{0:T(256)S(1)} %bitcast.777, ...), kind=kLoop, calls=%fused_computation.212 | loop fusion | flops 19578624 | bytes 17148928 | tf_op jit(solution)/shard_map/transpose(jvp())/reduce_sum | solution.py:94
  1563.0 10.5 broadcast_multiply_fusion
  1610.8 11.9 fusion.155
  1632.5 11.2 copy.662
  1698.1 17.7 fusion.167
  1726.2 154.9 %all-reduce.27.cloned.1.call-done = (f32[1536]{0:T(1024)}, f32[4,3328]{1,0:T(4,128)}, f32[3328]{0:T(1024)}, f32[48]{0:T(128)}, f32[48]{0:T(128)}, /*index=5*/f32[48]{0:T(128)}, f32[3072]{0:T(1024)}, f32[1536]{0:T(1024)}) async-done(((f32[1536]{0:T(1024)}, f32[4,3328]{1,0:T(4,128)}, f32[3328]{0:T(1024)}, f32[48]{0:T(128)}, f32[48]{0:T(128)}, /*index=5*/f32[48]{0:T(128)}, f32[3072]{0:T(1024)}, ...) | async-done | bytes 91728
  1887.5 110.0 %reduce-scatter.31.cloned.1.call-done = bf16[384,2048]{1,0:T(8,128)(2,1)} async-done(((bf16[1536,2048]{1,0:T(8,128)(2,1)}), bf16[384,2048]{1,0:T(8,128)(2,1)}) %reduce-scatter.31.cloned.1.call-update) | async-done | bytes 1572880
  2003.9 107.2 %reduce-scatter.25.cloned.1.call-done = bf16[4,384,512]{2,1,0:T(8,128)(2,1)} async-done(((bf16[4,1536,512]{2,1,0:T(8,128)(2,1)}), bf16[4,384,512]{2,1,0:T(8,128)(2,1)}) %reduce-scatter.25.cloned.1.call-update) | async-done | bytes 1572880 | tf_op jit(solution)/shard_map/reduce_scatter | solution.py:491
  2114.6 110.0 %reduce-scatter.27.cloned.1.call-done = bf16[4,384,512]{2,1,0:T(8,128)(2,1)} async-done(((bf16[4,1536,512]{2,1,0:T(8,128)(2,1)}), bf16[4,384,512]{2,1,0:T(8,128)(2,1)}) %reduce-scatter.27.cloned.1.call-update) | async-done | bytes 1572880 | tf_op jit(solution)/shard_map/reduce_scatter | solution.py:494
  2228.2 118.6 %reduce-scatter.19.cloned.1.call-done = f32[48,1024]{1,0:T(8,128)} async-done(((f32[1536,1024]{1,0:T(8,128)}), f32[48,1024]{1,0:T(8,128)}) %reduce-scatter.19.cloned.1.call-update) | async-done | bytes 196624 | tf_op jit(solution)/shard_map/reduce_scatter | solution.py:486
  2346.8 119.9 %reduce-scatter.21.cloned.1.call-done = f32[48,1024]{1,0:T(8,128)} async-done(((f32[1536,1024]{1,0:T(8,128)}), f32[48,1024]{1,0:T(8,128)}) %reduce-scatter.21.cloned.1.call-update) | async-done | bytes 196624 | tf_op jit(solution)/shard_map/reduce_scatter | solution.py:487
  2466.7 120.5 %reduce-scatter.23.cloned.1.call-done = f32[32,1536]{1,0:T(8,128)} async-done(((f32[1024,1536]{1,0:T(8,128)}), f32[32,1536]{1,0:T(8,128)}) %reduce-scatter.23.cloned.1.call-update) | async-done | bytes 196624 | tf_op jit(solution)/shard_map/reduce_scatter | solution.py:488
  2587.2 213.0 %reduce-scatter.17.cloned.1.call-done = f32[96,1536]{1,0:T(8,128)} async-done(((f32[3072,1536]{1,0:T(8,128)}), f32[96,1536]{1,0:T(8,128)}) %reduce-scatter.17.cloned.1.call-update) | async-done | bytes 589840 | tf_op jit(solution)/shard_map/reduce_scatter | solution.py:483
  2800.2 371.0 %reduce-scatter.15.cloned.1.call-done = f32[48,6448]{1,0:T(8,128)} async-done(((f32[1536,6448]{1,0:T(8,128)}), f32[48,6448]{1,0:T(8,128)}) %reduce-scatter.15.cloned.1.call-update) | async-done | bytes 1238032 | tf_op jit(solution)/shard_map/reduce_scatter | solution.py:479
  (729 shorter events, 727.0 us)
Async XLA Ops:
  7.2 138.1 %all-gather.16.cloned.1.call-start = ((), (), s32[]{:S(2)}) async-start(), calls=%async_computation.13 | async-start | bytes 20680704 | tf_op jit(solution)/shard_map/all_gather | solution.py:237
  7.9 398.5 %all-gather.32.cloned.1.call-start = ((), (), s32[]{:S(2)}) async-start(), calls=%async_computation.28 | async-start | bytes 3932160 | tf_op jit(solution)/shard_map/all_gather | solution.py:27
  55.1 90.2 %copy-start.54 = (f32[1536]{0:T(1024)}, f32[1536]{0:T(1024)S(1)}, u32[]{:S(2)}) copy-start(f32[1536]{0:T(1024)S(1)} %convert_element_type.276) | copy-start | bytes 18436
  126.1 52.3 %copy-start.98 = (f32[1,256]{1,0:T(1,128)}, f32[1,256]{1,0:T(1,128)S(1)}, u32[]{:S(2)}) copy-start(f32[1,256]{1,0:T(1,128)S(1)} %get-tuple-element.1276) | copy-start | bytes 3076
  126.1 52.3 %copy-start.100 = (f32[1,256]{1,0:T(1,128)}, f32[1,256]{1,0:T(1,128)S(1)}, u32[]{:S(2)}) copy-start(f32[1,256]{1,0:T(1,128)S(1)} %get-tuple-element.1277) | copy-start | bytes 3076
  126.1 52.3 %copy-start.102 = (f32[1,256]{1,0:T(1,128)}, f32[1,256]{1,0:T(1,128)S(1)}, u32[]{:S(2)}) copy-start(f32[1,256]{1,0:T(1,128)S(1)} %get-tuple-element.1278) | copy-start | bytes 3076
  126.2 255.4 %copy-start.105 = (f32[1,256]{1,0:T(1,128)}, f32[1,256]{1,0:T(1,128)S(1)}, u32[]{:S(2)}) copy-start(f32[1,256]{1,0:T(1,128)S(1)} %get-tuple-element.1275) | copy-start | bytes 3076
  126.3 52.1 %copy-start.78 = (f32[3328]{0:T(1024)}, f32[3328]{0:T(1024)S(1)}, u32[]{:S(2)}) copy-start(f32[3328]{0:T(1024)S(1)} %get-tuple-element.1125) | copy-start | bytes 39940
  126.3 52.1 %copy-start.80 = (f32[3328]{0:T(1024)}, f32[3328]{0:T(1024)S(1)}, u32[]{:S(2)}) copy-start(f32[3328]{0:T(1024)S(1)} %get-tuple-element.1126) | copy-start | bytes 39940
  126.3 52.1 %copy-start.82 = (f32[3328]{0:T(1024)}, f32[3328]{0:T(1024)S(1)}, u32[]{:S(2)}) copy-start(f32[3328]{0:T(1024)S(1)} %get-tuple-element.1127) | copy-start | bytes 39940
  126.3 52.1 %copy-start.84 = (f32[3328]{0:T(1024)}, f32[3328]{0:T(1024)S(1)}, u32[]{:S(2)}) copy-start(f32[3328]{0:T(1024)S(1)} %get-tuple-element.1128) | copy-start | bytes 39940
  161.6 16.7 collective-permute-start
  342.6 70.2 %copy-start.23 = (f32[2,1,128,128]{3,2,1,0:T(8,128)}, f32[2,1,128,128]{3,2,1,0:T(8,128)S(1)}, u32[]{:S(2)}) copy-start(f32[2,1,128,128]{3,2,1,0:T(8,128)S(1)} %get-tuple-element.1806) | copy-start | bytes 393220
  343.6 146.2 %all-gather.18.cloned.1.call-start = ((), (), s32[]{:S(2)}) async-start(), calls=%async_computation.14 | async-start | bytes 9732096 | tf_op jit(solution)/shard_map/all_gather | solution.py:241
  344.4 320.7 %all-gather.28.cloned.1.call-start = ((), (), s32[]{:S(2)}) async-start(), calls=%async_computation.19 | async-start | bytes 7864320 | tf_op jit(solution)/shard_map/all_gather | solution.py:263
  345.0 391.3 %all-gather.26.cloned.1.call-start = ((), (), s32[]{:S(2)}) async-start(), calls=%async_computation.18 | async-start | bytes 7864320 | tf_op jit(solution)/shard_map/all_gather | solution.py:262
  345.6 494.9 %all-gather.30.cloned.1.call-start = ((), (), s32[]{:S(2)}) async-start(), calls=%async_computation.20 | async-start | bytes 7864320 | tf_op jit(solution)/shard_map/all_gather | solution.py:264
  357.7 90.0 %copy-start.75 = (f32[3072]{0:T(1024)}, f32[3072]{0:T(1024)S(1)}, u32[]{:S(2)}) copy-start(f32[3072]{0:T(1024)S(1)} %convert_element_type.284) | copy-start | bytes 36868
  357.8 138.7 %copy-start.86 = (f32[1536]{0:T(1024)}, f32[1536]{0:T(1024)S(1)}, u32[]{:S(2)}) copy-start(f32[1536]{0:T(1024)S(1)} %convert_element_type.286) | copy-start | bytes 18436
  453.2 43.2 %copy-start.31 = (bf16[1,256,3072]{2,0,1:T(2,128)(2,1)}, bf16[1,256,3072]{2,0,1:T(2,128)(2,1)S(1)}, u32[]{:S(2)}) copy-start(bf16[1,256,3072]{2,0,1:T(2,128)(2,1)S(1)} %multiply_convert_fusion.4) | copy-start | bytes 4718596
  497.8 752.1 %copy-start.11 = (bf16[256,1536]{1,0:T(8,128)(2,1)}, bf16[256,1536]{1,0:T(8,128)(2,1)S(1)}, u32[]{:S(2)}) copy-start(bf16[256,1536]{1,0:T(8,128)(2,1)S(1)} %multiply_convert_fusion.5) | copy-start | bytes 2359300
  513.8 82.5 %copy-start.32 = (bf16[1,256,1536]{2,1,0:T(8,128)(2,1)S(1)}, bf16[1,256,1536]{2,1,0:T(8,128)(2,1)}, u32[]{:S(2)}) copy-start(bf16[1,256,1536]{2,1,0:T(8,128)(2,1)} %param.33) | copy-start | bytes 2359300
  513.8 136.0 %all-to-all-start = ((bf16[32,60,1536]{2,1,0:T(8,128)(2,1)}), bf16[32,60,1536]{2,1,0:T(8,128)(2,1)}, u32[]{:S(2)}, u32[]{:S(2)}) async-start(bf16[32,60,1536]{2,1,0:T(8,128)(2,1)} %reshape.1999), calls=%async_computation | async-start | bytes 12582912 | tf_op jit(solution)/shard_map/all_to_all | solution.py:334
  518.8 443.1 %all-gather.20.cloned.1.call-start = ((), (), s32[]{:S(2)}) async-start(), calls=%async_computation.15 | async-start | bytes 3244032 | tf_op jit(solution)/shard_map/all_gather | solution.py:244
  649.8 76.4 %all-to-all-start.2 = ((bf16[32,60,1536]{2,1,0:T(8,128)(2,1)}), bf16[32,60,1536]{2,1,0:T(8,128)(2,1)}, u32[]{:S(2)}, u32[]{:S(2)}) async-start(bf16[32,60,1536]{2,1,0:T(8,128)(2,1)} %multiply_convert_fusion), calls=%async_computation.2 | async-start | bytes 12582912 | tf_op jit(solution)/shard_map/all_to_all | solution.py:366
  654.6 346.9 %all-gather.22.cloned.1.call-start = ((), (), s32[]{:S(2)}) async-start(), calls=%async_computation.16 | async-start | bytes 3244032 | tf_op jit(solution)/shard_map/all_gather | solution.py:245
  868.5 78.4 %all-to-all-start.1 = ((bf16[4,480,1536]{2,0,1:T(4,128)(2,1)}), bf16[4,480,1536]{2,0,1:T(4,128)(2,1)}, u32[]{:S(2)}, u32[]{:S(2)}) async-start(bf16[4,480,1536]{2,0,1:T(4,128)(2,1)} %copy.602), calls=%async_computation.1 | async-start | bytes 11796480 | tf_op jit(solution)/shard_map/all_to_all | solution.py:343
  873.2 188.0 %all-gather.24.cloned.1.call-start = ((), (), s32[]{:S(2)}) async-start(), calls=%async_computation.17 | async-start | bytes 3244032 | tf_op jit(solution)/shard_map/all_gather | solution.py:246
  907.4 44.3 %copy-start.92 = (s32[1,256,6]{1,0,2:T(1,128)S(1)}, s32[1,256,6]{1,0,2:T(1,128)}, u32[]{:S(2)}) copy-start(s32[1,256,6]{1,0,2:T(1,128)} %param.32) | copy-start | bytes 18436
  907.4 44.3 %copy-start.60 = (s32[256,6,1]{1,0,2:T(8,128)S(1)}, s32[256,6,1]{1,0,2:T(8,128)}, u32[]{:S(2)}) copy-start(s32[256,6,1]{1,0,2:T(8,128)} %get-tuple-element.1272) | copy-start | bytes 18436
  907.4 44.5 %copy-start.62 = (f32[1,256,48]{1,2,0:T(8,128)S(1)}, f32[1,256,48]{1,2,0:T(8,128)}, u32[]{:S(2)}) copy-start(f32[1,256,48]{1,2,0:T(8,128)} %copy-done.61) | copy-start | bytes 147460
  946.9 167.1 %all-to-all-start.3 = ((bf16[4,480,1536]{2,0,1:T(4,128)(2,1)}), bf16[4,480,1536]{2,0,1:T(4,128)(2,1)}, u32[]{:S(2)}, u32[]{:S(2)}) async-start(bf16[4,480,1536]{2,0,1:T(4,128)(2,1)} %copy.607), calls=%async_computation.3 | async-start | bytes 11796480 | tf_op jit(solution)/shard_map/all_to_all | solution.py:386
  951.7 323.7 %all-gather.34.cloned.1.call-start = ((), (), s32[]{:S(2)}) async-start(), calls=%async_computation.29 | async-start | bytes 3932160 | tf_op jit(solution)/shard_map/all_gather | solution.py:46
  964.8 96.4 %copy-start.33 = (bf16[1,256,1536]{2,1,0:T(8,128)(2,1)S(1)}, bf16[1,256,1536]{2,1,0:T(8,128)(2,1)}, u32[]{:S(2)}) copy-start(bf16[1,256,1536]{2,1,0:T(8,128)(2,1)} %param.33) | copy-start | bytes 2359300
  1212.9 508.7 %reduce-scatter.29.cloned.1.call-start = ((), (), s32[]{:S(2)}) async-start(), calls=%async_computation.30 | async-start | bytes 811008
  1251.3 629.8 %all-reduce.27.cloned.1.call-start = ((), (), s32[]{:S(2)}) async-start(), calls=%async_computation.32 | async-start | bytes 199680
  1584.1 17.3 collective-permute-start.1
  1622.7 374.8 %reduce-scatter.31.cloned.1.call-start = ((), (), s32[]{:S(2)}) async-start(), calls=%async_computation.31 | async-start | bytes 7864320
  1652.0 459.1 %reduce-scatter.25.cloned.1.call-start = ((), (), s32[]{:S(2)}) async-start(), calls=%async_computation.26 | async-start | bytes 7864320 | tf_op jit(solution)/shard_map/reduce_scatter | solution.py:491
  1662.1 562.6 %reduce-scatter.27.cloned.1.call-start = ((), (), s32[]{:S(2)}) async-start(), calls=%async_computation.27 | async-start | bytes 7864320 | tf_op jit(solution)/shard_map/reduce_scatter | solution.py:494
  1671.7 675.1 %reduce-scatter.19.cloned.1.call-start = ((), (), s32[]{:S(2)}) async-start(), calls=%async_computation.23 | async-start | bytes 6488064 | tf_op jit(solution)/shard_map/reduce_scatter | solution.py:486
  1676.7 790.0 %reduce-scatter.21.cloned.1.call-start = ((), (), s32[]{:S(2)}) async-start(), calls=%async_computation.24 | async-start | bytes 6488064 | tf_op jit(solution)/shard_map/reduce_scatter | solution.py:487
  1681.5 905.8 %reduce-scatter.23.cloned.1.call-start = ((), (), s32[]{:S(2)}) async-start(), calls=%async_computation.25 | async-start | bytes 6488064 | tf_op jit(solution)/shard_map/reduce_scatter | solution.py:488
  1686.5 1113.7 %reduce-scatter.17.cloned.1.call-start = ((), (), s32[]{:S(2)}) async-start(), calls=%async_computation.22 | async-start | bytes 19464192 | tf_op jit(solution)/shard_map/reduce_scatter | solution.py:483
  1698.0 1473.1 %reduce-scatter.15.cloned.1.call-start = ((), (), s32[]{:S(2)}) async-start(), calls=%async_computation.21 | async-start | bytes 41361408 | tf_op jit(solution)/shard_map/reduce_scatter | solution.py:479
  2114.6 1056.5 %copy-start.129 = (f32[48]{0:T(128)S(1)}, f32[48]{0:T(128)}, u32[]{:S(2)}) copy-start(f32[48]{0:T(128)} %get-tuple-element.1737) | copy-start | bytes 580
  2114.6 1057.0 %copy-start.128 = (f32[48]{0:T(128)S(1)}, f32[48]{0:T(128)}, u32[]{:S(2)}) copy-start(f32[48]{0:T(128)} %get-tuple-element.1738) | copy-start | bytes 580
  2114.6 1057.5 %copy-start.127 = (f32[48]{0:T(128)S(1)}, f32[48]{0:T(128)}, u32[]{:S(2)}) copy-start(f32[48]{0:T(128)} %get-tuple-element.1739) | copy-start | bytes 580
  (134 other events, 1081.7 us)
Sparse Core Ops, SparseCore 0:
  10.8 134.4 all-gather.15
  343.8 62.6 all-gather.31
  409.2 80.5 all-gather.17
  491.3 119.0 all-gather.27
  611.8 113.7 all-gather.25
  726.9 113.5 all-gather.29
  843.4 77.7 all-gather.19
  924.1 77.2 all-gather.21
  1004.3 56.8 all-gather.23
  1213.0 62.3 all-gather.33
  1280.5 94.1 reduce-scatter.28
  1622.9 258.1 all-reduce.26
  1885.4 112.0 reduce-scatter.30
  1999.8 111.2 reduce-scatter.24
  2113.4 111.2 reduce-scatter.26
  2231.7 115.0 reduce-scatter.18
  2352.9 113.7 reduce-scatter.20
  2473.7 113.4 reduce-scatter.22
  2594.2 205.9 reduce-scatter.16
  2807.0 364.0 reduce-scatter.14
where the time goes:
time: 3200 us; the launch traced here: 3180 us
  waiting for transfers between devices  1790 us (56%)
  local copies, waits for them, and re-layouts  563 us (18%)
  matrix products  305 us (10%)
  other arithmetic  261 us (8%)
  blocking collectives  196 us (6%)
    reduce_scatter x1, waiting for transfers between devices, on_device(): lax.psum_scatter(grad_w_in, ('dp', 'ctx'), scatter_dimension=0, tiled=True)  371 us
    unnamed x23, waiting for transfers between devices  270 us
    reduce_scatter x1, waiting for transfers between devices, on_device(): lax.psum_scatter(grad_w_out, ('dp', 'ctx'), scatter_dimension=0, tiled=True)  213 us
    dynamic_update_slice x10, local copies, waits for them, and re-layouts, scan_blocks(): lax.scan(jax.checkpoint(block_step), (memory, previous), inputs)  149 us
    reduce_scatter x1, waiting for transfers between devices, on_device(): lax.psum_scatter(grad_w_sdown, ('dp', 'ctx'), scatter_dimension=0, tiled=...  121 us
    reduce_scatter x1, waiting for transfers between devices, on_device(): lax.psum_scatter(grad_w_sup, ('dp', 'ctx'), scatter_dimension=0, tiled=True)  120 us
    reduce_scatter x1, waiting for transfers between devices, on_device(): lax.psum_scatter(grad_w_sgate, ('dp', 'ctx'), scatter_dimension=0, tiled=...  119 us
    reduce_scatter x1, waiting for transfers between devices, on_device(): lax.psum_scatter(grad_e_up.astype(jnp.bfloat16), 'ctx', scatter_dimension...  110 us
  transfers between devices with their start and end apart: 26, of which 18 were waited for; matrix products, arithmetic and copies ran while one was open for 26% of the time, Pallas kernels for 0%

commit v1 on v0

--- a/solution.py
+++ b/solution.py
@@ -3,6 +3,8 @@
 import jax
 import jax.numpy as jnp
 from jax import lax
+from jax.experimental import pallas as pl
+from jax.experimental.pallas import tpu as pltpu
 from jax.sharding import PartitionSpec as P
 
 HEADS = 48
@@ -203,7 +205,7 @@
     )
 
 
-def on_device(
+def on_device_general(
     layer_in,
     seg_ids,
     route_ids,
@@ -525,6 +527,1037 @@
     )
 
 
+GROUP = 8
+WIDE = GROUP * HEAD
+VMEM_MOST = 56 * 1024 * 1024
+
+
+def spread_rows(rows):
+    count, width = rows.shape
+    return jnp.broadcast_to(rows[:, None, :], (count, HEAD, width)).reshape(count * HEAD, width)
+
+
+def head_sums(value):
+    return jnp.sum(value.reshape(GROUP, HEAD, value.shape[-1]), axis=1)
+
+
+def mul_nn(left, right):
+    return lax.dot_general(
+        left, right, (((1,), (0,)), ((), ())), preferred_element_type=jnp.float32
+    )
+
+
+def mul_nt(left, right):
+    return lax.dot_general(
+        left, right, (((1,), (1,)), ((), ())), preferred_element_type=jnp.float32
+    )
+
+
+def mul_tn(left, right):
+    return lax.dot_general(
+        left, right, (((0,), (0,)), ((), ())), preferred_element_type=jnp.float32
+    )
+
+
+def half(value):
+    return value.astype(jnp.bfloat16)
+
+
+def call_steps(kernel, steps, ins, in_specs, outs, out_specs, scratch=(), flops=1 << 30):
+    return pl.pallas_call(
+        kernel,
+        grid=(steps,),
+        in_specs=in_specs,
+        out_specs=out_specs,
+        out_shape=outs,
+        scratch_shapes=list(scratch),
+        cost_estimate=pl.CostEstimate(flops=flops, bytes_accessed=8 << 20, transcendentals=0),
+        compiler_params=pltpu.CompilerParams(
+            vmem_limit_bytes=VMEM_MOST, dimension_semantics=("arbitrary",)
+        ),
+    )(*ins)
+
+
+def block(shape, index):
+    return pl.BlockSpec(shape, index)
+
+
+def whole(array):
+    return pl.BlockSpec(array.shape, lambda i: (0,) * array.ndim)
+
+
+def f32_out(*shape):
+    return jax.ShapeDtypeStruct(shape, jnp.float32)
+
+
+def bf16_out(*shape):
+    return jax.ShapeDtypeStruct(shape, jnp.bfloat16)
+
+
+def conv_steps(x, taps, masks):
+    total = taps[:, 4:5] + taps[:, 3:4] * x * masks[0:1]
+    for back in (1, 2, 3):
+        total = total + taps[:, 3 - back : 4 - back] * pltpu.roll(x, back, 1) * masks[back : back + 1]
+    return total
+
+
+def conv_kernel(x_ref, taps_ref, masks_ref, pre_ref):
+    tokens = pre_ref.shape[1]
+    pre_ref[...] = conv_steps(x_ref[...], taps_ref[...], masks_ref[...])[:, :tokens]
+
+
+def conv_adjoint(grad_pre, x, taps, masks):
+    width = x.shape[1]
+    grad_x = jnp.zeros_like(x)
+    columns = []
+    for back in (3, 2, 1, 0):
+        part = grad_pre * masks[back : back + 1]
+        moved = x if back == 0 else pltpu.roll(x, back, 1)
+        columns.append(jnp.sum(part * moved, axis=1, keepdims=True))
+        tap = taps[:, 3 - back : 4 - back]
+        grad_x = grad_x + tap * (part if back == 0 else pltpu.roll(part, width - back, 1))
+    columns.append(jnp.sum(grad_pre, axis=1, keepdims=True))
+    lane = lax.broadcasted_iota(jnp.int32, (x.shape[0], 8), 1)
+    packed = jnp.zeros((x.shape[0], 8), jnp.float32)
+    for place, column in enumerate(columns):
+        packed = jnp.where(lane == place, column, packed)
+    return grad_x, packed
+
+
+def conv_back_kernel(grad_ref, pre_ref, x_ref, taps_ref, masks_ref, grad_x_ref, taps_out_ref):
+    grad_pre = grad_ref[...] * silu_slope(pre_ref[...])
+    rest = x_ref.shape[1] - grad_pre.shape[1]
+    grad_pre = jnp.concatenate([grad_pre, jnp.zeros((grad_pre.shape[0], rest), jnp.float32)], axis=1)
+    grad_x, packed = conv_adjoint(grad_pre, x_ref[...], taps_ref[...], masks_ref[...])
+    grad_x_ref[...] = grad_x.astype(grad_x_ref.dtype)
+    taps_out_ref[...] = packed
+
+
+def link_mask(seg_row, seg_col):
+    count = seg_row.shape[1]
+    source = lax.broadcasted_iota(jnp.int32, (count, count), 0)
+    target = lax.broadcasted_iota(jnp.int32, (count, count), 1)
+    linked = jnp.logical_and(source <= target, seg_row == seg_col)
+    return jnp.where(linked, 0.0, -1e30)
+
+
+def state_kernel(x_ref, taps_ref, masks_ref, bc_ref, dt_ref, cum_ref, flags_ref, pre_ref, state_ref):
+    tokens = pre_ref.shape[1]
+    pre = conv_steps(x_ref[...], taps_ref[...], masks_ref[...])[:, :tokens]
+    pre_ref[...] = pre
+    b_t = half(jax.nn.silu(bc_ref[:STATE, :]))
+    cum = cum_ref[...]
+    tail = jnp.exp(cum[:, tokens - 1 :] - cum) * flags_ref[1:2, :] * dt_ref[...]
+    scaled = half(jax.nn.silu(pre) * spread_rows(tail))
+    state_ref[...] = half(mul_nt(scaled, b_t))
+
+
+def inner_kernel(
+    pre_ref, bc_ref, dt_ref, cum_ref, cum_col_ref, skip_ref, flags_ref, seg_col_ref, y_ref, mask_s, inner_s
+):
+    @pl.when(pl.program_id(0) == 0)
+    def _():
+        mask_s[...] = link_mask(flags_ref[2:3, :], seg_col_ref[:, 0:1])
+        bc = half(jax.nn.silu(bc_ref[...]))
+        inner_s[...] = mul_tn(bc[:STATE], bc[STATE:])
+
+    x = jax.nn.silu(pre_ref[...])
+    scaled = half(x * spread_rows(dt_ref[...]))
+    cum, cum_col = cum_ref[...], cum_col_ref[0]
+    for head in range(GROUP):
+        rows = slice(head * HEAD, (head + 1) * HEAD)
+        spread = cum[head : head + 1, :] - cum_col[:, head : head + 1] + mask_s[...]
+        weights = half(jnp.exp(spread) * inner_s[...])
+        y_ref[rows, :] = mul_nn(scaled[rows], weights) + x[rows] * skip_ref[head : head + 1, :]
+
+
+def join_kernel(
+    y_ref, state_ref, bc_ref, cum_ref, z_ref, gain_ref, flags_ref, y_out_ref, gated_ref, sums_ref, u_s, sum_s
+):
+    step, groups = pl.program_id(0), u_s.shape[0]
+
+    @pl.when(step == 0)
+    def _():
+        sum_s[...] = jnp.zeros_like(sum_s)
+
+    @pl.when(step < groups)
+    def _():
+        c_t = half(jax.nn.silu(bc_ref[STATE:, :]))
+        reach = jnp.exp(cum_ref[...]) * flags_ref[0:1, :]
+        y = y_ref[...] + mul_nn(state_ref[...], c_t) * spread_rows(reach)
+        y_out_ref[...] = y
+        u = y * jax.nn.silu(z_ref[...])
+        u_s[step] = u
+        sum_s[...] += jnp.sum(u * u, axis=0, keepdims=True)
+
+    @pl.when(step >= groups)
+    def _():
+        scale = lax.rsqrt(sum_s[0:1, :] * (1.0 / DI) + 1e-05)
+        gated_ref[...] = half(u_s[step - groups] * scale * gain_ref[:, 0:1])
+        sums_ref[...] = jnp.broadcast_to(scale, sums_ref.shape)
+
+
+def gate_back_kernel(
+    y_ref, z_ref, grad_ref, gain_ref, rows_ref, bc_ref, cum_ref, flags_ref, grad_y_ref, grad_z_ref, grad_state_ref
+):
+    y, z, gain = y_ref[...], z_ref[...], gain_ref[:, 0:1]
+    squashed = jax.nn.sigmoid(z)
+    u = y * z * squashed
+    grad_u = gain * rows_ref[0:1, :] * grad_ref[...] - u * rows_ref[1:2, :]
+    grad_y = grad_u * z * squashed
+    grad_y_ref[...] = grad_y
+    grad_z_ref[...] = half(grad_u * y * (squashed * (1.0 + z * (1.0 - squashed))))
+    c_t = half(jax.nn.silu(bc_ref[STATE:, :]))
+    reach = jnp.exp(cum_ref[...]) * flags_ref[0:1, :]
+    grad_state_ref[...] = half(mul_nt(half(grad_y * spread_rows(reach)), c_t))
+
+
+def inner_back_kernel(
+    pre_ref, grad_y_ref, bc_ref, dt_ref, cum_ref, cum_col_ref, flags_ref, seg_col_ref,
+    grad_x_ref, grad_cum_ref, grad_skip_ref, grad_bc_ref, mask_s, inner_s, total_s,
+):
+    step = pl.program_id(0)
+
+    @pl.when(step == 0)
+    def _():
+        mask_s[...] = link_mask(flags_ref[2:3, :], seg_col_ref[:, 0:1])
+        bc = half(jax.nn.silu(bc_ref[...]))
+        inner_s[...] = mul_tn(bc[:STATE], bc[STATE:])
+        total_s[...] = jnp.zeros_like(total_s)
+
+    x = jax.nn.silu(pre_ref[...])
+    grad_y = grad_y_ref[...]
+    grad_skip_ref[...] = head_sums(x * grad_y)
+    scaled = half(x * spread_rows(dt_ref[...]))
+    grad_half = half(grad_y)
+    cum, cum_col = cum_ref[...], cum_col_ref[0]
+    ones = jnp.ones((8, cum.shape[1]), jnp.bfloat16)
+    for head in range(GROUP):
+        rows = slice(head * HEAD, (head + 1) * HEAD)
+        decay = jnp.exp(cum[head : head + 1, :] - cum_col[:, head : head + 1] + mask_s[...])
+        weights = decay * inner_s[...]
+        grad_x_ref[rows, :] = mul_nt(grad_half[rows], half(weights))
+        grad_weights = mul_tn(scaled[rows], grad_half[rows])
+        total_s[...] += grad_weights * decay
+        moved = half(grad_weights * weights)
+        sums = mul_nn(ones, moved) - mul_nt(ones, moved)
+        grad_cum_ref[head : head + 1, :] = sums[0:1]
+
+    @pl.when(step == pl.num_programs(0) - 1)
+    def _():
+        bc = half(jax.nn.silu(bc_ref[...]))
+        total = half(total_s[...])
+        grad_bc_ref[:STATE, :] = mul_nt(bc[STATE:], total)
+        grad_bc_ref[STATE:, :] = mul_nn(bc[:STATE], total)
+
+
+def join_back_kernel(
+    grad_in_ref, grad_y_ref, pre_ref, x_ref, taps_ref, masks_ref, state_ref, grad_state_ref,
+    bc_ref, dt_ref, cum_ref, skip_ref, flags_ref,
+    grad_x_ref, taps_out_ref, grad_dt_ref, grad_cum_ref, grad_last_ref, grad_bc_ref,
+):
+    step = pl.program_id(0)
+
+    @pl.when(step == 0)
+    def _():
+        grad_bc_ref[...] = jnp.zeros_like(grad_bc_ref)
+
+    bc = half(jax.nn.silu(bc_ref[...]))
+    b_t, c_t = bc[:STATE], bc[STATE:]
+    pre, grad_y, cum, dt = pre_ref[...], grad_y_ref[...], cum_ref[...], dt_ref[...]
+    tokens = pre.shape[1]
+    state, grad_state = state_ref[...], grad_state_ref[...]
+    x = jax.nn.silu(pre)
+    reached = grad_y * spread_rows(jnp.exp(cum) * flags_ref[0:1, :])
+    grad_cum = head_sums(reached * mul_nn(state, c_t))
+    grad_bc_ref[STATE:, :] += mul_tn(state, half(reached))
+    tail = spread_rows(jnp.exp(cum[:, tokens - 1 :] - cum) * flags_ref[1:2, :])
+    dt_wide = spread_rows(dt)
+    scaled = x * dt_wide
+    from_state = mul_nn(grad_state, b_t) * tail
+    grad_bc_ref[:STATE, :] += mul_tn(grad_state, half(scaled * tail))
+    tails = head_sums(scaled * from_state)
+    grad_cum_ref[...] = grad_cum - tails
+    last = jnp.sum(tails, axis=1, keepdims=True)
+    through = jnp.sum(
+        head_sums(state.astype(jnp.float32) * grad_state.astype(jnp.float32)), axis=1, keepdims=True
+    )
+    lane = lax.broadcasted_iota(jnp.int32, (GROUP, 128), 1)
+    grad_last_ref[...] = jnp.where(lane == 0, last, jnp.where(lane == 1, through, 0.0))
+    grad_scaled = grad_in_ref[...] + from_state
+    grad_dt_ref[...] = head_sums(grad_scaled * x)
+    grad_pre = (grad_scaled * dt_wide + grad_y * spread_rows(skip_ref[...])) * silu_slope(pre)
+    rest = x_ref.shape[1] - tokens
+    grad_pre = jnp.concatenate([grad_pre, jnp.zeros((grad_pre.shape[0], rest), jnp.float32)], axis=1)
+    grad_x, packed = conv_adjoint(grad_pre, x_ref[...], taps_ref[...], masks_ref[...])
+    grad_x_ref[...] = half(grad_x)
+    taps_out_ref[...] = packed
+
+
+def mixer_rows(dt_raw, dt_bias, a_log, d_skip, seg_window, taps):
+    tokens = dt_raw.shape[1]
+    dt = jax.nn.softplus(dt_raw + dt_bias[:, None])
+    decay = -jnp.exp(a_log)[:, None] * dt
+    upper = jnp.triu(jnp.ones((tokens, tokens), jnp.float32))
+    cum = jnp.dot(decay, upper, precision=lax.Precision.HIGHEST)
+    cum_col = jnp.swapaxes(cum.reshape(-1, GROUP, tokens), 1, 2)
+    seg_now = seg_window[taps - 1 :]
+    before = seg_window[taps - 2]
+    reach = (seg_now == before).astype(jnp.float32)
+    tail = (seg_now == seg_now[-1]).astype(jnp.float32)
+    none = jnp.zeros((5, tokens), jnp.float32)
+    flags = jnp.concatenate([jnp.stack([reach, tail, seg_now.astype(jnp.float32)]), none])
+    seg_col = jnp.broadcast_to(seg_now.astype(jnp.float32)[:, None], (tokens, 8))
+    masks = [
+        (seg_window[taps - 1 - back : taps - 1 - back + tokens] == seg_now).astype(jnp.float32)
+        for back in range(taps)
+    ]
+    masks = jnp.pad(jnp.stack(masks), ((0, 8 - taps), (0, 128)))
+    through = jnp.exp(cum[:, -1]) * (seg_now[-1] == before).astype(jnp.float32)
+    skip = jnp.broadcast_to(d_skip[:, None], dt.shape)
+    return dt, decay, cum, cum_col, flags, seg_col, masks, through, skip
+
+
+def mixer_forward_states(proj, taps, masks, dt, cum, flags):
+    tokens, groups = dt.shape[1], HEADS // GROUP
+    wide = proj.shape[1]
+    bc_pre = call_steps(
+        conv_kernel, 1, (proj, taps, masks),
+        [block((2 * STATE, wide), lambda i: (DI // STATE, 0)),
+         block((2 * STATE, 8), lambda i: (DI // (2 * STATE), 0)), whole(masks)],
+        f32_out(2 * STATE, tokens), block((2 * STATE, tokens), lambda i: (0, 0)),
+    )
+    rows = block((GROUP, tokens), lambda i: (i, 0))
+    pre, state = call_steps(
+        state_kernel, groups, (proj, taps, masks, bc_pre, dt, cum, flags),
+        [block((WIDE, wide), lambda i: (i + groups, 0)), block((WIDE, 8), lambda i: (i, 0)), whole(masks),
+         whole(bc_pre), rows, rows, whole(flags)],
+        [f32_out(DI, tokens), bf16_out(DI, STATE)],
+        [block((WIDE, tokens), lambda i: (i, 0)), block((WIDE, STATE), lambda i: (i, 0))],
+    )
+    return bc_pre, pre, state
+
+
+def mixer_forward_inner(pre, bc_pre, dt, cum, cum_col, skip, flags, seg_col):
+    tokens, groups = dt.shape[1], HEADS // GROUP
+    rows = block((GROUP, tokens), lambda i: (i, 0))
+    wide = block((WIDE, tokens), lambda i: (i, 0))
+    square = pltpu.VMEM((tokens, tokens), jnp.float32)
+    return call_steps(
+        inner_kernel, groups, (pre, bc_pre, dt, cum, cum_col, skip, flags, seg_col),
+        [wide, whole(bc_pre), rows, rows, block((1, tokens, GROUP), lambda i: (i, 0, 0)), rows,
+         whole(flags), whole(seg_col)],
+        f32_out(DI, tokens), wide, (square, square), flops=30 << 30,
+    )
+
+
+def mixer_forward_join(y, state_in, bc_pre, cum, proj, gain_col, flags):
+    tokens, groups = y.shape[1], HEADS // GROUP
+    first = lambda i: (jnp.minimum(i, groups - 1), 0)
+    second = lambda i: (jnp.maximum(i - groups, 0), 0)
+    return call_steps(
+        join_kernel, 2 * groups, (y, state_in, bc_pre, cum, proj, gain_col, flags),
+        [block((WIDE, tokens), first), block((WIDE, STATE), first), whole(bc_pre),
+         block((GROUP, tokens), first), block((WIDE, tokens), first), block((WIDE, 8), second), whole(flags)],
+        [f32_out(DI, tokens), bf16_out(DI, tokens), f32_out(8, tokens)],
+        [block((WIDE, tokens), first), block((WIDE, tokens), second), block((8, tokens), lambda i: (0, 0))],
+        (pltpu.VMEM((groups, WIDE, tokens), jnp.float32), pltpu.VMEM((8, tokens), jnp.float32)),
+    )
+
+
+def mixer_back_gate(y, proj, grad_gated, gain_col, gate_rows, bc_pre, cum, flags):
+    tokens, groups = y.shape[1], HEADS // GROUP
+    wide = block((WIDE, tokens), lambda i: (i, 0))
+    return call_steps(
+        gate_back_kernel, groups, (y, proj, grad_gated, gain_col, gate_rows, bc_pre, cum, flags),
+        [wide, wide, wide, block((WIDE, 8), lambda i: (i, 0)), whole(gate_rows), whole(bc_pre),
+         block((GROUP, tokens), lambda i: (i, 0)), whole(flags)],
+        [f32_out(DI, tokens), bf16_out(DI, tokens), bf16_out(DI, STATE)],
+        [wide, wide, block((WIDE, STATE), lambda i: (i, 0))],
+    )
+
+
+def mixer_back_inner(pre, grad_y, bc_pre, dt, cum, cum_col, flags, seg_col):
+    tokens, groups = dt.shape[1], HEADS // GROUP
+    rows = block((GROUP, tokens), lambda i: (i, 0))
+    wide = block((WIDE, tokens), lambda i: (i, 0))
+    square = pltpu.VMEM((tokens, tokens), jnp.float32)
+    return call_steps(
+        inner_back_kernel, groups, (pre, grad_y, bc_pre, dt, cum, cum_col, flags, seg_col),
+        [wide, wide, whole(bc_pre), rows, rows, block((1, tokens, GROUP), lambda i: (i, 0, 0)),
+         whole(flags), whole(seg_col)],
+        [f32_out(DI, tokens), f32_out(HEADS, tokens), f32_out(HEADS, tokens), f32_out(2 * STATE, tokens)],
+        [wide, rows, rows, block((2 * STATE, tokens), lambda i: (0, 0))],
+        (square, square, square), flops=50 << 30,
+    )
+
+
+def mixer_back_join(grad_scaled, grad_y, pre, proj, taps, masks, state_in, grad_state, bc_pre, dt, cum, skip, flags):
+    tokens, groups = dt.shape[1], HEADS // GROUP
+    rows = block((GROUP, tokens), lambda i: (i, 0))
+    wide = block((WIDE, tokens), lambda i: (i, 0))
+    longer = block((WIDE, proj.shape[1]), lambda i: (i, 0))
+    later = block((WIDE, proj.shape[1]), lambda i: (i + groups, 0))
+    states = block((WIDE, STATE), lambda i: (i, 0))
+    narrow = block((WIDE, 8), lambda i: (i, 0))
+    return call_steps(
+        join_back_kernel, groups,
+        (grad_scaled, grad_y, pre, proj, taps, masks, state_in, grad_state, bc_pre, dt, cum, skip, flags),
+        [wide, wide, wide, later, narrow, whole(masks), states, states, whole(bc_pre), rows, rows, rows,
+         whole(flags)],
+        [bf16_out(DI, proj.shape[1]), f32_out(DI, 8), f32_out(HEADS, tokens), f32_out(HEADS, tokens),
+         f32_out(HEADS, 128), f32_out(2 * STATE, tokens)],
+        [longer, narrow, rows, rows, block((GROUP, 128), lambda i: (i, 0)),
+         block((2 * STATE, tokens), lambda i: (0, 0))],
+    )
+
+
+def mixer_back_conv(grad_bc, bc_pre, proj, taps, masks):
+    place = DI // (2 * STATE)
+    wide = proj.shape[1]
+    return call_steps(
+        conv_back_kernel, 1, (grad_bc, bc_pre, proj, taps, masks),
+        [whole(grad_bc), whole(bc_pre), block((2 * STATE, wide), lambda i: (2 * place, 0)),
+         block((2 * STATE, 8), lambda i: (place, 0)), whole(masks)],
+        [bf16_out(2 * STATE, wide), f32_out(2 * STATE, 8)],
+        [block((2 * STATE, wide), lambda i: (0, 0)), block((2 * STATE, 8), lambda i: (0, 0))],
+    )
+
+
+def cut(array_index, rows, columns, row_step, column_step):
+    found = []
+    for row in range(0, rows, row_step):
+        for column in range(0, columns, column_step):
+            found.append(
+                (array_index, row, min(row_step, rows - row), column, min(column_step, columns - column))
+            )
+    return found
+
+
+def places(lined):
+    dp, z = lax.axis_index("dp"), lax.axis_index("ctx")
+    y, x, core = lax.div(dp, 4), lax.rem(lax.div(dp, 2), 2), lax.rem(dp, 2)
+    others = {
+        "x": (dp + 2 - 4 * x, z),
+        "y": (dp + 4 - 8 * y, z),
+        "core": (dp + 1 - 2 * core, z),
+    }
+    for away in (1, 2, 3) if lined else ():
+        others[away] = (dp, lax.rem(z + away, 4))
+    return y, x, core, z, others
+
+
+def greet(others):
+    barrier = pltpu.get_barrier_semaphore()
+    for device in others.values():
+        pl.semaphore_signal(
+            barrier, inc=1, device_id=device, device_id_type=pl.DeviceIdType.MESH
+        )
+    pl.semaphore_wait(barrier, len(others))
+
+
+def send(source, target, sems, piece, leg, device):
+    return pltpu.make_async_remote_copy(
+        src_ref=source,
+        dst_ref=target,
+        send_sem=sems[0].at[piece, leg],
+        recv_sem=sems[1].at[piece, leg],
+        device_id=device,
+        device_id_type=pl.DeviceIdType.MESH,
+    )
+
+
+def gather_kernel(pieces, ahead, count, lined, *refs):
+    ins, outs, (sent, came, kept) = refs[:count], refs[count : 2 * count], refs[2 * count :]
+    y, x, core, z, others = places(lined)
+    greet(others)
+    sems = (sent, came)
+    started = []
+
+    def legs(number):
+        array, row, rows, column, columns = pieces[number]
+        area = (pl.ds(row, rows), pl.ds(column, columns))
+        out = outs[array]
+        first, second = ("x", "y") if number % 2 == 0 else ("y", "x")
+        rest = ((slice(None),) if lined else ()) + area
+        own = ins[array].at[area]
+        mine = out.at[(y, x, core) + ((z,) if lined else ()) + area]
+        line = out.at[(y, x, core) + rest]
+        if first == "x":
+            plane = out.at[(y, slice(None), core) + rest]
+        else:
+            plane = out.at[(slice(None), x, core) + rest]
+        every = out.at[(slice(None), slice(None), core) + rest]
+        return {
+            "keep": lambda: pltpu.make_async_copy(own, mine, kept.at[number]),
+            "line": lambda: [
+                send(own, mine, sems, number, away - 1, others[away])
+                for away in ((1, 2, 3) if lined else ())
+            ],
+            "first": lambda: send(line if lined else own, line, sems, number, 3, others[first]),
+            "second": lambda: send(plane, plane, sems, number, 4, others[second]),
+            "core": lambda: send(every, every, sems, number, 5, others["core"]),
+        }
+
+    def begin(number):
+        if number < len(pieces):
+            leg = legs(number)
+            leg["keep"]().start()
+            for copy in leg["line"]():
+                copy.start()
+
+    def advance(number, stage):
+        if not 0 <= number < len(pieces):
+            return
+        leg = legs(number)
+        if stage == 0:
+            leg["keep"]().wait()
+            for copy in leg["line"]():
+                copy.wait_recv()
+            leg["first"]().start()
+        elif stage == 1:
+            leg["first"]().wait_recv()
+            leg["second"]().start()
+        elif stage == 2:
+            leg["second"]().wait_recv()
+            leg["core"]().start()
+        else:
+            leg["core"]().wait_recv()
+
+    for number in range(2 * ahead):
+        begin(number)
+    pairs = -(-len(pieces) // 2)
+    for turn in range(pairs + 3):
+        for stage in range(4):
+            for number in (2 * (turn - stage), 2 * (turn - stage) + 1):
+                advance(number, stage)
+                if stage == 0 and number < len(pieces):
+                    begin(number + 2 * ahead)
+    for number in range(len(pieces)):
+        leg = legs(number)
+        for copy in leg["line"]() + [leg["first"](), leg["second"](), leg["core"]()]:
+            copy.wait_send()
+
+
+def pallas_gather(parts, steps, name_id, lined=True, ahead=2):
+    pieces = []
+    for index, (part, (row_step, column_step)) in enumerate(zip(parts, steps)):
+        pieces += cut(index, part.shape[0], part.shape[1], row_step, column_step)
+    count = len(parts)
+    lead = (2, 2, 2, 4) if lined else (2, 2, 2)
+    anywhere = pl.BlockSpec(memory_space=pl.ANY)
+    outs = pl.pallas_call(
+        partial(gather_kernel, pieces, ahead, count, lined),
+        in_specs=[anywhere] * count,
+        out_specs=[anywhere] * count,
+        out_shape=[jax.ShapeDtypeStruct(lead + part.shape, part.dtype) for part in parts],
+        scratch_shapes=[
+            pltpu.SemaphoreType.DMA((len(pieces), 6)),
+            pltpu.SemaphoreType.DMA((len(pieces), 6)),
+            pltpu.SemaphoreType.DMA((len(pieces),)),
+        ],
+        compiler_params=pltpu.CompilerParams(collective_id=name_id, has_side_effects=True),
+    )(*parts)
+    return [out.reshape((-1,) + part.shape) for out, part in zip(outs, parts)]
+
+
+def reduce_kernel(pieces, ahead, count, lined, *refs):
+    ins, outs = refs[:count], refs[count : 2 * count]
+    sent, came, kept, put = refs[2 * count : 2 * count + 4]
+    room = refs[2 * count + 4 :]
+    y, x, core, z, others = places(lined)
+    greet(others)
+    sems = (sent, came)
+    amount = len(pieces)
+
+    def held(number):
+        return room[6 * number : 6 * number + 6]
+
+    def legs(number):
+        array, row, rows, column, columns = pieces[number]
+        area = (pl.ds(row, rows), pl.ds(column, columns))
+        total, from_core, from_first, from_second, from_line, result = held(number)
+        every = (slice(None), slice(None))
+        rest = ((slice(None),) if lined else ()) + area
+        side = number % 2 == 0
+        return {
+            "load": lambda: pltpu.make_async_copy(
+                ins[array].at[every + (core,) + rest], total, kept.at[number]
+            ),
+            "core": lambda: send(
+                ins[array].at[every + (1 - core,) + rest],
+                from_core, sems, number, 0, others["core"],
+            ),
+            "first": lambda: send(
+                total.at[:, 1 - x] if side else total.at[1 - y],
+                from_first, sems, number, 1, others["x" if side else "y"],
+            ),
+            "second": lambda: send(
+                total.at[1 - y, x] if side else total.at[y, 1 - x],
+                from_second, sems, number, 2, others["y" if side else "x"],
+            ),
+            "line": lambda: [
+                send(
+                    total.at[y, x, lax.rem(z + away, 4)], from_line.at[away - 1],
+                    sems, number, 2 + away, others[away],
+                )
+                for away in ((1, 2, 3) if lined else ())
+            ],
+            "store": lambda: pltpu.make_async_copy(result, outs[array].at[area], put.at[number]),
+        }
+
+    def begin(number):
+        if number < amount:
+            leg = legs(number)
+            leg["load"]().start()
+            leg["core"]().start()
+
+    def advance(number, stage):
+        if not 0 <= number < amount:
+            return
+        leg = legs(number)
+        total, from_core, from_first, from_second, from_line, result = held(number)
+        deep = 4 if lined else 1
+
+        def place(at, *lead):
+            return lead + ((lax.rem(at, deep),) if lined else ())
+
+        if stage == 0:
+            leg["load"]().wait()
+            leg["core"]().wait_recv()
+
+            @pl.loop(0, 4 * deep)
+            def _(at):
+                here = place(at, lax.div(at, 2 * deep), lax.rem(lax.div(at, deep), 2))
+                total[here] = total[here] + from_core[here]
+
+            leg["first"]().start()
+        elif stage == 1:
+            leg["first"]().wait_recv()
+
+            @pl.loop(0, 2 * deep)
+            def _(at):
+                outer = lax.div(at, deep)
+                here = place(at, outer, x) if number % 2 == 0 else place(at, y, outer)
+                total[here] = total[here] + from_first[place(at, outer)]
+
+            leg["second"]().start()
+        elif stage == 2:
+            leg["second"]().wait_recv()
+            if lined:
+
+                @pl.loop(0, 4)
+                def _(at):
+                    total[y, x, at] = total[y, x, at] + from_second[at]
+
+                for copy in leg["line"]():
+                    copy.start()
+            else:
+                result[...] = total[y, x].astype(jnp.float32) + from_second[...].astype(jnp.float32)
+                leg["store"]().start()
+        elif lined:
+            for copy in leg["line"]():
+                copy.wait_recv()
+            summed = total[y, x, z].astype(jnp.float32)
+            for away in range(3):
+                summed = summed + from_line[away].astype(jnp.float32)
+            result[...] = summed
+            leg["store"]().start()
+
+    for number in range(2 * ahead):
+        begin(number)
+    pairs = -(-amount // 2)
+    for turn in range(pairs + 3):
+        for stage in range(4):
+            for number in (2 * (turn - stage), 2 * (turn - stage) + 1):
+                advance(number, stage)
+                if stage == 0 and number >= 0:
+                    begin(number + 2 * ahead)
+    for number in range(amount):
+        leg = legs(number)
+        for copy in [leg["core"](), leg["first"](), leg["second"]()] + leg["line"]():
+            copy.wait_send()
+        leg["store"]().wait()
+
+
+def pallas_reduce(parts, steps, name_id, lined=True, ahead=2):
+    shapes = [part.shape[1:] for part in parts]
+    pieces = []
+    for index, (shape, (row_step, column_step)) in enumerate(zip(shapes, steps)):
+        pieces += cut(index, shape[0], shape[1], row_step, column_step)
+    count, amount = len(parts), len(pieces)
+    anywhere = pl.BlockSpec(memory_space=pl.ANY)
+    room = []
+    for array, _, rows, _, columns in pieces:
+        kind = parts[array].dtype
+        deep = (4,) if lined else ()
+        for lead in ((2, 2) + deep, (2, 2) + deep, (2,) + deep, deep, (3,) if lined else (1,)):
+            room.append(pltpu.VMEM(lead + (rows, columns), kind))
+        room.append(pltpu.VMEM((rows, columns), jnp.float32))
+    return pl.pallas_call(
+        partial(reduce_kernel, pieces, ahead, count, lined),
+        in_specs=[anywhere] * count,
+        out_specs=[anywhere] * count,
+        out_shape=[jax.ShapeDtypeStruct(shape, jnp.float32) for shape in shapes],
+        scratch_shapes=[
+            pltpu.SemaphoreType.DMA((amount, 6)),
+            pltpu.SemaphoreType.DMA((amount, 6)),
+            pltpu.SemaphoreType.DMA((amount,)),
+            pltpu.SemaphoreType.DMA((amount,)),
+        ] + room,
+        compiler_params=pltpu.CompilerParams(
+            collective_id=name_id, has_side_effects=True, vmem_limit_bytes=VMEM_MOST
+        ),
+        )(*[part.reshape((2, 2, 2) + ((4,) if lined else ()) + shape) for part, shape in zip(parts, shapes)])
+
+
+def chained_states(local, through, step):
+    count = lax.axis_size("ctx")
+    total, factor = None, None
+    rows = jnp.pad(through[:, None], ((0, 0), (0, 127)))
+    for away in range(1, count):
+        arrived = from_behind(local, "ctx", step * away).astype(jnp.float32)
+        if factor is not None:
+            arrived = (arrived.reshape(HEADS, HEAD, STATE) * factor[:, None, None]).reshape(DI, STATE)
+        total = arrived if total is None else total + arrived
+        if away < count - 1:
+            passed = from_behind(rows, "ctx", step * away)[:, 0]
+            factor = passed if factor is None else factor * passed
+    return half(total)
+
+
+BOTH = ("dp", "ctx")
+
+
+def after(values, *earlier):
+    return lax.optimization_barrier((values, earlier))[0]
+
+
+def two_parts(value):
+    high = value.astype(jnp.bfloat16)
+    low = (value - high.astype(jnp.float32)).astype(jnp.bfloat16)
+    return high, low
+
+
+def route_table(routes, expert_count):
+    named = jnp.any(
+        routes[:, :, None] == jnp.arange(expert_count, dtype=jnp.int32), axis=1
+    )
+    rows = routes.shape[0]
+    earlier = jnp.tril(jnp.ones((rows, rows), jnp.bfloat16), -1)
+    ranks = jnp.dot(earlier, named.astype(jnp.bfloat16), preferred_element_type=jnp.float32)
+    return named, jnp.where(named, ranks, -1.0)
+
+
+def on_device(
+    layer_in,
+    seg_ids,
+    route_ids,
+    out_grad,
+    norm_in,
+    w_in,
+    conv_w,
+    conv_b,
+    dt_bias,
+    a_log,
+    d_skip,
+    norm_gate,
+    w_out,
+    norm_mid,
+    w_router,
+    w_sgate,
+    w_sup,
+    w_sdown,
+    e_gate,
+    e_up,
+    e_down,
+):
+    f32, bf16 = jnp.float32, jnp.bfloat16
+    row_count, d_model = layer_in.shape[1:]
+    devices = lax.axis_size("dp") * lax.axis_size("ctx")
+    ctx_place = lax.axis_index("ctx")
+    first_expert = lax.axis_index("dp") * EXP_DEV
+    blocks = lax.axis_size("dp")
+    expert_count = EXP_DEV * blocks
+    capacity = row_count * TOP * 5 // (expert_count * 4)
+    slots = -(-capacity // 64) * 64
+    tap_count = conv_w.shape[0]
+    halo = 8
+
+    small_parts = (norm_in, conv_w, conv_b, norm_gate, norm_mid, w_router)
+    small_flat = jnp.concatenate([part.reshape(-1) for part in small_parts])
+    small_flat = jnp.pad(small_flat, (0, 4096 - small_flat.shape[0])).reshape(32, 128)
+    w_in_all, small_all = pallas_gather([w_in, small_flat], [(16, 1664), (32, 128)], 1)
+    small_all = small_all.reshape(devices, 4096)
+    taken, pieces = 0, []
+    for part in small_parts:
+        pieces.append(small_all[:, taken : taken + part.size])
+        taken += part.size
+    gain_in = pieces[0].reshape(-1).astype(f32)
+    conv_weight = jnp.moveaxis(pieces[1].reshape(devices, tap_count, -1), 0, 1).reshape(tap_count, CONV).astype(f32)
+    conv_bias = pieces[2].reshape(-1).astype(f32)
+    gain_gate = pieces[3].reshape(-1).astype(f32)
+    gain_mid = pieces[4].reshape(-1).astype(f32)
+    router_weight = pieces[5].reshape(d_model, expert_count)
+    weight_in = w_in_all.reshape(d_model, PROJ)
+    expert_gate = lax.all_gather(e_gate, "ctx", axis=1, tiled=True)
+    expert_up = lax.all_gather(e_up, "ctx", axis=1, tiled=True)
+    expert_down = lax.all_gather(e_down, "ctx", axis=2, tiled=True)
+    named, ranks = route_table(route_ids[0], expert_count)
+
+    own_in = layer_in[0]
+    edge_in = from_behind(own_in[row_count - halo :], "ctx", 1)
+    input_f = jnp.concatenate(
+        [own_in, jnp.zeros((128 - halo, d_model), bf16), edge_in], axis=0
+    ).astype(f32)
+    normed = scaled_norm(input_f, gain_in).astype(bf16)
+    projected = lax.dot_general(
+        weight_in, normed, (((0,), (1,)), ((), ())), preferred_element_type=f32
+    )
+    seg_pad = jnp.concatenate([jnp.full((tap_count - 1,), -1, jnp.int32), seg_ids[0]])
+    seg_window = lax.dynamic_slice_in_dim(
+        seg_pad, ctx_place * row_count, row_count + tap_count - 1, 0
+    )
+    taps = jnp.concatenate(
+        [conv_weight.T, conv_bias[:, None], jnp.zeros((CONV, 7 - tap_count), f32)], axis=1
+    )
+    dt_raw = projected[DI + CONV :, :row_count]
+    dt_pos, decay, cumul, cumul_col, flags, seg_col, masks, through, skip_rows = mixer_rows(
+        dt_raw, dt_bias, a_log, d_skip, seg_window, tap_count
+    )
+    bc_pre, pre, state_out = mixer_forward_states(projected, taps, masks, dt_pos, cumul, flags)
+    state_in = chained_states(state_out, through, 1)
+    w_out_all, sgate_all, sup_all, sdown_all = pallas_gather(
+        after([w_out, w_sgate, w_sup, w_sdown], state_out),
+        [(16, 1536), (16, 1024), (16, 1024), (16, 1536)],
+        2,
+    )
+    weight_out = w_out_all.reshape(DI, d_model)
+    sgate_weight = sgate_all.reshape(d_model, -1)
+    sup_weight = sup_all.reshape(d_model, -1)
+    sdown_weight = sdown_all.reshape(-1, d_model)
+    y_inner = mixer_forward_inner(pre, bc_pre, dt_pos, cumul, cumul_col, skip_rows, flags, seg_col)
+    gain_col = jnp.broadcast_to(gain_gate[:, None], (DI, 8))
+    y_heads, gated, gate_scale = mixer_forward_join(
+        after(y_inner, weight_out), state_in, bc_pre, cumul, projected, gain_col, flags
+    )
+
+    mixed = times_rows(gated, weight_out)
+    resid_mid = own_in.astype(f32) + mixed
+    normed_mid_f, pull_mid = jax.vjp(scaled_norm, resid_mid, gain_mid)
+    normed_mid = normed_mid_f.astype(bf16)
+    logits = jnp.dot(normed_mid, router_weight, preferred_element_type=f32)
+    top_logit = jnp.max(jnp.where(named, logits, -jnp.inf), axis=-1, keepdims=True)
+    powers = jnp.where(named, jnp.exp(jnp.where(named, logits - top_logit, 0.0)), 0.0)
+    gates = powers / jnp.sum(powers, axis=-1, keepdims=True)
+    gate_high, gate_low = two_parts(gates)
+    side = jnp.concatenate(
+        [gate_high, gate_low, ranks.astype(bf16), jnp.zeros((row_count, 128 - 3 * expert_count), bf16)],
+        axis=1,
+    )
+    token_rows, grad_rows, side_all = pallas_gather(
+        [normed_mid, out_grad[0], side], [(16, 1536), (16, 1536), (128, 128)], 3, lined=False, ahead=4
+    )
+    shared_gate = jnp.dot(normed_mid, sgate_weight, preferred_element_type=f32)
+    shared_up = jnp.dot(normed_mid, sup_weight, preferred_element_type=f32)
+    shared_act = (jax.nn.silu(shared_gate) * shared_up).astype(bf16)
+    shared_out = jnp.dot(shared_act, sdown_weight, preferred_element_type=f32)
+
+    mine_of = partial(lax.dynamic_slice_in_dim, slice_size=EXP_DEV, axis=2)
+    my_gate = mine_of(side_all, first_expert).astype(f32) + mine_of(
+        side_all, first_expert + expert_count
+    ).astype(f32)
+    my_rank = mine_of(side_all, first_expert + 2 * expert_count).astype(f32)
+    my_gate, my_rank = jnp.swapaxes(my_gate, 1, 2), jnp.swapaxes(my_rank, 1, 2)
+    chosen = my_rank[:, :, None, :] == jnp.arange(slots, dtype=f32)[None, None, :, None]
+    select = chosen.astype(bf16)
+    slot_gate = jnp.sum(jnp.where(chosen, my_gate[:, :, None, :], 0.0), axis=-1)
+    gate_col = jnp.swapaxes(slot_gate, 0, 1).reshape(EXP_DEV, blocks * slots, 1)
+
+    def to_slots(rows):
+        taken = jnp.einsum("best,btd->ebsd", select, rows, preferred_element_type=f32)
+        return taken.astype(bf16).reshape(EXP_DEV, blocks * slots, -1)
+
+    def to_tokens(rows):
+        rows = rows.reshape(EXP_DEV, blocks, slots, -1)
+        return jnp.einsum("best,ebsd->btd", select, rows, preferred_element_type=f32).astype(bf16)
+
+    def each(spec, left, right):
+        return jnp.einsum(spec, left, right, preferred_element_type=f32)
+
+    slot_in = to_slots(token_rows)
+    slot_grad = to_slots(grad_rows)
+    hidden_gate = each("erd,edf->erf", slot_in, expert_gate)
+    hidden_up = each("erd,edf->erf", slot_in, expert_up)
+    hidden_act = (jax.nn.silu(hidden_gate) * hidden_up).astype(bf16)
+    expert_out = each("erf,efd->erd", hidden_act, expert_down).astype(bf16)
+    slot_dgate = jnp.sum(slot_grad.astype(f32) * expert_out.astype(f32), axis=-1)
+    grad_out_slots = (gate_col * slot_grad).astype(bf16)
+    grad_act = each("erd,efd->erf", grad_out_slots, expert_down)
+    grad_e_down = each("erf,erd->efd", hidden_act, grad_out_slots)
+    grad_hgate = (grad_act * hidden_up * silu_slope(hidden_gate)).astype(bf16)
+    grad_hup = (grad_act * jax.nn.silu(hidden_gate)).astype(bf16)
+    grad_slots = (
+        each("erf,edf->erd", grad_hgate, expert_gate) + each("erf,edf->erd", grad_hup, expert_up)
+    ).astype(bf16)
+    slot_dgate = jnp.swapaxes(slot_dgate.reshape(EXP_DEV, blocks, slots), 0, 1)
+    token_dgate = jnp.sum(jnp.where(chosen, slot_dgate[..., None], 0.0), axis=2)
+    held = jnp.arange(EXP_DEV, dtype=jnp.int32)[:, None] + first_expert
+    dgate_table = jnp.sum(
+        token_dgate[..., None] * (jnp.arange(expert_count) == held).astype(f32)[:, None, :], axis=1
+    )
+    dgate_high, dgate_low = two_parts(dgate_table)
+    back_side = jnp.concatenate(
+        [dgate_high, dgate_low, jnp.zeros((blocks, row_count, 128 - 2 * expert_count), bf16)], axis=-1
+    )
+    back_rows, routed, back_side = pallas_reduce(
+        [to_tokens(grad_slots), to_tokens((gate_col * expert_out).astype(bf16)), back_side],
+        [(32, 1536), (32, 1536), (128, 128)],
+        4,
+        lined=False,
+    )
+    grad_e_gate = each("erd,erf->edf", slot_in, grad_hgate)
+    grad_e_up = each("erd,erf->edf", slot_in, grad_hup)
+
+    def to_owner(grad, axis):
+        sent = lax.psum_scatter(grad.astype(bf16), "ctx", scatter_dimension=axis + 1, tiled=True)
+        return sent.astype(f32)
+
+    expert_grads = (to_owner(grad_e_gate, 0), to_owner(grad_e_up, 0), to_owner(grad_e_down, 1))
+
+    layer_out = (resid_mid + shared_out + routed).astype(bf16)[None]
+    grad_top = out_grad[0].astype(f32)
+    grad_shared_out = out_grad[0]
+    grad_w_sdown = times_rows(shared_act, grad_shared_out)
+    grad_shared_act = times_back(grad_shared_out, sdown_weight)
+    grad_sgate = (grad_shared_act * shared_up * silu_slope(shared_gate)).astype(bf16)
+    grad_sup = (grad_shared_act * jax.nn.silu(shared_gate)).astype(bf16)
+    grad_w_sgate = times_rows(normed_mid, grad_sgate)
+    grad_w_sup = times_rows(normed_mid, grad_sup)
+    grad_mid_shared = times_back(grad_sgate, sgate_weight) + times_back(grad_sup, sup_weight)
+    grad_gates = back_side[:, :expert_count] + back_side[:, expert_count : 2 * expert_count]
+    grad_pick = gates * (grad_gates - jnp.sum(gates * grad_gates, axis=-1, keepdims=True))
+    grad_logits = grad_pick.astype(bf16)
+    grad_w_router = times_rows(normed_mid, grad_logits)
+    grad_mid = (
+        back_rows + grad_mid_shared + times_back(grad_logits, router_weight)
+    )
+    grad_resid_part, grad_gain_mid = pull_mid(grad_mid)
+    grad_resid = grad_top + grad_resid_part
+    grad_mixed = grad_resid.astype(bf16)
+
+    def owned(grad):
+        return grad.astype(bf16).reshape(devices, -1, grad.shape[-1])
+
+    grad_w_out = jnp.dot(gated, grad_mixed, preferred_element_type=f32)
+    grad_gated = times_back(weight_out, grad_mixed)
+    scaled_u = y_heads * jax.nn.silu(projected[:DI, :row_count])
+    scale_row = gate_scale[:1]
+    along = jnp.sum(grad_gated * gain_gate[:, None] * scaled_u, axis=0, keepdims=True)
+    grad_gain_gate = jnp.sum(grad_gated * scaled_u * scale_row, axis=1)
+    gate_rows = jnp.concatenate(
+        [scale_row, scale_row * scale_row * scale_row * along * (1.0 / DI), jnp.zeros((6, row_count), f32)]
+    )
+    grad_y, grad_z, grad_state_local = mixer_back_gate(
+        y_heads, projected, grad_gated, gain_col, gate_rows, bc_pre, cumul, flags
+    )
+    grad_state_out = chained_states(grad_state_local, through, -1)
+    sum_out, sum_sgate, sum_sup, sum_sdown = pallas_reduce(
+        after(
+            [owned(grad_w_out), owned(grad_w_sgate), owned(grad_w_sup), owned(grad_w_sdown)],
+            grad_state_local,
+        ),
+        [(16, 1536), (16, 1024), (16, 1024), (16, 1536)],
+        5,
+    )
+    grad_scaled, grad_cum_inner, grad_skip, grad_bc_inner = mixer_back_inner(
+        pre, grad_y, bc_pre, dt_pos, cumul, cumul_col, flags, seg_col
+    )
+    grad_x, grad_taps_x, grad_dt, grad_cum_join, grad_last, grad_bc_join = mixer_back_join(
+        after(grad_scaled, sum_out), grad_y, pre, projected, taps, masks, state_in, grad_state_out,
+        bc_pre, dt_pos, cumul, skip_rows, flags,
+    )
+    grad_bc, grad_taps_bc = mixer_back_conv(
+        grad_bc_inner + grad_bc_join, bc_pre, projected, taps, masks
+    )
+    grad_cum = grad_cum_inner + grad_cum_join
+    grad_last = grad_last[:, 0] + through * grad_last[:, 1]
+    lower = jnp.tril(jnp.ones((row_count, row_count), f32))
+    grad_decay = jnp.dot(grad_cum, lower, precision=lax.Precision.HIGHEST) + grad_last[:, None]
+    grad_dt = grad_dt - jnp.exp(a_log)[:, None] * grad_decay
+    grad_raw = grad_dt * jax.nn.sigmoid(dt_raw + dt_bias[:, None])
+    grad_taps = jnp.concatenate([grad_taps_x, grad_taps_bc])
+    grad_conv_w, grad_conv_b = grad_taps[:, :tap_count].T, grad_taps[:, tap_count]
+    head_sums_all = jnp.concatenate(
+        [jnp.sum(grad_raw, axis=1), jnp.sum(decay * grad_decay, axis=1), jnp.sum(grad_skip, axis=1)]
+    )
+    grad_proj = jnp.concatenate(
+        [
+            jnp.pad(grad_z, ((0, 0), (0, 128))),
+            grad_x,
+            grad_bc,
+            jnp.pad(grad_raw.astype(bf16), ((0, 0), (0, 128))),
+        ]
+    )
+    grad_w_in = lax.dot_general(
+        normed, grad_proj, (((0,), (1,)), ((), ())), preferred_element_type=f32
+    )
+    grad_normed = lax.dot_general(
+        grad_proj, weight_in, (((0,), (1,)), ((), ())), preferred_element_type=f32
+    )
+    edge_grad = from_behind(grad_normed[row_count + 128 - halo :], "ctx", -1)
+    grad_normed = jnp.concatenate(
+        [grad_normed[: row_count - halo], grad_normed[row_count - halo : row_count] + edge_grad],
+        axis=0,
+    )
+    _, pull_in = jax.vjp(scaled_norm, own_in.astype(f32), gain_in)
+    grad_input_part, grad_gain_in = pull_in(grad_normed)
+    grad_in = (grad_resid + grad_input_part)[None]
+
+    small_grads = jnp.concatenate(
+        [
+            grad_gain_in.reshape(devices, -1),
+            jnp.moveaxis(grad_conv_w.reshape(tap_count, devices, -1), 1, 0).reshape(devices, -1),
+            grad_conv_b.reshape(devices, -1),
+            grad_gain_gate.reshape(devices, -1),
+            grad_gain_mid.reshape(devices, -1),
+            grad_w_router.reshape(devices, -1),
+            jnp.broadcast_to(head_sums_all, (devices, 3 * HEADS)),
+        ],
+        axis=1,
+    )
+    small_grads = jnp.pad(small_grads, ((0, 0), (0, 3072 - small_grads.shape[1])))
+    sum_in, sum_small = pallas_reduce(
+        [owned(grad_w_in), small_grads.reshape(devices, 24, 128)], [(16, 1664), (24, 128)], 6
+    )
+    sum_small = sum_small.reshape(-1)
+    taken, mine = 0, []
+    for part in small_parts:
+        mine.append(sum_small[taken : taken + part.size].reshape(part.shape))
+        taken += part.size
+    return (
+        layer_out,
+        grad_in,
+        mine[0],
+        sum_in,
+        mine[1],
+        mine[2],
+        sum_small[taken : taken + HEADS],
+        sum_small[taken + HEADS : taken + 2 * HEADS],
+        sum_small[taken + 2 * HEADS : taken + 3 * HEADS],
+        mine[3],
+        sum_out,
+        mine[4],
+        mine[5],
+        sum_sgate,
+        sum_sup,
+        sum_sdown,
+        expert_grads[0],
+        expert_grads[1],
+        expert_grads[2],
+    )
+
+
 def solution(mesh):
     in_specs = (
         P("dp", "ctx", None),
@@ -570,6 +1603,7 @@
         P("dp", "ctx", None),
         P("dp", None, "ctx"),
     )
+    one_each = mesh.shape["ctx"] == EXP_DEV and mesh.shape["dp"] == 8
     return jax.shard_map(
-        on_device, mesh=mesh, in_specs=in_specs, out_specs=out_specs, check_vma=False
-    )
+        on_device if one_each else on_device_general, mesh=mesh, in_specs=in_specs, out_specs=out_specs, check_vma=False
+    )

time: 3200 us -> 1370 us (0.43)
  waiting for transfers between devices: 1790 us -> 17.7 us
  Pallas kernels: 0 us -> 909 us
  local copies, waits for them, and re-layouts: 563 us -> 108 us
  other arithmetic: 261 us -> 48.7 us
  blocking collectives: 196 us -> 0 us
  matrix products: 305 us -> 234 us
    reduce_scatter x7 -> x2, waiting for transfers between devices: 1160 us -> 0.01 us  [to_owner(): lax.psum_scatter(grad.astype(bf16), 'ctx', scatter_dimension=axis + 1, ti...]
    pallas_call x0 -> x14, Pallas kernels: none -> 909 us  [the longest x3 445 us: pallas_gather(): pl.pallas_call(partial(gather_kernel, pieces, ahead, count, lined), in_sp...]
    unnamed x23 -> x7, waiting for transfers between devices: 270 us -> 1.44 us
    all_gather x10 -> x3, waiting for transfers between devices: 268 us -> 0.01 us  [the longest x1 0.01 us: on_device(): expert_gate = lax.all_gather(e_gate, 'ctx', axis=1, tiled=True)]
    dynamic_update_slice x10 -> x0, local copies, waits for them, and re-layouts: 149 us -> none  [scan_blocks(): lax.scan(jax.checkpoint(block_step), (memory, previous), inputs)]
    all_gather x2 -> x0, blocking collectives: 142 us -> none  [the longest x1 75.3 us: on_device(): lax.all_gather(w_router, ('dp', 'ctx'), axis=0, tiled=True)]
    all_to_all x4 -> x0, waiting for transfers between devices: 90.9 us -> none  [the longest x1 51.4 us: on_device(): lax.all_to_all(grad_slots, 'dp', split_axis=0, concat_axis=1, tiled=True)]
    gather x9 -> x0, local copies, waits for them, and re-layouts: 78.8 us -> none  [the longest x2 19.5 us: on_device(): grad_pad[token_of]]
  transfers between devices with their start and end apart: 26 -> 18, of which waited for: 18 -> 2; matrix products, arithmetic and copies ran while one was open for 26% -> 24% of each run, Pallas kernels for 0% -> 67%
where the time goes in v1:
time: 1370 us; the launch traced here: 1360 us
  Pallas kernels  909 us (66%)
  matrix products  234 us (17%)
  local copies, waits for them, and re-layouts  108 us (8%)
  other arithmetic  48.7 us (4%)
  starting transfers between devices  23.4 us (2%)
  waiting for transfers between devices  17.7 us (1%)
  between operations  17.4 us (1%)
    pallas_call x3, Pallas kernels, pallas_gather(): pl.pallas_call(partial(gather_kernel, pieces, ahead, count, lined), in_sp...  445 us
    pallas_call x3, Pallas kernels, pallas_reduce(): pl.pallas_call(partial(reduce_kernel, pieces, ahead, count, lined), in_sp...  387 us
    dot_general x9, matrix products, each(): return jnp.einsum(spec, left, right, preferred_element_type=f32)  103 us
    pallas_call x8, Pallas kernels, call_steps(): pl.pallas_call(kernel, grid=(steps,), in_specs=in_specs, out_specs=out_sp...  76.7 us
    unnamed x207, local copies, waits for them, and re-layouts  43.6 us
  transfers between devices with their start and end apart: 18, of which 2 were waited for; matrix products, arithmetic and copies ran while one was open for 24% of the time, Pallas kernels for 67%

profile of v1, /device:TPU:0, one launch (start us, length us, event | category | flops | bytes accessed | tf_op | source)
XLA Modules:
  0.0 1358.3 jit_solution(8665312976764216997)
XLA Ops:
  8.8 4.9 collective-permute-start
  14.9 149.8 %shard_map.348 = (bf16[2,2,2,4,48,6448]{5,4,3,2,1,0:T(8,128)(2,1)}, bf16[2,2,2,4,32,128]{5,4,3,2,1,0:T(8,128)(2,1)}) custom-call(bf16[48,6448]{1,0:T(8,128)(2,1)} %refs_0_.1, bf16[32,128]{1,0:T(8,128)(2,1)} %pad_bitcast_fusion.1.refs_1_), custom_call_target="tpu_custom_call" | custom-call | tf_op jit(solution)/shard_map/pallas_call | solution.py:1049
  176.3 14.5 %fusion.71.x_ref.z_ref = f32[6448,384]{1,0:T(8,128)S(1)} fusion(bf16[1536,6448]{1,0:T(8,128)(2,1)} %bitcast.230, f32[1536]{0:T(1024)S(1)} %reshape.335, f32[384]{0:T(512)S(1)} %add_rsqrt_fusion, bf16[8,1536]{1,0:T(8,128)(2,1)S(1)} %collective-permute-done, bf16[256,1536]{1,0:T(8,128)(2,1)S(1)} %bitcast.176, bf16[384]{0:T(512)(128)(2,1)S(1)} %pad.65.clone), kind=kOutput, calls=%fused_computation.188 | convolution fusion | flops 7611678720 | bytes 30531840 | tf_op jit(solution)/shard_map/dot_general | solution.py:1314
  190.9 3.8 copy-done
  198.1 10.0 shard_map.350
  212.1 3.6 collective-permute-start.1
  221.3 7.8 shard_map.351.y_ref
  229.1 227.2 %shard_map.352 = (bf16[2,2,2,4,96,1536]{5,4,3,2,1,0:T(8,128)(2,1)}, bf16[2,2,2,4,48,1024]{5,4,3,2,1,0:T(8,128)(2,1)}, bf16[2,2,2,4,48,1024]{5,4,3,2,1,0:T(8,128)(2,1)}, bf16[2,2,2,4,32,1536]{5,4,3,2,1,0:T(8,128)(2,1)}) custom-call(bf16[96,1536]{1,0:T(8,128)(2,1)} %refs_0_.2, bf16[48,1024]{1,0:T(8,128)(2,1)} %refs_1_, bf16[48,1024]{1,0:T(8,128)(2,1)} %refs_2_, ...), custom_call_target="tpu_custom_call" | custom-call | tf_op jit(solution)/shard_map/pallas_call | solution.py:1049
  457.0 3.4 add_convert_fusion.2.state_ref
  462.0 10.9 shard_map.353
  472.9 5.9 multiply_reduce_fusion.4
  482.4 68.2 %shard_map.354 = (bf16[2,2,2,256,1536]{4,3,2,1,0:T(8,128)(2,1)}, bf16[2,2,2,256,1536]{4,3,2,1,0:T(8,128)(2,1)}, bf16[2,2,2,256,128]{4,3,2,1,0:T(8,128)(2,1)}) custom-call(bf16[256,1536]{1,0:T(8,128)(2,1)} %copy-done.1, bf16[256,1536]{1,0:T(8,128)(2,1)} %bitcast.179, bf16[256,128]{1,0:T(8,128)(2,1)} %maximum_maximum_fusion.2.refs_2_), custom_call_target="tpu_custom_call" | custom-call | tf_op jit(solution)/shard_map/pallas_call | solution.py:1049
  552.2 4.6 convert_bitcast_fusion.1
  559.9 9.0 convert_bitcast_fusion
  569.0 11.1 copy.148
  580.8 10.2 fusion.83
  590.9 20.1 %multiply_convert_fusion = (bf16[4,512,512]{2,1,0:T(8,128)(2,1)}, f32[4,512,512]{2,1,0:T(8,128)}) fusion(f32[4,512,512]{2,1,0:T(8,128)} %fusion.83, bf16[4,512,1536]{2,1,0:T(8,128)(2,1)} %bitcast.181, bf16[4,1536,512]{2,1,0:T(8,128)(2,1)} %all-gather.6.cloned.1.call-done), kind=kOutput, calls=%fused_computation.26 | convolution fusion | flops 3227516928 | bytes 23068672 | tf_op jit(solution)/shard_map/erd,edf->erf/dot_general | solution.py:1386
  611.0 13.0 fusion.1
  625.1 10.8 fusion
  638.6 5.3 convolution_convert_fusion.2
  643.9 11.2 copy.176
  655.1 8.1 copy.181
  663.4 13.0 multiply_convert_fusion.1
  677.8 9.2 convolution_convert_fusion.4
  691.5 6.9 collective-permute-done.8
  698.5 9.4 collective-permute-done.10
  728.8 9.6 fusion.84
  738.4 13.3 add_convert_fusion
  751.7 7.2 bitcast_convert_fusion.1
  758.9 7.4 bitcast_convert_fusion
  766.3 62.3 %shard_map.355 = (f32[256,1536]{1,0:T(8,128)}, f32[256,1536]{1,0:T(8,128)}, f32[256,128]{1,0:T(8,128)}) custom-call(bf16[2,2,2,256,1536]{4,3,2,1,0:T(8,128)(2,1)} %bitcast.184, bf16[2,2,2,256,1536]{4,3,2,1,0:T(8,128)(2,1)} %bitcast.186, bf16[2,2,2,256,128]{4,3,2,1,0:T(8,128)(2,1)} %maximum_maximum_fusion.refs_2_), custom_call_target="tpu_custom_call" | custom-call | tf_op jit(solution)/shard_map/pallas_call | solution.py:1197
  831.0 3.5 fusion.12
  838.5 7.1 multiply_reduce_fusion
  847.0 8.7 shard_map.356
  859.6 9.3 convolution_convert_fusion.3
  868.9 14.9 %shard_map.357 = (f32[3072,256]{1,0:T(8,128)}, f32[48,256]{1,0:T(8,128)}, f32[48,256]{1,0:T(8,128)}, f32[256,256]{1,0:T(8,128)}) custom-call(f32[3072,256]{1,0:T(8,128)} %get-tuple-element.69.pre_ref, f32[3072,256]{1,0:T(8,128)} %get-tuple-element.90.grad_y_ref, f32[256,256]{1,0:T(8,128)} %shard_map.349.bc_ref.pre_ref, f32[48,256]{1,0:T(8,128)} %copy-done.38, ...), custom_call_target="tpu_custom_call" | custom-call | flops 53687091200 | bytes 8388608 | tf_op jit(solution)/shard_map/pallas_call | solution.py:567
  883.9 5.0 convolution_convert_fusion.1
  888.9 214.5 %shard_map.358 = (f32[96,1536]{1,0:T(8,128)}, f32[48,1024]{1,0:T(8,128)}, f32[48,1024]{1,0:T(8,128)}, f32[32,1536]{1,0:T(8,128)}) custom-call(bf16[2,2,2,4,96,1536]{5,4,3,2,1,0:T(8,128)(2,1)} %bitcast.166, bf16[2,2,2,4,48,1024]{5,4,3,2,1,0:T(8,128)(2,1)} %bitcast.169, bf16[2,2,2,4,48,1024]{5,4,3,2,1,0:T(8,128)(2,1)} %bitcast.170, ...), custom_call_target="tpu_custom_call" | custom-call | tf_op jit(solution)/shard_map/pallas_call | solution.py:1197
  1106.4 4.4 fusion.14
  1110.8 3.6 add_convert_fusion.1.grad_state_ref
  1114.4 18.6 %shard_map.359 = (bf16[3072,384]{1,0:T(8,128)(2,1)}, f32[3072,8]{1,0:T(8,128)}, f32[48,256]{1,0:T(8,128)}, f32[48,256]{1,0:T(8,128)}, f32[48,128]{1,0:T(8,128)}, /*index=5*/f32[256,256]{1,0:T(8,128)}) custom-call(f32[3072,256]{1,0:T(8,128)} %get-tuple-element.98.grad_in_ref, f32[3072,256]{1,0:T(8,128)} %get-tuple-element.90.grad_y_ref, ...), custom_call_target="tpu_custom_call" | custom-call | flops 1073741824 | bytes 8388608 | tf_op jit(solution)/shard_map/pallas_call | solution.py:567
  1134.8 3.3 shard_map.360
  1139.7 19.2 %fusion.74 = f32[384,1536]{1,0:T(8,128)} fusion(bf16[1536,6448]{1,0:T(8,128)(2,1)} %bitcast.231, bf16[48,256]{1,0:T(8,128)(2,1)S(1)} %get-tuple-element.200, bf16[3072,256]{1,0:T(8,128)(2,1)} %get-tuple-element.89, bf16[256,384]{1,0:T(8,128)(2,1)} %get-tuple-element.102, bf16[3072,384]{1,0:T(8,128)(2,1)} %get-tuple-element.99), kind=kOutput, calls=%fused_computation.189 | convolution fusion | flops 7636082688 | bytes 26320896 | tf_op jit(solution)/shard_map/dot_general | solution.py:1505
  1161.6 22.5 %convolution_convert_fusion = bf16[1536,6448]{0,1:T(8,128)(2,1)} fusion(f32[1536]{0:T(1024)S(1)} %copy-done.50, f32[384]{0:T(512)S(1)} %copy-done.77, bf16[8,1536]{1,0:T(8,128)(2,1)S(1)} %copy-done.59, bf16[256,1536]{1,0:T(8,128)(2,1)S(1)} %bitcast.177, bf16[384]{0:T(512)(128)(2,1)S(1)} %copy-done.72, bf16[48,256]{1,0:T(8,128)(2,1)S(1)} %get-tuple-element.200, ...), kind=kOutput, calls=%fused_computation | convolution fusion | flops 7651295232 | bytes 24781056 | tf_op jit(solution)/shard_map/dot_general | solution.py:1502
  1185.7 25.1 %copy.157 = bf16[1536,6448]{1,0:T(8,128)(2,1)} copy(bf16[1536,6448]{0,1:T(8,128)(2,1)} %convolution_convert_fusion) | data formatting | bytes 39616512 | tf_op jit(solution)/shard_map/convert_element_type | solution.py:1450
  1213.8 109.9 %shard_map.361 = (f32[48,6448]{1,0:T(8,128)}, f32[24,128]{1,0:T(8,128)}) custom-call(bf16[2,2,2,4,48,6448]{5,4,3,2,1,0:T(8,128)(2,1)} %bitcast.165, f32[2,2,2,4,24,128]{5,4,3,2,1,0:T(8,128)} %bitcast.201), custom_call_target="tpu_custom_call" | custom-call | tf_op jit(solution)/shard_map/pallas_call | solution.py:1197
  1339.8 3.5 convert_element_type.332
  1343.4 3.7 convert_element_type.334
  (388 shorter events, 112.1 us)
Async XLA Ops:
  7.3 158.7 %copy-start.73 = (s32[1,1024]{1,0:T(1,128)S(1)}, s32[1,1024]{1,0:T(1,128)}, u32[]{:S(2)}) copy-start(s32[1,1024]{1,0:T(1,128)} %param.22) | copy-start | bytes 12292
  7.3 160.0 %copy-start.70 = (s32[1,256,6]{1,0,2:T(1,128)S(1)}, s32[1,256,6]{1,0,2:T(1,128)}, u32[]{:S(2)}) copy-start(s32[1,256,6]{1,0,2:T(1,128)} %param.23) | copy-start | bytes 18436
  7.3 573.5 %all-gather.8.cloned.1.call-start = ((), (), s32[]{:S(2)}) async-start(), calls=%async_computation.5 | async-start | bytes 7864320 | tf_op jit(solution)/shard_map/all_gather | solution.py:1303
  8.0 162.5 %copy-start.91 = (f32[48]{0:T(128)S(1)}, f32[48]{0:T(128)}, u32[]{:S(2)}) copy-start(f32[48]{0:T(128)} %param.30) | copy-start | bytes 580
  8.0 582.9 %all-gather.6.cloned.1.call-start = ((), (), s32[]{:S(2)}) async-start(), calls=%async_computation.4 | async-start | bytes 7864320 | tf_op jit(solution)/shard_map/all_gather | solution.py:1304
  8.8 602.3 %all-gather.4.cloned.1.call-start = ((), (), s32[]{:S(2)}) async-start(), calls=%async_computation.3 | async-start | bytes 7864320 | tf_op jit(solution)/shard_map/all_gather | solution.py:1305
  8.8 167.0 %collective-permute-start = (bf16[8,1536]{1,0:T(8,128)(2,1)S(1)}, bf16[8,1536]{1,0:T(8,128)(2,1)S(1)}, u32[]{:S(2)}, u32[]{:S(2)}) collective-permute-start(bf16[8,1536]{1,0:T(8,128)(2,1)S(1)} %slice_bitcast_fusion), channel_id=1, source_target_pairs={{0,1},{1,2},{2,3},{4,5},{5,6},{6,7},{8,9},{9,10},{10,11},{12,13},{... | collective-permute-start | bytes 73736 | tf_op jit(solution)/shard_map/ppermute | solution.py:23
  13.8 1319.7 %reduce-scatter.10.cloned.1.call-start = ((), (), s32[]{:S(2)}) async-start(), calls=%async_computation.8 | async-start | bytes 7864320
  171.0 26.1 %copy-start.81 = (f32[48]{0:T(128)}, f32[48]{0:T(128)S(1)}, u32[]{:S(2)}) copy-start(f32[48]{0:T(128)S(1)} %get-tuple-element.229) | copy-start | bytes 580
  174.9 285.5 %copy-start.52 = (f32[3072]{0:T(1024)}, f32[3072]{0:T(1024)S(1)}, u32[]{:S(2)}) copy-start(f32[3072]{0:T(1024)S(1)} %reshape.342) | copy-start | bytes 36868
  175.0 303.9 %copy-start.45 = (f32[1536]{0:T(1024)}, f32[1536]{0:T(1024)S(1)}, u32[]{:S(2)}) copy-start(f32[1536]{0:T(1024)S(1)} %reshape.343) | copy-start | bytes 18436
  175.2 305.0 %copy-start.18 = (bf16[1536,32]{1,0:T(8,128)(2,1)}, bf16[1536,32]{1,0:T(8,128)(2,1)S(1)}, u32[]{:S(2)}) copy-start(bf16[1536,32]{1,0:T(8,128)(2,1)S(1)} %reshape.308) | copy-start | bytes 294916
  208.2 248.7 %collective-permute-start.4 = (bf16[3072,128]{1,0:T(8,128)(2,1)}, bf16[3072,128]{1,0:T(8,128)(2,1)S(1)}, u32[]{:S(2)}, u32[]{:S(2)}) collective-permute-start(bf16[3072,128]{1,0:T(8,128)(2,1)} %get-tuple-element.70), channel_id=1, source_target_pairs={{0,3},{4,7},{8,11},{12,15},{16,19},{20,23},{24,27},{28,31}} | collective-permute-start | bytes 2359304 | tf_op jit(solution)/shard_map/ppermute | solution.py:23
  210.8 246.2 %collective-permute-start.2 = (bf16[3072,128]{1,0:T(8,128)(2,1)}, bf16[3072,128]{1,0:T(8,128)(2,1)S(1)}, u32[]{:S(2)}, u32[]{:S(2)}) collective-permute-start(bf16[3072,128]{1,0:T(8,128)(2,1)} %get-tuple-element.70), channel_id=1, source_target_pairs={{0,2},{1,3},{4,6},{5,7},{8,10},{9,11},{12,14},{13,15},{16,18},{17,... | collective-permute-start | bytes 2359304 | tf_op jit(solution)/shard_map/ppermute | solution.py:23
  212.1 244.8 %collective-permute-start.1 = (bf16[3072,128]{1,0:T(8,128)(2,1)}, bf16[3072,128]{1,0:T(8,128)(2,1)}, u32[]{:S(2)}, u32[]{:S(2)}) collective-permute-start(bf16[3072,128]{1,0:T(8,128)(2,1)} %get-tuple-element.70), channel_id=1, source_target_pairs={{0,1},{1,2},{2,3},{4,5},{5,6},{6,7},{8,9},{9,10},{10,11},{12,13},{... | collective-permute-start | bytes 2359304 | tf_op jit(solution)/shard_map/ppermute | solution.py:23
  215.8 240.5 %collective-permute-start.3 = (f32[48,128]{1,0:T(8,128)S(1)}, f32[48,128]{1,0:T(8,128)S(1)}, u32[]{:S(2)}, u32[]{:S(2)}) collective-permute-start(f32[48,128]{1,0:T(8,128)S(1)} %pad.28), channel_id=1, source_target_pairs={{0,1},{1,2},{2,3},{4,5},{5,6},{6,7},{8,9},{9,10},{10,11},{12,13},{... | collective-permute-start | bytes 73736 | tf_op jit(solution)/shard_map/ppermute | solution.py:23
  217.1 239.4 %collective-permute-start.5 = (f32[48,128]{1,0:T(8,128)S(1)}, f32[48,128]{1,0:T(8,128)S(1)}, u32[]{:S(2)}, u32[]{:S(2)}) collective-permute-start(f32[48,128]{1,0:T(8,128)S(1)} %pad.28), channel_id=1, source_target_pairs={{0,2},{1,3},{4,6},{5,7},{8,10},{9,11},{12,14},{13,15},{16,18},{17,... | collective-permute-start | bytes 73736 | tf_op jit(solution)/shard_map/ppermute | solution.py:23
  663.2 676.6 %reduce-scatter.6.cloned.1.call-start = ((), (), s32[]{:S(2)}) async-start(), calls=%async_computation.6 | async-start | bytes 7864320 | tf_op jit(solution)/shard_map/reduce_scatter | solution.py:1423
  687.0 22.7 %copy-start.2 = (bf16[256,1536]{1,0:T(8,128)(2,1)S(1)}, bf16[256,1536]{1,0:T(8,128)(2,1)}, u32[]{:S(2)}) copy-start(bf16[256,1536]{1,0:T(8,128)(2,1)} %copy-done.1) | copy-start | bytes 2359300
  687.0 656.4 %reduce-scatter.8.cloned.1.call-start = ((), (), s32[]{:S(2)}) async-start(), calls=%async_computation.7 | async-start | bytes 7864320 | tf_op jit(solution)/shard_map/reduce_scatter | solution.py:1423
  687.3 26.5 %copy-start.65 = (f32[256]{0:T(256)}, f32[256]{0:T(256)S(1)}, u32[]{:S(2)}) copy-start(f32[256]{0:T(256)S(1)} %fusion.21) | copy-start | bytes 3076
  687.7 10.7 collective-permute-start.8
  690.2 17.6 %collective-permute-start.10 = (f32[48,128]{1,0:T(8,128)S(1)}, f32[48,128]{1,0:T(8,128)S(1)}, u32[]{:S(2)}, u32[]{:S(2)}) collective-permute-start(f32[48,128]{1,0:T(8,128)S(1)} %copy-done.61), channel_id=1, source_target_pairs={{2,0},{3,1},{6,4},{7,5},{10,8},{11,9},{14,12},{15,13},{18,16},{19,... | collective-permute-start | bytes 73736 | tf_op jit(solution)/shard_map/ppermute | solution.py:23
  766.3 62.4 %copy-start.34 = (f32[256,32]{1,0:T(8,128)S(1)}, f32[256,32]{1,0:T(8,128)}, u32[]{:S(2)}) copy-start(f32[256,32]{1,0:T(8,128)} %get-tuple-element.205) | copy-start | bytes 98308
  766.3 64.7 %copy-start.13 = (f32[256,1536]{1,0:T(8,128)S(1)}, f32[256,1536]{1,0:T(8,128)}, u32[]{:S(2)}) copy-start(f32[256,1536]{1,0:T(8,128)} %fusion.85) | copy-start | bytes 4718596
  766.3 64.7 %copy-start.28 = (bf16[256,1024]{1,0:T(8,128)(2,1)S(1)}, bf16[256,1024]{1,0:T(8,128)(2,1)}, u32[]{:S(2)}) copy-start(bf16[256,1024]{1,0:T(8,128)(2,1)} %copy-done.27) | copy-start | bytes 1572868
  766.3 68.3 %copy-start.19 = (bf16[1536,32]{1,0:T(8,128)(2,1)S(1)}, bf16[1536,32]{1,0:T(8,128)(2,1)}, u32[]{:S(2)}) copy-start(bf16[1536,32]{1,0:T(8,128)(2,1)} %copy-done.18) | copy-start | bytes 294916
  766.3 68.3 %copy-start.46 = (f32[1536]{0:T(1024)S(1)}, f32[1536]{0:T(1024)}, u32[]{:S(2)}) copy-start(f32[1536]{0:T(1024)} %copy-done.45) | copy-start | bytes 18436
  766.3 68.3 %copy-start.63 = (f32[256]{0:T(256)S(1)}, f32[256]{0:T(256)}, u32[]{:S(2)}) copy-start(f32[256]{0:T(256)} %copy-done.62) | copy-start | bytes 3076
  855.7 255.1 %collective-permute-start.9 = (bf16[3072,128]{1,0:T(8,128)(2,1)}, bf16[3072,128]{1,0:T(8,128)(2,1)}, u32[]{:S(2)}, u32[]{:S(2)}) collective-permute-start(bf16[3072,128]{1,0:T(8,128)(2,1)} %get-tuple-element.92), channel_id=1, source_target_pairs={{3,0},{7,4},{11,8},{15,12},{19,16},{23,20},{27,24},{31,28}} | collective-permute-start | bytes 2359304 | tf_op jit(solution)/shard_map/ppermute | solution.py:23
  857.0 253.8 %collective-permute-start.7 = (bf16[3072,128]{1,0:T(8,128)(2,1)}, bf16[3072,128]{1,0:T(8,128)(2,1)}, u32[]{:S(2)}, u32[]{:S(2)}) collective-permute-start(bf16[3072,128]{1,0:T(8,128)(2,1)} %get-tuple-element.92), channel_id=1, source_target_pairs={{2,0},{3,1},{6,4},{7,5},{10,8},{11,9},{14,12},{15,13},{18,16},{19,... | collective-permute-start | bytes 2359304 | tf_op jit(solution)/shard_map/ppermute | solution.py:23
  858.3 252.5 %collective-permute-start.6 = (bf16[3072,128]{1,0:T(8,128)(2,1)}, bf16[3072,128]{1,0:T(8,128)(2,1)}, u32[]{:S(2)}, u32[]{:S(2)}) collective-permute-start(bf16[3072,128]{1,0:T(8,128)(2,1)} %get-tuple-element.92), channel_id=1, source_target_pairs={{1,0},{2,1},{3,2},{5,4},{6,5},{7,6},{9,8},{10,9},{11,10},{13,12},{... | collective-permute-start | bytes 2359304 | tf_op jit(solution)/shard_map/ppermute | solution.py:23
  888.9 214.6 %copy-start.57 = (f32[1536]{0:T(1024)S(1)}, f32[1536]{0:T(1024)}, u32[]{:S(2)}) copy-start(f32[1536]{0:T(1024)} %get-tuple-element.193) | copy-start | bytes 18436
  888.9 214.6 %copy-start.36 = (bf16[256,32]{1,0:T(8,128)(2,1)S(1)}, bf16[256,32]{1,0:T(8,128)(2,1)}, u32[]{:S(2)}) copy-start(bf16[256,32]{1,0:T(8,128)(2,1)} %copy-done.35) | copy-start | bytes 49156
  888.9 217.4 %copy-start.55 = (f32[48,256]{1,0:T(8,128)S(1)}, f32[48,256]{1,0:T(8,128)}, u32[]{:S(2)}) copy-start(f32[48,256]{1,0:T(8,128)} %get-tuple-element.109) | copy-start | bytes 147460
  888.9 217.5 %copy-start.21 = (bf16[256,1024]{1,0:T(8,128)(2,1)S(1)}, bf16[256,1024]{1,0:T(8,128)(2,1)}, u32[]{:S(2)}) copy-start(bf16[256,1024]{1,0:T(8,128)(2,1)} %copy-done.20) | copy-start | bytes 1572868
  1139.6 21.8 %copy-start.47 = (f32[256,8]{1,0:T(8,128)S(1)}, f32[256,8]{1,0:T(8,128)}, u32[]{:S(2)}) copy-start(f32[256,8]{1,0:T(8,128)} %get-tuple-element.108) | copy-start | bytes 24580
  1139.6 21.9 %copy-start.6 = (bf16[1,256,1536]{2,1,0:T(8,128)(2,1)S(1)}, bf16[1,256,1536]{2,1,0:T(8,128)(2,1)}, u32[]{:S(2)}) copy-start(bf16[1,256,1536]{2,1,0:T(8,128)(2,1)} %param.21) | copy-start | bytes 2359300
  1139.7 21.9 %copy-start.50 = (f32[1536]{0:T(1024)S(1)}, f32[1536]{0:T(1024)}, u32[]{:S(2)}) copy-start(f32[1536]{0:T(1024)} %copy-done.49) | copy-start | bytes 18436
  1139.7 21.9 %copy-start.59 = (bf16[8,1536]{1,0:T(8,128)(2,1)S(1)}, bf16[8,1536]{1,0:T(8,128)(2,1)}, u32[]{:S(2)}) copy-start(bf16[8,1536]{1,0:T(8,128)(2,1)} %copy-done.58) | copy-start | bytes 73732
  1139.7 21.9 %copy-start.72 = (bf16[384]{0:T(512)(128)(2,1)S(1)}, bf16[384]{0:T(512)(128)(2,1)}, u32[]{:S(2)}) copy-start(bf16[384]{0:T(512)(128)(2,1)} %copy-done.71) | copy-start | bytes 2308
  1139.7 21.9 %copy-start.77 = (f32[384]{0:T(512)S(1)}, f32[384]{0:T(512)}, u32[]{:S(2)}) copy-start(f32[384]{0:T(512)} %copy-done.76) | copy-start | bytes 4612
  1139.7 21.9 %copy-start.89 = (bf16[256,384]{1,0:T(8,128)(2,1)S(1)}, bf16[256,384]{1,0:T(8,128)(2,1)}, u32[]{:S(2)}) copy-start(bf16[256,384]{1,0:T(8,128)(2,1)} %get-tuple-element.102) | copy-start | bytes 589828
  1159.7 51.5 %collective-permute-start.11 = (f32[8,1536]{1,0:T(8,128)S(1)}, f32[8,1536]{1,0:T(8,128)S(1)}, u32[]{:S(2)}, u32[]{:S(2)}) collective-permute-start(f32[8,1536]{1,0:T(8,128)S(1)} %slice.178), channel_id=1, source_target_pairs={{1,0},{2,1},{3,2},{5,4},{6,5},{7,6},{9,8},{10,9},{11,10},{13,12},{... | collective-permute-start | bytes 147464 | tf_op jit(solution)/shard_map/ppermute | solution.py:23
  1185.7 26.4 %copy-start.10 = (f32[248,1536]{1,0:T(8,128)}, f32[248,1536]{1,0:T(8,128)S(1)}, u32[]{:S(2)}) copy-start(f32[248,1536]{1,0:T(8,128)S(1)} %slice.176) | copy-start | bytes 4571140
  1185.7 26.3 %copy-start.64 = (f32[256]{0:T(256)S(1)}, f32[256]{0:T(256)}, u32[]{:S(2)}) copy-start(f32[256]{0:T(256)} %fusion.61) | copy-start | bytes 3076
  1213.8 115.4 %copy-start.66 = (f32[256]{0:T(256)S(1)}, f32[256]{0:T(256)}, u32[]{:S(2)}) copy-start(f32[256]{0:T(256)} %copy-done.65) | copy-start | bytes 3076
  1213.8 116.8 %copy-start.9 = (f32[256,1536]{1,0:T(8,128)S(1)}, f32[256,1536]{1,0:T(8,128)}, u32[]{:S(2)}) copy-start(f32[256,1536]{1,0:T(8,128)} %copy-done.7) | copy-start | bytes 4718596
  (66 other events, 427.1 us)
Sparse Core Ops, SparseCore 0:
  9.7 165.3 all-gather.7
  176.7 184.6 all-gather.5
  363.0 147.8 all-gather.3
  663.3 123.1 reduce-scatter.9
  788.6 163.3 reduce-scatter.5
  954.2 153.6 reduce-scatter.7

commit v2 on v1

--- a/solution.py
+++ b/solution.py
@@ -530,6 +530,7 @@
 GROUP = 8
 WIDE = GROUP * HEAD
 VMEM_MOST = 56 * 1024 * 1024
+BRIEF = pl.CostEstimate(flops=1024, bytes_accessed=1024, transcendentals=0)
 
 
 def spread_rows(rows):
@@ -563,7 +564,7 @@
     return value.astype(jnp.bfloat16)
 
 
-def call_steps(kernel, steps, ins, in_specs, outs, out_specs, scratch=(), flops=1 << 30):
+def call_steps(kernel, steps, ins, in_specs, outs, out_specs, scratch=(), name_id=None):
     return pl.pallas_call(
         kernel,
         grid=(steps,),
@@ -571,9 +572,12 @@
         out_specs=out_specs,
         out_shape=outs,
         scratch_shapes=list(scratch),
-        cost_estimate=pl.CostEstimate(flops=flops, bytes_accessed=8 << 20, transcendentals=0),
+        cost_estimate=BRIEF,
         compiler_params=pltpu.CompilerParams(
-            vmem_limit_bytes=VMEM_MOST, dimension_semantics=("arbitrary",)
+            vmem_limit_bytes=VMEM_MOST,
+            dimension_semantics=("arbitrary",),
+            collective_id=name_id,
+            has_side_effects=name_id is not None,
         ),
     )(*ins)
 
@@ -652,51 +656,6 @@
     state_ref[...] = half(mul_nt(scaled, b_t))
 
 
-def inner_kernel(
-    pre_ref, bc_ref, dt_ref, cum_ref, cum_col_ref, skip_ref, flags_ref, seg_col_ref, y_ref, mask_s, inner_s
-):
-    @pl.when(pl.program_id(0) == 0)
-    def _():
-        mask_s[...] = link_mask(flags_ref[2:3, :], seg_col_ref[:, 0:1])
-        bc = half(jax.nn.silu(bc_ref[...]))
-        inner_s[...] = mul_tn(bc[:STATE], bc[STATE:])
-
-    x = jax.nn.silu(pre_ref[...])
-    scaled = half(x * spread_rows(dt_ref[...]))
-    cum, cum_col = cum_ref[...], cum_col_ref[0]
-    for head in range(GROUP):
-        rows = slice(head * HEAD, (head + 1) * HEAD)
-        spread = cum[head : head + 1, :] - cum_col[:, head : head + 1] + mask_s[...]
-        weights = half(jnp.exp(spread) * inner_s[...])
-        y_ref[rows, :] = mul_nn(scaled[rows], weights) + x[rows] * skip_ref[head : head + 1, :]
-
-
-def join_kernel(
-    y_ref, state_ref, bc_ref, cum_ref, z_ref, gain_ref, flags_ref, y_out_ref, gated_ref, sums_ref, u_s, sum_s
-):
-    step, groups = pl.program_id(0), u_s.shape[0]
-
-    @pl.when(step == 0)
-    def _():
-        sum_s[...] = jnp.zeros_like(sum_s)
-
-    @pl.when(step < groups)
-    def _():
-        c_t = half(jax.nn.silu(bc_ref[STATE:, :]))
-        reach = jnp.exp(cum_ref[...]) * flags_ref[0:1, :]
-        y = y_ref[...] + mul_nn(state_ref[...], c_t) * spread_rows(reach)
-        y_out_ref[...] = y
-        u = y * jax.nn.silu(z_ref[...])
-        u_s[step] = u
-        sum_s[...] += jnp.sum(u * u, axis=0, keepdims=True)
-
-    @pl.when(step >= groups)
-    def _():
-        scale = lax.rsqrt(sum_s[0:1, :] * (1.0 / DI) + 1e-05)
-        gated_ref[...] = half(u_s[step - groups] * scale * gain_ref[:, 0:1])
-        sums_ref[...] = jnp.broadcast_to(scale, sums_ref.shape)
-
-
 def gate_back_kernel(
     y_ref, z_ref, grad_ref, gain_ref, rows_ref, bc_ref, cum_ref, flags_ref, grad_y_ref, grad_z_ref, grad_state_ref
 ):
@@ -713,10 +672,11 @@
 
 
 def inner_back_kernel(
-    pre_ref, grad_y_ref, bc_ref, dt_ref, cum_ref, cum_col_ref, flags_ref, seg_col_ref,
-    grad_x_ref, grad_cum_ref, grad_skip_ref, grad_bc_ref, mask_s, inner_s, total_s,
+    local_ref, passed_ref, pre_ref, grad_y_ref, bc_ref, dt_ref, cum_ref, cum_col_ref, flags_ref, seg_col_ref,
+    grad_x_ref, grad_state_ref, grad_cum_ref, grad_skip_ref, grad_bc_ref, mask_s, inner_s, total_s, *chain,
 ):
     step = pl.program_id(0)
+    first, last, device = chain_places(step, False)
 
     @pl.when(step == 0)
     def _():
@@ -725,6 +685,7 @@
         inner_s[...] = mul_tn(bc[:STATE], bc[STATE:])
         total_s[...] = jnp.zeros_like(total_s)
 
+    grad_state_ref[...] = chain_step(step, first, last, device, local_ref, passed_ref, *chain)
     x = jax.nn.silu(pre_ref[...])
     grad_y = grad_y_ref[...]
     grad_skip_ref[...] = head_sums(x * grad_y)
@@ -749,6 +710,7 @@
         total = half(total_s[...])
         grad_bc_ref[:STATE, :] = mul_nt(bc[STATE:], total)
         grad_bc_ref[STATE:, :] = mul_nn(bc[:STATE], total)
+        chain_end(chain[0].shape[0], last, device, *chain)
 
 
 def join_back_kernel(
@@ -838,33 +800,6 @@
     return bc_pre, pre, state
 
 
-def mixer_forward_inner(pre, bc_pre, dt, cum, cum_col, skip, flags, seg_col):
-    tokens, groups = dt.shape[1], HEADS // GROUP
-    rows = block((GROUP, tokens), lambda i: (i, 0))
-    wide = block((WIDE, tokens), lambda i: (i, 0))
-    square = pltpu.VMEM((tokens, tokens), jnp.float32)
-    return call_steps(
-        inner_kernel, groups, (pre, bc_pre, dt, cum, cum_col, skip, flags, seg_col),
-        [wide, whole(bc_pre), rows, rows, block((1, tokens, GROUP), lambda i: (i, 0, 0)), rows,
-         whole(flags), whole(seg_col)],
-        f32_out(DI, tokens), wide, (square, square), flops=30 << 30,
-    )
-
-
-def mixer_forward_join(y, state_in, bc_pre, cum, proj, gain_col, flags):
-    tokens, groups = y.shape[1], HEADS // GROUP
-    first = lambda i: (jnp.minimum(i, groups - 1), 0)
-    second = lambda i: (jnp.maximum(i - groups, 0), 0)
-    return call_steps(
-        join_kernel, 2 * groups, (y, state_in, bc_pre, cum, proj, gain_col, flags),
-        [block((WIDE, tokens), first), block((WIDE, STATE), first), whole(bc_pre),
-         block((GROUP, tokens), first), block((WIDE, tokens), first), block((WIDE, 8), second), whole(flags)],
-        [f32_out(DI, tokens), bf16_out(DI, tokens), f32_out(8, tokens)],
-        [block((WIDE, tokens), first), block((WIDE, tokens), second), block((8, tokens), lambda i: (0, 0))],
-        (pltpu.VMEM((groups, WIDE, tokens), jnp.float32), pltpu.VMEM((8, tokens), jnp.float32)),
-    )
-
-
 def mixer_back_gate(y, proj, grad_gated, gain_col, gate_rows, bc_pre, cum, flags):
     tokens, groups = y.shape[1], HEADS // GROUP
     wide = block((WIDE, tokens), lambda i: (i, 0))
@@ -877,18 +812,20 @@
     )
 
 
-def mixer_back_inner(pre, grad_y, bc_pre, dt, cum, cum_col, flags, seg_col):
+def mixer_back_inner(local, passed, pre, grad_y, bc_pre, dt, cum, cum_col, flags, seg_col, name_id):
     tokens, groups = dt.shape[1], HEADS // GROUP
     rows = block((GROUP, tokens), lambda i: (i, 0))
     wide = block((WIDE, tokens), lambda i: (i, 0))
+    states = block((WIDE, STATE), lambda i: (i, 0))
     square = pltpu.VMEM((tokens, tokens), jnp.float32)
     return call_steps(
-        inner_back_kernel, groups, (pre, grad_y, bc_pre, dt, cum, cum_col, flags, seg_col),
-        [wide, wide, whole(bc_pre), rows, rows, block((1, tokens, GROUP), lambda i: (i, 0, 0)),
+        inner_back_kernel, groups, (local, passed, pre, grad_y, bc_pre, dt, cum, cum_col, flags, seg_col),
+        [states, block((WIDE, 8), lambda i: (i, 0)), wide, wide, whole(bc_pre), rows, rows, block((1, tokens, GROUP), lambda i: (i, 0, 0)),
          whole(flags), whole(seg_col)],
-        [f32_out(DI, tokens), f32_out(HEADS, tokens), f32_out(HEADS, tokens), f32_out(2 * STATE, tokens)],
-        [wide, rows, rows, block((2 * STATE, tokens), lambda i: (0, 0))],
-        (square, square, square), flops=50 << 30,
+        [f32_out(DI, tokens), bf16_out(DI, STATE), f32_out(HEADS, tokens), f32_out(HEADS, tokens),
+         f32_out(2 * STATE, tokens)],
+        [wide, states, rows, rows, block((2 * STATE, tokens), lambda i: (0, 0))],
+        (square, square, square) + chain_room(groups), name_id=name_id,
     )
 
 
@@ -934,7 +871,13 @@
     return found
 
 
-def places(lined):
+def flipped(z, bits):
+    if bits & 1:
+        z = z + 1 - 2 * lax.rem(z, 2)
+    return lax.rem(z + (bits & 2), 4)
+
+
+def places(line):
     dp, z = lax.axis_index("dp"), lax.axis_index("ctx")
     y, x, core = lax.div(dp, 4), lax.rem(lax.div(dp, 2), 2), lax.rem(dp, 2)
     others = {
@@ -942,9 +885,28 @@
         "y": (dp + 4 - 8 * y, z),
         "core": (dp + 1 - 2 * core, z),
     }
-    for away in (1, 2, 3) if lined else ():
+    for away in line:
         others[away] = (dp, lax.rem(z + away, 4))
+    others["beside"] = (dp, flipped(z, 1))
     return y, x, core, z, others
+
+
+def moved(moves, refs_in, refs_out, z, others, sems):
+    copies = []
+    for at, (source, target, take, put, bits) in enumerate(moves):
+        source, target = refs_in[source], refs_out[target]
+        source, target = source.at[take(z)], target.at[put(z)]
+        copies.append(
+            pltpu.make_async_remote_copy(
+                src_ref=source,
+                dst_ref=target,
+                send_sem=sems[0].at[at],
+                recv_sem=sems[1].at[at],
+                device_id=others["beside" if bits == 1 else 2],
+                device_id_type=pl.DeviceIdType.MESH,
+            )
+        )
+    return copies
 
 
 def greet(others):
@@ -967,22 +929,35 @@
     )
 
 
-def gather_kernel(pieces, ahead, count, lined, *refs):
-    ins, outs, (sent, came, kept) = refs[:count], refs[count : 2 * count], refs[2 * count :]
-    y, x, core, z, others = places(lined)
+def gather_kernel(pieces, ahead, count, line, moves, sizes, *refs):
+    ins, more_in = refs[:count], refs[count : count + sizes[0]]
+    refs = refs[count + sizes[0] :]
+    outs, more_out = refs[:count], refs[count : count + sizes[1]]
+    sent, came, kept, *more_sems = refs[count + sizes[1] :]
+    y, x, core, z, others = places(line)
+    deep = len(line) + 1
+    slot = z if deep == 4 else lax.div(z, 2)
     greet(others)
     sems = (sent, came)
-    started = []
+
+    def extra():
+        return moved(moves, more_in if sizes[2] else more_out, more_out, z, others, more_sems) if moves else []
+
+    def extra_turn(turn, turns):
+        share = -(-len(moves) // turns)
+        if turn < turns:
+            for copy in extra()[share * turn : share * (turn + 1)]:
+                copy.start()
 
     def legs(number):
         array, row, rows, column, columns = pieces[number]
         area = (pl.ds(row, rows), pl.ds(column, columns))
         out = outs[array]
         first, second = ("x", "y") if number % 2 == 0 else ("y", "x")
-        rest = ((slice(None),) if lined else ()) + area
+        rest = ((slice(None),) if line else ()) + area
         own = ins[array].at[area]
-        mine = out.at[(y, x, core) + ((z,) if lined else ()) + area]
-        line = out.at[(y, x, core) + rest]
+        mine = out.at[(y, x, core) + ((slot,) if line else ()) + area]
+        lane = out.at[(y, x, core) + rest]
         if first == "x":
             plane = out.at[(y, slice(None), core) + rest]
         else:
@@ -992,9 +967,9 @@
             "keep": lambda: pltpu.make_async_copy(own, mine, kept.at[number]),
             "line": lambda: [
                 send(own, mine, sems, number, away - 1, others[away])
-                for away in ((1, 2, 3) if lined else ())
+                for away in line
             ],
-            "first": lambda: send(line if lined else own, line, sems, number, 3, others[first]),
+            "first": lambda: send(lane if line else own, lane, sems, number, 3, others[first]),
             "second": lambda: send(plane, plane, sems, number, 4, others[second]),
             "core": lambda: send(every, every, sems, number, 5, others["core"]),
         }
@@ -1028,6 +1003,7 @@
         begin(number)
     pairs = -(-len(pieces) // 2)
     for turn in range(pairs + 3):
+        extra_turn(turn, pairs)
         for stage in range(4):
             for number in (2 * (turn - stage), 2 * (turn - stage) + 1):
                 advance(number, stage)
@@ -1037,38 +1013,64 @@
         leg = legs(number)
         for copy in leg["line"]() + [leg["first"](), leg["second"](), leg["core"]()]:
             copy.wait_send()
-
-
-def pallas_gather(parts, steps, name_id, lined=True, ahead=2):
+    for copy in extra():
+        copy.wait()
+
+
+def move_room(moves):
+    if not moves:
+        return []
+    return [pltpu.SemaphoreType.DMA((len(moves),))] * 2
+
+
+def pallas_gather(parts, steps, name_id, line=(1, 2, 3), ahead=2, more=(), more_shapes=(), moves=()):
     pieces = []
     for index, (part, (row_step, column_step)) in enumerate(zip(parts, steps)):
         pieces += cut(index, part.shape[0], part.shape[1], row_step, column_step)
     count = len(parts)
-    lead = (2, 2, 2, 4) if lined else (2, 2, 2)
+    made = more_shapes or [part.shape for part in more]
+    lead = (2, 2, 2) + ((len(line) + 1,) if line else ())
     anywhere = pl.BlockSpec(memory_space=pl.ANY)
     outs = pl.pallas_call(
-        partial(gather_kernel, pieces, ahead, count, lined),
-        in_specs=[anywhere] * count,
-        out_specs=[anywhere] * count,
-        out_shape=[jax.ShapeDtypeStruct(lead + part.shape, part.dtype) for part in parts],
+        partial(gather_kernel, pieces, ahead, count, line, moves, (len(more), len(made), bool(more_shapes))),
+        in_specs=[anywhere] * (count + len(more)),
+        out_specs=[anywhere] * (count + len(made)),
+        out_shape=[jax.ShapeDtypeStruct(lead + part.shape, part.dtype) for part in parts]
+        + [bf16_out(*shape) for shape in made],
         scratch_shapes=[
             pltpu.SemaphoreType.DMA((len(pieces), 6)),
             pltpu.SemaphoreType.DMA((len(pieces), 6)),
             pltpu.SemaphoreType.DMA((len(pieces),)),
-        ],
+        ]
+        + move_room(moves),
+        input_output_aliases={} if more_shapes else {count + at: count + at for at in range(len(more))},
+        cost_estimate=BRIEF,
         compiler_params=pltpu.CompilerParams(collective_id=name_id, has_side_effects=True),
-    )(*parts)
-    return [out.reshape((-1,) + part.shape) for out, part in zip(outs, parts)]
-
-
-def reduce_kernel(pieces, ahead, count, lined, *refs):
-    ins, outs = refs[:count], refs[count : 2 * count]
-    sent, came, kept, put = refs[2 * count : 2 * count + 4]
-    room = refs[2 * count + 4 :]
-    y, x, core, z, others = places(lined)
+    )(*parts, *more)
+    return [out.reshape((-1,) + part.shape) for out, part in zip(outs, parts)] + list(outs[count:])
+
+
+def reduce_kernel(pieces, ahead, count, lines, moves, sizes, *refs):
+    ins, more_in = refs[:count], refs[count : count + sizes[0]]
+    refs = refs[count + sizes[0] :]
+    outs, more_out = refs[:count], refs[count : count + sizes[1]]
+    sent, came, kept, put = refs[count + sizes[1] : count + sizes[1] + 4]
+    room = refs[count + sizes[1] + 4 :]
+    if moves:
+        more_sems, room = room[:2], room[2:]
+    y, x, core, z, others = places(max(lines, key=len))
     greet(others)
     sems = (sent, came)
     amount = len(pieces)
+
+    def extra():
+        return moved(moves, more_in, more_out, z, others, more_sems) if moves else []
+
+    def extra_turn(turn, turns):
+        share = -(-len(moves) // turns)
+        if turn < turns:
+            for copy in extra()[share * turn : share * (turn + 1)]:
+                copy.start()
 
     def held(number):
         return room[6 * number : 6 * number + 6]
@@ -1078,7 +1080,10 @@
         area = (pl.ds(row, rows), pl.ds(column, columns))
         total, from_core, from_first, from_second, from_line, result = held(number)
         every = (slice(None), slice(None))
-        rest = ((slice(None),) if lined else ()) + area
+        line = lines[array]
+        deep = len(line) + 1
+        slot = z if deep == 4 else lax.div(z, 2)
+        rest = ((slice(None),) if line else ()) + area
         side = number % 2 == 0
         return {
             "load": lambda: pltpu.make_async_copy(
@@ -1098,10 +1103,10 @@
             ),
             "line": lambda: [
                 send(
-                    total.at[y, x, lax.rem(z + away, 4)], from_line.at[away - 1],
-                    sems, number, 2 + away, others[away],
+                    total.at[y, x, lax.rem(z + away, 4) if deep == 4 else 1 - slot],
+                    from_line.at[away - line[0]], sems, number, 2 + away, others[away],
                 )
-                for away in ((1, 2, 3) if lined else ())
+                for away in line
             ],
             "store": lambda: pltpu.make_async_copy(result, outs[array].at[area], put.at[number]),
         }
@@ -1117,10 +1122,12 @@
             return
         leg = legs(number)
         total, from_core, from_first, from_second, from_line, result = held(number)
-        deep = 4 if lined else 1
+        line = lines[pieces[number][0]]
+        deep = len(line) + 1
+        slot = z if deep == 4 else lax.div(z, 2)
 
         def place(at, *lead):
-            return lead + ((lax.rem(at, deep),) if lined else ())
+            return lead + ((lax.rem(at, deep),) if line else ())
 
         if stage == 0:
             leg["load"]().wait()
@@ -1144,9 +1151,9 @@
             leg["second"]().start()
         elif stage == 2:
             leg["second"]().wait_recv()
-            if lined:
-
-                @pl.loop(0, 4)
+            if line:
+
+                @pl.loop(0, deep)
                 def _(at):
                     total[y, x, at] = total[y, x, at] + from_second[at]
 
@@ -1155,11 +1162,11 @@
             else:
                 result[...] = total[y, x].astype(jnp.float32) + from_second[...].astype(jnp.float32)
                 leg["store"]().start()
-        elif lined:
+        elif line:
             for copy in leg["line"]():
                 copy.wait_recv()
-            summed = total[y, x, z].astype(jnp.float32)
-            for away in range(3):
+            summed = total[y, x, slot].astype(jnp.float32)
+            for away in range(len(line)):
                 summed = summed + from_line[away].astype(jnp.float32)
             result[...] = summed
             leg["store"]().start()
@@ -1168,6 +1175,7 @@
         begin(number)
     pairs = -(-amount // 2)
     for turn in range(pairs + 3):
+        extra_turn(turn, pairs)
         for stage in range(4):
             for number in (2 * (turn - stage), 2 * (turn - stage) + 1):
                 advance(number, stage)
@@ -1178,9 +1186,12 @@
         for copy in [leg["core"](), leg["first"](), leg["second"]()] + leg["line"]():
             copy.wait_send()
         leg["store"]().wait()
-
-
-def pallas_reduce(parts, steps, name_id, lined=True, ahead=2):
+    for copy in extra():
+        copy.wait()
+
+
+def pallas_reduce(parts, steps, name_id, lines=None, ahead=2, more=(), more_shapes=(), moves=()):
+    lines = lines or [(1, 2, 3)] * len(parts)
     shapes = [part.shape[1:] for part in parts]
     pieces = []
     for index, (shape, (row_step, column_step)) in enumerate(zip(shapes, steps)):
@@ -1189,48 +1200,197 @@
     anywhere = pl.BlockSpec(memory_space=pl.ANY)
     room = []
     for array, _, rows, _, columns in pieces:
-        kind = parts[array].dtype
-        deep = (4,) if lined else ()
-        for lead in ((2, 2) + deep, (2, 2) + deep, (2,) + deep, deep, (3,) if lined else (1,)):
+        kind, line = parts[array].dtype, lines[array]
+        deep = (len(line) + 1,) if line else ()
+        for lead in ((2, 2) + deep, (2, 2) + deep, (2,) + deep, deep, (max(len(line), 1),)):
             room.append(pltpu.VMEM(lead + (rows, columns), kind))
         room.append(pltpu.VMEM((rows, columns), jnp.float32))
     return pl.pallas_call(
-        partial(reduce_kernel, pieces, ahead, count, lined),
-        in_specs=[anywhere] * count,
-        out_specs=[anywhere] * count,
-        out_shape=[jax.ShapeDtypeStruct(shape, jnp.float32) for shape in shapes],
+        partial(reduce_kernel, pieces, ahead, count, lines, moves, (len(more), len(more_shapes))),
+        in_specs=[anywhere] * (count + len(more)),
+        out_specs=[anywhere] * (count + len(more_shapes)),
+        out_shape=[jax.ShapeDtypeStruct(shape, jnp.float32) for shape in shapes]
+        + [bf16_out(*shape) for shape in more_shapes],
         scratch_shapes=[
             pltpu.SemaphoreType.DMA((amount, 6)),
             pltpu.SemaphoreType.DMA((amount, 6)),
             pltpu.SemaphoreType.DMA((amount,)),
             pltpu.SemaphoreType.DMA((amount,)),
-        ] + room,
+        ]
+        + move_room(moves)
+        + room,
+        cost_estimate=BRIEF,
         compiler_params=pltpu.CompilerParams(
             collective_id=name_id, has_side_effects=True, vmem_limit_bytes=VMEM_MOST
         ),
-        )(*[part.reshape((2, 2, 2) + ((4,) if lined else ()) + shape) for part, shape in zip(parts, shapes)])
-
-
-def chained_states(local, through, step):
-    count = lax.axis_size("ctx")
-    total, factor = None, None
-    rows = jnp.pad(through[:, None], ((0, 0), (0, 127)))
-    for away in range(1, count):
-        arrived = from_behind(local, "ctx", step * away).astype(jnp.float32)
-        if factor is not None:
-            arrived = (arrived.reshape(HEADS, HEAD, STATE) * factor[:, None, None]).reshape(DI, STATE)
-        total = arrived if total is None else total + arrived
-        if away < count - 1:
-            passed = from_behind(rows, "ctx", step * away)[:, 0]
-            factor = passed if factor is None else factor * passed
-    return half(total)
+        )(*[part.reshape((2, 2, 2) + ((len(line) + 1,) if line else ()) + shape) for part, shape, line in zip(parts, shapes, lines)], *more)
+
+
+def proj_back_kernel(normed_ref, weight_ref, grad_ref, grad_weight_ref, grad_normed_ref):
+    step, width = pl.program_id(0), weight_ref.shape[1]
+    last = pl.num_programs(0) - 1
+    grad = grad_ref[...]
+    grad_weight_ref[...] = half(mul_nt(normed_ref[...], grad))
+
+    @pl.when(step == 0)
+    def _():
+        grad_normed_ref[...] = jnp.zeros_like(grad_normed_ref)
+
+    @pl.when(step < last)
+    def _():
+        grad_normed_ref[...] += mul_nn(weight_ref[...], grad)
+
+    @pl.when(step == last)
+    def _():
+        left = PROJ - last * width
+        lane = lax.broadcasted_iota(jnp.int32, weight_ref.shape, 1)
+        row = lax.broadcasted_iota(jnp.int32, grad.shape, 0)
+        weight = jnp.where(lane < left, weight_ref[...], jnp.zeros_like(weight_ref))
+        grad_normed_ref[...] += mul_nn(weight, jnp.where(row < left, grad, jnp.zeros_like(grad)))
+
+
+def proj_back(normed_t, weight, grad_t):
+    features, tokens = normed_t.shape
+    width = 512
+    return call_steps(
+        proj_back_kernel, -(-PROJ // width), (normed_t, weight, grad_t),
+        [whole(normed_t), block((features, width), lambda i: (0, i)), block((width, tokens), lambda i: (i, 0))],
+        [bf16_out(features, PROJ), f32_out(features, tokens)],
+        [block((features, width), lambda i: (0, i)), block((features, tokens), lambda i: (0, 0))],
+
+    )
+
+
+def hop(group, leaving, arrived, sent, came, device):
+    return pltpu.make_async_remote_copy(
+        src_ref=leaving.at[group],
+        dst_ref=arrived.at[group],
+        send_sem=sent.at[group],
+        recv_sem=came.at[group],
+        device_id=device,
+        device_id_type=pl.DeviceIdType.MESH,
+    )
+
+
+def chain_places(step, forward):
+    dp, z = lax.axis_index("dp"), lax.axis_index("ctx")
+    others = {"left": (dp, lax.rem(z + 3, 4)), "right": (dp, lax.rem(z + 1, 4))}
+
+    @pl.when(step == 0)
+    def _():
+        greet(others)
+
+    if forward:
+        return z == 0, z == 3, others["right"]
+    return z == 3, z == 0, others["left"]
+
+
+def chain_step(step, first, last, device, local_ref, passed_ref, leaving, arrived, sent, came):
+    @pl.when(first)
+    def _():
+        arrived[step] = jnp.zeros(arrived.shape[1:], arrived.dtype)
+
+    @pl.when(jnp.logical_not(first))
+    def _():
+        hop(step, leaving, arrived, sent, came, device).wait_recv()
+
+    here = arrived[step]
+    leaving[step] = half(here.astype(jnp.float32) * passed_ref[:, 0:1] + local_ref[...].astype(jnp.float32))
+
+    @pl.when(jnp.logical_not(last))
+    def _():
+        hop(step, leaving, arrived, sent, came, device).start()
+
+    return here
+
+
+def chain_end(groups, last, device, leaving, arrived, sent, came):
+    @pl.when(jnp.logical_not(last))
+    def _():
+        for group in range(groups):
+            hop(group, leaving, arrived, sent, came, device).wait_send()
+
+
+def chain_room(groups):
+    slots = pltpu.VMEM((groups, WIDE, STATE), jnp.bfloat16)
+    sems = pltpu.SemaphoreType.DMA((groups,))
+    return (slots, slots, sems, sems)
+
+
+def forward_kernel(
+    local_ref, passed_ref, pre_ref, bc_ref, dt_ref, cum_ref, cum_col_ref, skip_ref, flags_ref, seg_col_ref,
+    z_ref, gain_ref, y_ref, state_ref, gated_ref, scale_ref, mask_s, inner_s, u_s, sum_s, *chain,
+):
+    step, groups = pl.program_id(0), u_s.shape[0]
+    first, last, device = chain_places(step, True)
+
+    @pl.when(step == 0)
+    def _():
+        mask_s[...] = link_mask(flags_ref[2:3, :], seg_col_ref[:, 0:1])
+        bc = half(jax.nn.silu(bc_ref[...]))
+        inner_s[...] = mul_tn(bc[:STATE], bc[STATE:])
+        sum_s[...] = jnp.zeros_like(sum_s)
+
+    @pl.when(step < groups)
+    def _():
+        here = chain_step(step, first, last, device, local_ref, passed_ref, *chain)
+        state_ref[...] = here
+        cum, cum_col = cum_ref[...], cum_col_ref[0]
+        c_t = half(jax.nn.silu(bc_ref[STATE:, :]))
+        x = jax.nn.silu(pre_ref[...])
+        scaled = half(x * spread_rows(dt_ref[...]))
+        reach = jnp.exp(cum) * flags_ref[0:1, :]
+        y_ref[...] = mul_nn(here, c_t) * spread_rows(reach) + x * spread_rows(skip_ref[...])
+        for head in range(GROUP):
+            rows = slice(head * HEAD, (head + 1) * HEAD)
+            spread = cum[head : head + 1, :] - cum_col[:, head : head + 1] + mask_s[...]
+            y_ref[rows, :] += mul_nn(scaled[rows], half(jnp.exp(spread) * inner_s[...]))
+        u = y_ref[...] * jax.nn.silu(z_ref[...])
+        u_s[step] = u
+        sum_s[...] += jnp.sum(u * u, axis=0, keepdims=True)
+
+    @pl.when(step >= groups)
+    def _():
+        scale = lax.rsqrt(sum_s[0:1, :] * (1.0 / DI) + 1e-05)
+        gated_ref[...] = half(u_s[step - groups] * scale * gain_ref[:, 0:1])
+        scale_ref[...] = jnp.broadcast_to(scale, scale_ref.shape)
+
+    @pl.when(step == 2 * groups - 1)
+    def _():
+        chain_end(groups, last, device, *chain)
+
+
+def mixer_forward(local, passed, pre, bc_pre, dt, cum, cum_col, skip, flags, seg_col, proj, gain_col, name_id):
+    tokens, groups = dt.shape[1], HEADS // GROUP
+    first = lambda i: (jnp.minimum(i, groups - 1), 0)
+    second = lambda i: (jnp.maximum(i - groups, 0), 0)
+    rows, wide = block((GROUP, tokens), first), block((WIDE, tokens), first)
+    states = block((WIDE, STATE), first)
+    square = pltpu.VMEM((tokens, tokens), jnp.float32)
+    return call_steps(
+        forward_kernel, 2 * groups,
+        (local, passed, pre, bc_pre, dt, cum, cum_col, skip, flags, seg_col, proj, gain_col),
+        [states, block((WIDE, 8), first), wide, whole(bc_pre), rows, rows,
+         block((1, tokens, GROUP), lambda i: (jnp.minimum(i, groups - 1), 0, 0)), rows, whole(flags),
+         whole(seg_col), wide, block((WIDE, 8), second)],
+        [f32_out(DI, tokens), bf16_out(DI, STATE), bf16_out(DI, tokens), f32_out(8, tokens)],
+        [wide, states, block((WIDE, tokens), second), block((8, tokens), lambda i: (0, 0))],
+        (square, square, pltpu.VMEM((groups, WIDE, tokens), jnp.float32), pltpu.VMEM((8, tokens), jnp.float32))
+        + chain_room(groups),
+        name_id=name_id,
+    )
 
 
 BOTH = ("dp", "ctx")
 
 
-def after(values, *earlier):
-    return lax.optimization_barrier((values, earlier))[0]
+def nothing(value):
+    first = value[(0,) * value.ndim].astype(jnp.float32)
+    return jnp.minimum(jnp.abs(first), 0.0)
+
+
+def no_step(value):
+    return nothing(value).astype(jnp.int32)
 
 
 def two_parts(value):
@@ -1247,6 +1407,181 @@
     earlier = jnp.tril(jnp.ones((rows, rows), jnp.bfloat16), -1)
     ranks = jnp.dot(earlier, named.astype(jnp.bfloat16), preferred_element_type=jnp.float32)
     return named, jnp.where(named, ranks, -1.0)
+
+
+def swap(value, bits):
+    count = lax.axis_size("ctx")
+    return lax.ppermute(value, "ctx", [(source, source ^ bits) for source in range(count)])
+
+
+def held_experts(shard, other):
+    held = EXP_DEV // 2
+    half_at = lax.div(lax.axis_index("ctx"), 2)
+    return lax.dynamic_slice_in_dim(shard, held * (1 - half_at if other else half_at), held, 0)
+
+
+STRIP = 64
+
+
+def quarter(axis, width, bits, start):
+    def at(z):
+        first = flipped(z, bits) * width
+        if axis == 1:
+            return (slice(None), pl.ds(pl.multiple_of(first + start, STRIP), STRIP))
+        return (slice(None), pl.ds(start, STRIP), pl.ds(pl.multiple_of(first, 128), width))
+
+    return at
+
+
+def strip(start, *lead):
+    return lambda z: lead + (slice(None), pl.ds(start, STRIP))
+
+
+def strips(rows):
+    return range(0, rows, STRIP)
+
+
+def with_quarter(whole, own, axis):
+    place = lax.axis_index("ctx") * own.shape[axis]
+    return lax.dynamic_update_slice_in_dim(whole, own, place, axis)
+
+
+def own_quarter(whole, axis, bits):
+    width = whole.shape[axis] // 4
+    return lax.dynamic_slice_in_dim(whole, flipped(lax.axis_index("ctx"), bits) * width, width, axis)
+
+
+def expert_owners(near, far):
+    far = far.astype(jnp.float32)
+    low = lax.div(lax.axis_index("ctx"), 2) == 0
+    return jnp.concatenate([jnp.where(low, near, far), jnp.where(low, far, near)], axis=0)
+
+
+TILE = 4
+
+
+def experts_kernel(
+    rank_ref, gate_ref, rows_ref, grads_ref, first_ref, down_ref,
+    routed_ref, back_ref, dgate_ref, grad_first_ref, grad_down_ref,
+    x_s, g_s, sum_first_s, sum_down_s, ready_s, sem,
+):
+    tile, expert = pl.program_id(0), pl.program_id(1)
+    last = pl.num_programs(0) - 1
+    hidden = down_ref.shape[1]
+    slots = x_s.shape[0] // TILE
+    tokens = rank_ref.shape[2]
+    chosen, gates = [], []
+    number = lax.broadcasted_iota(jnp.int32, (slots, tokens), 0).astype(jnp.float32)
+    for at in range(TILE):
+        rows = pl.ds(at * slots, slots)
+        own = rank_ref[at, pl.ds(expert, 1), :] == number
+        chosen.append(own)
+        gates.append(jnp.sum(jnp.where(own, gate_ref[at, pl.ds(expert, 1), :], 0.0), axis=1, keepdims=True))
+        picker = half(own.astype(jnp.float32))
+        x_s[rows, :] = half(mul_nn(picker, rows_ref[at]))
+        g_s[rows, :] = half(mul_nn(picker, grads_ref[at]))
+    gate = jnp.concatenate(gates, axis=0)
+    x, grad = x_s[...], g_s[...].astype(jnp.float32)
+    both = mul_nn(x, first_ref[0])
+    hg, hu = both[:, :hidden], both[:, hidden:]
+    squashed = jax.nn.sigmoid(hg)
+    act = half(hg * squashed * hu)
+    out = half(mul_nn(act, down_ref[0]))
+    out_f = out.astype(jnp.float32)
+    dgate = jnp.sum(grad * out_f, axis=1, keepdims=True)
+    routed = half(gate * out_f)
+    grad_out = half(gate * grad)
+    grad_act = mul_nt(grad_out, down_ref[0])
+    grad_hg = half(grad_act * hu * (squashed * (1.0 + hg * (1.0 - squashed))))
+    grad_hu = half(grad_act * hg * squashed)
+    grad_both = jnp.concatenate([grad_hg, grad_hu], axis=1)
+    back = half(mul_nt(grad_both, first_ref[0]))
+
+    @pl.when(tile == 0)
+    def _():
+        sum_first_s[expert] = jnp.zeros(sum_first_s.shape[1:], jnp.float32)
+        sum_down_s[expert] = jnp.zeros(sum_down_s.shape[1:], jnp.float32)
+
+    @pl.loop(0, x_s.shape[1] // 256)
+    def _(at):
+        some = pl.ds(pl.multiple_of(at * 256, 256), 256)
+        sum_first_s[expert, some, :] += mul_tn(x_s[:, some], grad_both)
+
+    sum_down_s[expert] += mul_tn(act, grad_out)
+    for at in range(TILE):
+        rows = slice(at * slots, (at + 1) * slots)
+        picker = half(chosen[at].astype(jnp.float32))
+        routed_part, back_part = half(mul_tn(picker, routed[rows])), half(mul_tn(picker, back[rows]))
+
+        @pl.when(expert == 0)
+        def _():
+            routed_ref[at] = routed_part
+            back_ref[at] = back_part
+
+        @pl.when(expert > 0)
+        def _():
+            routed_ref[at] = routed_ref[at] + routed_part
+            back_ref[at] = back_ref[at] + back_part
+
+        dgate_ref[at, pl.ds(expert, 1), :] = jnp.sum(
+            jnp.where(chosen[at], dgate[rows], 0.0), axis=0, keepdims=True
+        )
+
+    @pl.when(tile == last)
+    def _():
+        height = ready_s.shape[0]
+        for sums, target in ((sum_first_s, grad_first_ref), (sum_down_s, grad_down_ref)):
+            width = sums.shape[2]
+            for at in range(sums.shape[1] // height):
+                some = pl.ds(at * height, height)
+                ready_s[:, :width] = half(sums[expert, some, :])
+                copy = pltpu.make_async_copy(
+                    ready_s.at[:, pl.ds(0, width)], target.at[expert, some, :], sem
+                )
+                copy.start()
+                copy.wait()
+
+
+def routed_experts(rank, gate, rows, grads, first, down, slots):
+    blocks, held, tokens = rank.shape
+    features, hidden = first.shape[1], down.shape[1]
+    some = lambda t, e: (t, 0, 0)
+    table = pl.BlockSpec((TILE, held, tokens), some)
+    wide = pl.BlockSpec((TILE, tokens, features), some)
+    once = pl.BlockSpec((TILE, tokens, features), some, pipeline_mode=pl.Buffered(1))
+    anywhere = pl.BlockSpec(memory_space=pl.ANY)
+    return pl.pallas_call(
+        experts_kernel,
+        grid=(blocks // TILE, held),
+        in_specs=[
+            table,
+            table,
+            once,
+            once,
+            pl.BlockSpec((1, features, 2 * hidden), lambda t, e: (e, 0, 0)),
+            pl.BlockSpec((1, hidden, features), lambda t, e: (e, 0, 0)),
+        ],
+        out_specs=[wide, wide, table, anywhere, anywhere],
+        out_shape=[
+            bf16_out(blocks, tokens, features),
+            bf16_out(blocks, tokens, features),
+            f32_out(blocks, held, tokens),
+            bf16_out(held, features, 2 * hidden),
+            bf16_out(held, hidden, features),
+        ],
+        scratch_shapes=[
+            pltpu.VMEM((TILE * slots, features), jnp.bfloat16),
+            pltpu.VMEM((TILE * slots, features), jnp.bfloat16),
+            pltpu.VMEM((held, features, 2 * hidden), jnp.float32),
+            pltpu.VMEM((held, hidden, features), jnp.float32),
+            pltpu.VMEM((256, features), jnp.bfloat16),
+            pltpu.SemaphoreType.DMA,
+        ],
+        cost_estimate=BRIEF,
+        compiler_params=pltpu.CompilerParams(
+            vmem_limit_bytes=62 * 1024 * 1024, dimension_semantics=("arbitrary", "arbitrary")
+        ),
+    )(rank, gate, rows, grads, first, down)
 
 
 def on_device(
@@ -1276,9 +1611,10 @@
     row_count, d_model = layer_in.shape[1:]
     devices = lax.axis_size("dp") * lax.axis_size("ctx")
     ctx_place = lax.axis_index("ctx")
-    first_expert = lax.axis_index("dp") * EXP_DEV
-    blocks = lax.axis_size("dp")
-    expert_count = EXP_DEV * blocks
+    held = EXP_DEV // 2
+    first_expert = lax.axis_index("dp") * EXP_DEV + lax.div(ctx_place, 2) * held
+    blocks = lax.axis_size("dp") * 2
+    expert_count = EXP_DEV * lax.axis_size("dp")
     capacity = row_count * TOP * 5 // (expert_count * 4)
     slots = -(-capacity // 64) * 64
     tap_count = conv_w.shape[0]
@@ -1287,8 +1623,33 @@
     small_parts = (norm_in, conv_w, conv_b, norm_gate, norm_mid, w_router)
     small_flat = jnp.concatenate([part.reshape(-1) for part in small_parts])
     small_flat = jnp.pad(small_flat, (0, 4096 - small_flat.shape[0])).reshape(32, 128)
-    w_in_all, small_all = pallas_gather([w_in, small_flat], [(16, 1664), (32, 128)], 1)
-    small_all = small_all.reshape(devices, 4096)
+    edge_rows = layer_in[0, row_count - halo :].reshape(-1, 128)
+    gate_up = jnp.concatenate([e_gate, e_up], axis=2)
+    width, hidden = e_gate.shape[1:]
+    first_strips, down_strips = strips(width), strips(hidden)
+    w_in_all, w_out_all, shared_all, sdown_all, small_all, expert_first, expert_down = pallas_gather(
+        [
+            w_in,
+            w_out,
+            jnp.concatenate([w_sgate, w_sup], axis=1),
+            w_sdown,
+            jnp.concatenate([small_flat, edge_rows]),
+        ],
+        [(16, 1664), (16, 1536), (16, 1024), (16, 1536), (128, 128)],
+        1,
+        ahead=3,
+        more=[held_experts(gate_up, True), held_experts(e_down, True)],
+        more_shapes=[(held, d_model, 2 * hidden), (held, hidden, d_model)],
+        moves=[
+            (part, part, strip(start), quarter(axis, width, 0, start), 2)
+            for part, axis, starts in ((0, 1, first_strips), (1, 2, down_strips))
+            for start in starts
+        ],
+    )
+    expert_first = with_quarter(expert_first, held_experts(gate_up, False), 1)
+    expert_down = with_quarter(expert_down, held_experts(e_down, False), 2)
+    edge_all = small_all[:, small_flat.shape[0] :].reshape(devices, halo, d_model)
+    small_all = small_all[:, : small_flat.shape[0]].reshape(devices, 4096)
     taken, pieces = 0, []
     for part in small_parts:
         pieces.append(small_all[:, taken : taken + part.size])
@@ -1300,13 +1661,15 @@
     gain_mid = pieces[4].reshape(-1).astype(f32)
     router_weight = pieces[5].reshape(d_model, expert_count)
     weight_in = w_in_all.reshape(d_model, PROJ)
-    expert_gate = lax.all_gather(e_gate, "ctx", axis=1, tiled=True)
-    expert_up = lax.all_gather(e_up, "ctx", axis=1, tiled=True)
-    expert_down = lax.all_gather(e_down, "ctx", axis=2, tiled=True)
+    weight_out = w_out_all.reshape(DI, d_model)
+    shared_weight = shared_all.reshape(d_model, -1)
+    sdown_weight = sdown_all.reshape(-1, d_model)
     named, ranks = route_table(route_ids[0], expert_count)
 
     own_in = layer_in[0]
-    edge_in = from_behind(own_in[row_count - halo :], "ctx", 1)
+    place = lax.axis_index("dp") * lax.axis_size("ctx") + ctx_place
+    edge_in = lax.dynamic_index_in_dim(edge_all, jnp.maximum(place - 1, 0), 0, keepdims=False)
+    edge_in = jnp.where(ctx_place > 0, edge_in, jnp.zeros_like(edge_in))
     input_f = jnp.concatenate(
         [own_in, jnp.zeros((128 - halo, d_model), bf16), edge_in], axis=0
     ).astype(f32)
@@ -1326,20 +1689,10 @@
         dt_raw, dt_bias, a_log, d_skip, seg_window, tap_count
     )
     bc_pre, pre, state_out = mixer_forward_states(projected, taps, masks, dt_pos, cumul, flags)
-    state_in = chained_states(state_out, through, 1)
-    w_out_all, sgate_all, sup_all, sdown_all = pallas_gather(
-        after([w_out, w_sgate, w_sup, w_sdown], state_out),
-        [(16, 1536), (16, 1024), (16, 1024), (16, 1536)],
-        2,
-    )
-    weight_out = w_out_all.reshape(DI, d_model)
-    sgate_weight = sgate_all.reshape(d_model, -1)
-    sup_weight = sup_all.reshape(d_model, -1)
-    sdown_weight = sdown_all.reshape(-1, d_model)
-    y_inner = mixer_forward_inner(pre, bc_pre, dt_pos, cumul, cumul_col, skip_rows, flags, seg_col)
+    passed = jnp.broadcast_to(jnp.repeat(through, HEAD)[:, None], (DI, 8))
     gain_col = jnp.broadcast_to(gain_gate[:, None], (DI, 8))
-    y_heads, gated, gate_scale = mixer_forward_join(
-        after(y_inner, weight_out), state_in, bc_pre, cumul, projected, gain_col, flags
+    y_heads, state_in, gated, gate_scale = mixer_forward(
+        state_out, passed, pre, bc_pre, dt_pos, cumul, cumul_col, skip_rows, flags, seg_col, projected, gain_col, 7
     )
 
     mixed = times_rows(gated, weight_out)
@@ -1355,86 +1708,77 @@
         [gate_high, gate_low, ranks.astype(bf16), jnp.zeros((row_count, 128 - 3 * expert_count), bf16)],
         axis=1,
     )
-    token_rows, grad_rows, side_all = pallas_gather(
-        [normed_mid, out_grad[0], side], [(16, 1536), (16, 1536), (128, 128)], 3, lined=False, ahead=4
-    )
-    shared_gate = jnp.dot(normed_mid, sgate_weight, preferred_element_type=f32)
-    shared_up = jnp.dot(normed_mid, sup_weight, preferred_element_type=f32)
+    token_rows, grad_rows, side_all, expert_first, expert_down = pallas_gather(
+        [normed_mid, out_grad[0], side],
+        [(16, 1536), (16, 1536), (128, 128)],
+        3,
+        line=(2,),
+        ahead=4,
+        more=[expert_first, expert_down],
+        moves=[
+            (part, part, quarter(axis, width, 2 * far, start), quarter(axis, width, 2 * far, start), 1)
+            for far in (0, 1)
+            for part, axis, starts in ((0, 1, first_strips), (1, 2, down_strips))
+            for start in starts
+        ],
+    )
+    shared_hidden = jnp.dot(normed_mid, shared_weight, preferred_element_type=f32)
+    shared_gate, shared_up = jnp.split(shared_hidden, 2, axis=1)
     shared_act = (jax.nn.silu(shared_gate) * shared_up).astype(bf16)
     shared_out = jnp.dot(shared_act, sdown_weight, preferred_element_type=f32)
 
-    mine_of = partial(lax.dynamic_slice_in_dim, slice_size=EXP_DEV, axis=2)
+    def owned(grad):
+        return grad.astype(bf16).reshape(devices, -1, grad.shape[-1])
+
+    mine_of = partial(lax.dynamic_slice_in_dim, slice_size=held, axis=2)
     my_gate = mine_of(side_all, first_expert).astype(f32) + mine_of(
         side_all, first_expert + expert_count
     ).astype(f32)
     my_rank = mine_of(side_all, first_expert + 2 * expert_count).astype(f32)
     my_gate, my_rank = jnp.swapaxes(my_gate, 1, 2), jnp.swapaxes(my_rank, 1, 2)
-    chosen = my_rank[:, :, None, :] == jnp.arange(slots, dtype=f32)[None, None, :, None]
-    select = chosen.astype(bf16)
-    slot_gate = jnp.sum(jnp.where(chosen, my_gate[:, :, None, :], 0.0), axis=-1)
-    gate_col = jnp.swapaxes(slot_gate, 0, 1).reshape(EXP_DEV, blocks * slots, 1)
-
-    def to_slots(rows):
-        taken = jnp.einsum("best,btd->ebsd", select, rows, preferred_element_type=f32)
-        return taken.astype(bf16).reshape(EXP_DEV, blocks * slots, -1)
-
-    def to_tokens(rows):
-        rows = rows.reshape(EXP_DEV, blocks, slots, -1)
-        return jnp.einsum("best,ebsd->btd", select, rows, preferred_element_type=f32).astype(bf16)
-
-    def each(spec, left, right):
-        return jnp.einsum(spec, left, right, preferred_element_type=f32)
-
-    slot_in = to_slots(token_rows)
-    slot_grad = to_slots(grad_rows)
-    hidden_gate = each("erd,edf->erf", slot_in, expert_gate)
-    hidden_up = each("erd,edf->erf", slot_in, expert_up)
-    hidden_act = (jax.nn.silu(hidden_gate) * hidden_up).astype(bf16)
-    expert_out = each("erf,efd->erd", hidden_act, expert_down).astype(bf16)
-    slot_dgate = jnp.sum(slot_grad.astype(f32) * expert_out.astype(f32), axis=-1)
-    grad_out_slots = (gate_col * slot_grad).astype(bf16)
-    grad_act = each("erd,efd->erf", grad_out_slots, expert_down)
-    grad_e_down = each("erf,erd->efd", hidden_act, grad_out_slots)
-    grad_hgate = (grad_act * hidden_up * silu_slope(hidden_gate)).astype(bf16)
-    grad_hup = (grad_act * jax.nn.silu(hidden_gate)).astype(bf16)
-    grad_slots = (
-        each("erf,edf->erd", grad_hgate, expert_gate) + each("erf,edf->erd", grad_hup, expert_up)
-    ).astype(bf16)
-    slot_dgate = jnp.swapaxes(slot_dgate.reshape(EXP_DEV, blocks, slots), 0, 1)
-    token_dgate = jnp.sum(jnp.where(chosen, slot_dgate[..., None], 0.0), axis=2)
-    held = jnp.arange(EXP_DEV, dtype=jnp.int32)[:, None] + first_expert
+    routed_rows, grad_slot_rows, token_dgate, grad_first, grad_down = routed_experts(
+        my_rank, my_gate, token_rows, grad_rows, expert_first, expert_down, slots
+    )
+    experts = jnp.arange(held, dtype=jnp.int32)[:, None] + first_expert
     dgate_table = jnp.sum(
-        token_dgate[..., None] * (jnp.arange(expert_count) == held).astype(f32)[:, None, :], axis=1
+        token_dgate[..., None] * (jnp.arange(expert_count) == experts).astype(f32)[:, None, :], axis=1
     )
     dgate_high, dgate_low = two_parts(dgate_table)
     back_side = jnp.concatenate(
         [dgate_high, dgate_low, jnp.zeros((blocks, row_count, 128 - 2 * expert_count), bf16)], axis=-1
     )
-    back_rows, routed, back_side = pallas_reduce(
-        [to_tokens(grad_slots), to_tokens((gate_col * expert_out).astype(bf16)), back_side],
-        [(32, 1536), (32, 1536), (128, 128)],
-        4,
-        lined=False,
-    )
-    grad_e_gate = each("erd,erf->edf", slot_in, grad_hgate)
-    grad_e_up = each("erd,erf->edf", slot_in, grad_hup)
-
-    def to_owner(grad, axis):
-        sent = lax.psum_scatter(grad.astype(bf16), "ctx", scatter_dimension=axis + 1, tiled=True)
-        return sent.astype(f32)
-
-    expert_grads = (to_owner(grad_e_gate, 0), to_owner(grad_e_up, 0), to_owner(grad_e_down, 1))
-
-    layer_out = (resid_mid + shared_out + routed).astype(bf16)[None]
-    grad_top = out_grad[0].astype(f32)
     grad_shared_out = out_grad[0]
     grad_w_sdown = times_rows(shared_act, grad_shared_out)
+    back_rows, routed, back_side, sum_sdown, beside_first, beside_down = pallas_reduce(
+        [grad_slot_rows, routed_rows, back_side, owned(grad_w_sdown)],
+        [(16, 1536), (16, 1536), (128, 128), (16, 1536)],
+        4,
+        lines=[(2,), (2,), (2,), (1, 2, 3)],
+        more=[grad_first, grad_down],
+        more_shapes=[(2, held, width, 2 * hidden), (2, held, hidden, width)],
+        moves=[
+            (part, part, quarter(axis, width, 2 * far + 1, start), strip(start, far), 1)
+            for far in (1, 0)
+            for part, axis, starts in ((0, 1, first_strips), (1, 2, down_strips))
+            for start in starts
+        ],
+    )
+    far_first, far_down = (
+        half(own_quarter(whole, axis, 2).astype(f32) + beside[1].astype(f32))
+        for whole, beside, axis in ((grad_first, beside_first, 1), (grad_down, beside_down, 2))
+    )
+    near_first, near_down = (
+        own_quarter(whole, axis, 0).astype(f32) + beside[0].astype(f32)
+        for whole, beside, axis in ((grad_first, beside_first, 1), (grad_down, beside_down, 2))
+    )
+
+    grad_top = out_grad[0].astype(f32)
     grad_shared_act = times_back(grad_shared_out, sdown_weight)
     grad_sgate = (grad_shared_act * shared_up * silu_slope(shared_gate)).astype(bf16)
     grad_sup = (grad_shared_act * jax.nn.silu(shared_gate)).astype(bf16)
-    grad_w_sgate = times_rows(normed_mid, grad_sgate)
-    grad_w_sup = times_rows(normed_mid, grad_sup)
-    grad_mid_shared = times_back(grad_sgate, sgate_weight) + times_back(grad_sup, sup_weight)
+    grad_shared = jnp.concatenate([grad_sgate, grad_sup], axis=1)
+    grad_w_shared = times_rows(normed_mid, grad_shared)
+    grad_mid_shared = times_back(grad_shared, shared_weight)
     grad_gates = back_side[:, :expert_count] + back_side[:, expert_count : 2 * expert_count]
     grad_pick = gates * (grad_gates - jnp.sum(gates * grad_gates, axis=-1, keepdims=True))
     grad_logits = grad_pick.astype(bf16)
@@ -1445,9 +1789,6 @@
     grad_resid_part, grad_gain_mid = pull_mid(grad_mid)
     grad_resid = grad_top + grad_resid_part
     grad_mixed = grad_resid.astype(bf16)
-
-    def owned(grad):
-        return grad.astype(bf16).reshape(devices, -1, grad.shape[-1])
 
     grad_w_out = jnp.dot(gated, grad_mixed, preferred_element_type=f32)
     grad_gated = times_back(weight_out, grad_mixed)
@@ -1461,20 +1802,11 @@
     grad_y, grad_z, grad_state_local = mixer_back_gate(
         y_heads, projected, grad_gated, gain_col, gate_rows, bc_pre, cumul, flags
     )
-    grad_state_out = chained_states(grad_state_local, through, -1)
-    sum_out, sum_sgate, sum_sup, sum_sdown = pallas_reduce(
-        after(
-            [owned(grad_w_out), owned(grad_w_sgate), owned(grad_w_sup), owned(grad_w_sdown)],
-            grad_state_local,
-        ),
-        [(16, 1536), (16, 1024), (16, 1024), (16, 1536)],
-        5,
-    )
-    grad_scaled, grad_cum_inner, grad_skip, grad_bc_inner = mixer_back_inner(
-        pre, grad_y, bc_pre, dt_pos, cumul, cumul_col, flags, seg_col
+    grad_scaled, grad_state_out, grad_cum_inner, grad_skip, grad_bc_inner = mixer_back_inner(
+        grad_state_local, passed, pre, grad_y, bc_pre, dt_pos, cumul, cumul_col, flags, seg_col, 8
     )
     grad_x, grad_taps_x, grad_dt, grad_cum_join, grad_last, grad_bc_join = mixer_back_join(
-        after(grad_scaled, sum_out), grad_y, pre, projected, taps, masks, state_in, grad_state_out,
+        grad_scaled, grad_y, pre, projected, taps, masks, state_in, grad_state_out,
         bc_pre, dt_pos, cumul, skip_rows, flags,
     )
     grad_bc, grad_taps_bc = mixer_back_conv(
@@ -1499,12 +1831,9 @@
             jnp.pad(grad_raw.astype(bf16), ((0, 0), (0, 128))),
         ]
     )
-    grad_w_in = lax.dot_general(
-        normed, grad_proj, (((0,), (1,)), ((), ())), preferred_element_type=f32
-    )
-    grad_normed = lax.dot_general(
-        grad_proj, weight_in, (((0,), (1,)), ((), ())), preferred_element_type=f32
-    )
+    normed_t = normed.T
+    grad_w_in, grad_normed = proj_back(normed_t, weight_in, grad_proj)
+    grad_normed = grad_normed.T
     edge_grad = from_behind(grad_normed[row_count + 128 - halo :], "ctx", -1)
     grad_normed = jnp.concatenate(
         [grad_normed[: row_count - halo], grad_normed[row_count - halo : row_count] + edge_grad],
@@ -1527,9 +1856,24 @@
         axis=1,
     )
     small_grads = jnp.pad(small_grads, ((0, 0), (0, 3072 - small_grads.shape[1])))
-    sum_in, sum_small = pallas_reduce(
-        [owned(grad_w_in), small_grads.reshape(devices, 24, 128)], [(16, 1664), (24, 128)], 6
-    )
+    sum_in, sum_out, sum_shared, sum_small, far_first, far_down = pallas_reduce(
+        [owned(grad_w_in), owned(grad_w_out), owned(grad_w_shared), small_grads.reshape(devices, 24, 128)],
+        [(16, 1664), (16, 1536), (16, 1024), (24, 128)],
+        6,
+        ahead=3,
+        more=[far_first, far_down],
+        more_shapes=[far_first.shape, far_down.shape],
+        moves=[
+            (part, part, strip(start), strip(start), 2)
+            for part, starts in ((0, first_strips), (1, down_strips))
+            for start in starts
+        ],
+    )
+    layer_out = (resid_mid + shared_out + routed).astype(bf16)[None]
+    sum_sgate, sum_sup = jnp.split(sum_shared, 2, axis=1)
+    grad_e_gate = expert_owners(near_first[..., :hidden], far_first[..., :hidden])
+    grad_e_up = expert_owners(near_first[..., hidden:], far_first[..., hidden:])
+    grad_e_down = expert_owners(near_down, far_down)
     sum_small = sum_small.reshape(-1)
     taken, mine = 0, []
     for part in small_parts:
@@ -1552,9 +1896,9 @@
         sum_sgate,
         sum_sup,
         sum_sdown,
-        expert_grads[0],
-        expert_grads[1],
-        expert_grads[2],
+        grad_e_gate,
+        grad_e_up,
+        grad_e_down,
     )
 
 

time: 1370 us -> 1270 us (0.927)
  matrix products: 234 us -> 68.1 us
  Pallas kernels: 909 us -> 1040 us
  local copies, waits for them, and re-layouts: 108 us -> 81.5 us
  starting transfers between devices: 23.4 us -> 1.46 us
  waiting for transfers between devices: 17.7 us -> 0.01 us
  between operations: 17.4 us -> 3.19 us
    dot_general x17 -> x1, matrix products: 177 us -> 4.74 us  [on_device(): jnp.dot(normed_mid, shared_weight, preferred_element_type=f32)]
    pallas_call x6 -> x5, Pallas kernels: 832 us -> 908 us  [the longest x2 401 us: pallas_reduce(): pl.pallas_call(partial(reduce_kernel, pieces, ahead, count, lines, moves,...]
    pallas_call x8, Pallas kernels: 76.7 us -> 135 us  [call_steps(): pl.pallas_call(kernel, grid=(steps,), in_specs=in_specs, out_specs=out_sp...]
    convert_element_type x3 -> x1, local copies, waits for them, and re-layouts: 39.3 us -> 1.15 us  [on_device(): normed_mid = normed_mid_f.astype(bf16)]
    concatenate x0 -> x5, other arithmetic: none -> 26.9 us  [the longest x1 19.8 us: on_device(): jnp.concatenate([jnp.pad(grad_z, ((0, 0), (0, 128))), grad_x, grad_bc, jn...]
    ppermute x12 -> x1, starting transfers between devices: 23 us -> 1.46 us  [from_behind(): lax.ppermute(value, axis, [(source, source + steps) for source in range(l...]
    unnamed x207 -> x163, local copies, waits for them, and re-layouts: 43.6 us -> 22.6 us
    convert_element_type x5 -> x1, other arithmetic: 19.9 us -> 0.07 us  [on_device(): (jnp.arange(expert_count) == experts).astype(f32)[:, None, :]]
  transfers between devices with their start and end apart: 18 -> 1, of which waited for: 2 -> 0; matrix products, arithmetic and copies ran while one was open for 24% -> 3% of each run, Pallas kernels for 67% -> 0%
where the time goes in v2:
time: 1270 us; the launch traced here: 1260 us
  Pallas kernels  1040 us (82%)
  local copies, waits for them, and re-layouts  81.5 us (6%)
  matrix products  68.1 us (5%)
  other arithmetic  62.1 us (5%)
    pallas_call x2, Pallas kernels, pallas_reduce(): pl.pallas_call(partial(reduce_kernel, pieces, ahead, count, lines, moves,...  401 us
    pallas_call x2, Pallas kernels, pallas_gather(): pl.pallas_call(partial(gather_kernel, pieces, ahead, count, line, moves,...  392 us
    pallas_call x8, Pallas kernels, call_steps(): pl.pallas_call(kernel, grid=(steps,), in_specs=in_specs, out_specs=out_sp...  135 us
    pallas_call x1, Pallas kernels, routed_experts(): pl.pallas_call(experts_kernel, grid=(blocks // TILE, held), in_specs=[tab...  115 us
  transfers between devices with their start and end apart: 1, of which 0 were waited for; matrix products, arithmetic and copies ran while one was open for 3% of the time, Pallas kernels for 0%

profile of v2, /device:TPU:0, one launch (start us, length us, event | category | flops | bytes accessed | tf_op | source)
XLA Modules:
  0.0 1259.6 jit_solution(18281337239581386810)
XLA Ops:
  3.2 2.8 concatenate.62
  6.0 2.7 constant_dynamic-update-slice_fusion.1
  9.9 2.8 constant_dynamic-slice_fusion.2.refs_5_
  15.0 235.3 %shard_map.348 = (bf16[2,2,2,4,48,6448]{5,4,3,2,1,0:T(8,128)(2,1)}, bf16[2,2,2,4,96,1536]{5,4,3,2,1,0:T(8,128)(2,1)}, bf16[2,2,2,4,48,2048]{5,4,3,2,1,0:T(8,128)...) custom-call(bf16[48,6448]{1,0:T(8,128)(2,1)} %refs_0_.1, ...), custom_call_target="tpu_custom_call" | custom-call | flops 1024 | bytes 1024 | tf_op jit(solution)/shard_map/pallas_call | solution.py:1034
  259.6 1.7 copy.127.taps_ref
  262.7 14.8 %fusion.64.x_ref.z_ref = f32[6448,384]{1,0:T(8,128)S(1)} fusion(bf16[1536,6448]{1,0:T(8,128)(2,1)} %bitcast.123, f32[1536]{0:T(1024)S(1)} %reshape.273, f32[384]{0:T(512)S(1)} %add_rsqrt_fusion, bf16[8,1536]{0,1:T(8,128)(2,1)S(1)} %select_bitcast_fusion, bf16[256,1536]{0,1:T(8,128)(2,1)S(1)} %bitcast.120, bf16[384]{0:T(512)(128)(2,1)S(1)} %pad.67.clone), kind=kOutput, calls=%fused_computation.177 | convolution fusion | flops 7611678720 | bytes 30531840 | tf_op jit(solution)/shard_map/dot_general | solution.py:1677
  277.5 3.9 copy-done
  283.5 2.4 shard_map.349.bc_ref.pre_ref
  286.6 10.0 shard_map.350
  296.6 1.6 broadcast_in_dim.118.passed_ref
  299.6 1.6 broadcast_in_dim.121.gain_ref
  301.2 25.5 %shard_map.351 = (f32[3072,256]{1,0:T(8,128)}, bf16[3072,128]{1,0:T(8,128)(2,1)}, bf16[3072,256]{1,0:T(8,128)(2,1)}, f32[8,256]{1,0:T(8,128)}) custom-call(bf16[3072,128]{1,0:T(8,128)(2,1)} %get-tuple-element.74.local_ref, f32[3072,8]{1,0:T(8,128)} %broadcast_in_dim.118.passed_ref, f32[3072,256]{1,0:T(8,128)} %get-tuple-element.75.pre_ref, ...), custom_call_target="tpu_custom_call" | custom-call | flops 1024 | bytes 1024 | tf_op jit(solution)/shard_map/pallas_call | solution.py:568
  326.7 7.0 multiply_reduce_fusion.4
  338.5 2.9 dynamic-slice_dynamic-update-slice_fusion.refs_3_
  344.3 157.2 %shard_map.352 = (bf16[2,2,2,2,256,1536]{5,4,3,2,1,0:T(8,128)(2,1)}, bf16[2,2,2,2,256,1536]{5,4,3,2,1,0:T(8,128)(2,1)}, bf16[2,2,2,2,256,128]{5,4,3,2,1,0:T(8,12...) custom-call(bf16[256,1536]{1,0:T(8,128)(2,1)} %copy.137.refs_0_, ...), custom_call_target="tpu_custom_call", output_to_operand_aliasing={{3}: (3, {}), {4}: (4, {})} | custom-call | flops 1024 | bytes 1024 | tf_op jit(solution)/shard_map/pallas_call | solution.py:1034
  504.3 114.6 %shard_map.353 = (bf16[16,256,1536]{2,1,0:T(8,128)(2,1)}, bf16[16,256,1536]{2,1,0:T(8,128)(2,1)}, f32[16,2,256]{2,1,0:T(2,128)}, bf16[2,1536,1024]{2,1,0:T(8,128)(2,1)}, bf16[2,512,1536]{2,1,0:T(8,128)(2,1)}) custom-call(f32[16,2,256]{2,1,0:T(2,128)} %convert_bitcast_fusion.rank_ref, f32[16,2,256]{2,1,0:T(2,128)} %add_bitcast_fusion.gate_ref, ...), custom_call_target="tpu_custom_call" | custom-call | flops 1024 | bytes 1024 | tf_op jit(solution)/shard_map/pallas_call | solution.py:1553
  619.9 1.9 copy.140
  621.8 2.7 subtract_convert_fusion
  624.6 4.7 fusion.73
  630.7 2.7 convolution_convert_fusion.2
  633.4 1.6 maximum_maximum_fusion.refs_2_
  635.0 182.7 %shard_map.354 = (f32[256,1536]{1,0:T(8,128)}, f32[256,1536]{1,0:T(8,128)}, f32[256,128]{1,0:T(8,128)}, f32[32,1536]{1,0:T(8,128)}, bf16[2,2,384,1024]{3,2,1,0:T(8,128)(2,1)}, /*index=5*/bf16[2,2,512,384]{3,2,1,0:T(8,128)(2,1)}) custom-call(bf16[2,2,2,2,256,1536]{5,4,3,2,1,0:T(8,128)(2,1)} %bitcast.131, bf16[2,2,2,2,256,1536]{5,4,3,2,1,0:T(8,128)(2,1)} %bitcast.130, ...), custom_call_target="tpu_custom_call" | custom-call | flops 1024 | bytes 1024 | tf_op jit(solution)/shard_map/pallas_call | solution.py:1208
  817.7 3.1 copy.143
  821.2 5.3 convolution_add_fusion.2
  828.6 2.0 copy-done.17
  830.6 10.3 multiply_reduce_fusion
  842.4 8.5 shard_map.355
  850.9 35.6 %shard_map.356 = (f32[3072,256]{1,0:T(8,128)}, bf16[3072,128]{1,0:T(8,128)(2,1)}, f32[48,256]{1,0:T(8,128)}, f32[48,256]{1,0:T(8,128)}, f32[256,256]{1,0:T(8,128)}) custom-call(bf16[3072,128]{1,0:T(8,128)(2,1)} %get-tuple-element.98.local_ref, f32[3072,8]{1,0:T(8,128)} %broadcast_in_dim.118.passed_ref, f32[3072,256]{1,0:T(8,128)} %get-tuple-element.75.pre_ref, ...), custom_call_target="tpu_custom_call" | custom-call | flops 1024 | bytes 1024 | tf_op jit(solution)/shard_map/pallas_call | solution.py:568
  886.5 19.6 %shard_map.357 = (bf16[3072,384]{1,0:T(8,128)(2,1)}, f32[3072,8]{1,0:T(8,128)}, f32[48,256]{1,0:T(8,128)}, f32[48,256]{1,0:T(8,128)}, f32[48,128]{1,0:T(8,128)}, /*index=5*/f32[256,256]{1,0:T(8,128)}) custom-call(f32[3072,256]{1,0:T(8,128)} %get-tuple-element.100.grad_in_ref, f32[3072,256]{1,0:T(8,128)} %get-tuple-element.99.grad_y_ref, ...), custom_call_target="tpu_custom_call" | custom-call | flops 1024 | bytes 1024 | tf_op jit(solution)/shard_map/pallas_call | solution.py:568
  906.0 1.7 add.250.grad_ref
  908.8 3.3 shard_map.358
  912.2 1.7 fusion.66
  913.9 19.8 %fusion.2.grad_ref = bf16[6448,384]{1,0:T(8,128)(2,1)} fusion(bf16[48,256]{1,0:T(8,128)(2,1)S(1)} %get-tuple-element.208, bf16[3072,256]{1,0:T(8,128)(2,1)S(1)} %copy-done.22, bf16[256,384]{1,0:T(8,128)(2,1)} %get-tuple-element.106, bf16[3072,384]{1,0:T(8,128)(2,1)S(1)} %copy-done.20), kind=kLoop, calls=%fused_computation.6 | loop fusion | flops 29712384 | bytes 9105408 | tf_op jit(solution)/shard_map/concatenate | solution.py:1826
  935.3 30.4 %shard_map.359 = (bf16[1536,6448]{1,0:T(8,128)(2,1)}, f32[1536,384]{1,0:T(8,128)}) custom-call(bf16[1536,384]{1,0:T(8,128)(2,1)} %fusion.63.normed_ref, bf16[1536,6448]{1,0:T(8,128)(2,1)} %bitcast.124, bf16[6448,384]{1,0:T(8,128)(2,1)} %fusion.2.grad_ref), custom_call_target="tpu_custom_call" | custom-call | flops 1024 | bytes 1024 | tf_op jit(solution)/shard_map/pallas_call | solution.py:568
  965.7 2.7 fusion.68
  970.4 8.2 convolution_convert_fusion
  978.6 4.4 convolution_convert_fusion.1
  984.3 3.2 copy.141
  987.5 4.6 fusion.8
  992.7 1.8 copy.151
  994.7 2.2 fusion.19.refs_5_
  997.0 6.6 convert_add_fusion
  1009.0 2.1 reshape.269
  1016.3 218.3 %shard_map.360 = (f32[48,6448]{1,0:T(8,128)}, f32[96,1536]{1,0:T(8,128)}, f32[48,2048]{1,0:T(8,128)}, f32[24,128]{1,0:T(8,128)}, bf16[2,384,1024]{2,1,0:T(8,128)(2,1)}, /*index=5*/bf16[2,512,384]{2,1,0:T(8,128)(2,1)}) custom-call(bf16[2,2,2,4,48,6448]{5,4,3,2,1,0:T(8,128)(2,1)} %bitcast.122, bf16[2,2,2,4,96,1536]{5,4,3,2,1,0:T(8,128)(2,1)} %bitcast.117, ...), custom_call_target="tpu_custom_call" | custom-call | flops 1024 | bytes 1024 | tf_op jit(solution)/shard_map/pallas_call | solution.py:1208
  1240.1 1.7 fusion.14
  1241.8 3.2 copy.156
  1250.6 1.9 pad_maximum_fusion.2
  1252.5 3.9 pad_maximum_fusion
  (284 shorter events, 67.3 us)
Async XLA Ops:
  0.7 8.0 copy-start.23
  9.9 3.8 copy-start.43
  9.9 3.8 copy-start.44
  15.0 237.5 %copy-start.33 = (bf16[1,256,1536]{2,1,0:T(8,128)(2,1)S(1)}, bf16[1,256,1536]{2,1,0:T(8,128)(2,1)}, u32[]{:S(2)}) copy-start(bf16[1,256,1536]{2,1,0:T(8,128)(2,1)} %param.21) | copy-start | bytes 2359300
  258.6 3.5 copy-start.70
  258.7 18.8 %copy-start.51 = (bf16[384]{0:T(512)(128)(2,1)}, bf16[384]{0:T(512)(128)(2,1)S(1)}, u32[]{:S(2)}) copy-start(bf16[384]{0:T(512)(128)(2,1)S(1)} %pad.67.clone) | copy-start | bytes 2308
  259.1 18.3 %copy-start.56 = (f32[384]{0:T(512)}, f32[384]{0:T(512)S(1)}, u32[]{:S(2)}) copy-start(f32[384]{0:T(512)S(1)} %add_rsqrt_fusion) | copy-start | bytes 4612
  262.6 18.9 %copy-start.72 = (f32[48]{0:T(128)}, f32[48]{0:T(128)S(1)}, u32[]{:S(2)}) copy-start(f32[48]{0:T(128)S(1)} %get-tuple-element.245) | copy-start | bytes 580
  262.7 18.7 %copy-start.64 = (f32[48]{0:T(128)S(1)}, f32[48]{0:T(128)}, u32[]{:S(2)}) copy-start(f32[48]{0:T(128)} %param.29) | copy-start | bytes 580
  277.5 3.9 copy-start
  281.5 4.4 copy-start.30
  281.8 4.0 copy-start.18
  283.5 16.2 %copy-start.45 = (f32[3072]{0:T(1024)}, f32[3072]{0:T(1024)S(1)}, u32[]{:S(2)}) copy-start(f32[3072]{0:T(1024)S(1)} %reshape.280) | copy-start | bytes 36868
  286.6 11.6 copy-start.63
  338.5 3.9 copy-start.7
  624.6 4.7 copy-start.8
  624.6 4.8 copy-start.16
  630.7 190.5 %copy-start.36 = (bf16[256,1024]{1,0:T(8,128)(2,1)}, bf16[256,1024]{1,0:T(8,128)(2,1)S(1)}, u32[]{:S(2)}) copy-start(bf16[256,1024]{1,0:T(8,128)(2,1)S(1)} %get-tuple-element.223) | copy-start | bytes 1572868
  821.1 5.3 copy-start.2
  821.2 5.3 copy-start.11
  821.2 5.3 copy-start.49
  828.6 12.4 copy-start.4
  886.5 19.6 %copy-start.40 = (f32[256,256]{1,0:T(8,128)S(1)}, f32[256,256]{1,0:T(8,128)}, u32[]{:S(2)}) copy-start(f32[256,256]{1,0:T(8,128)} %get-tuple-element.104) | copy-start | bytes 786436
  886.5 21.3 %copy-start.19 = (f32[48,256]{1,0:T(8,128)S(1)}, f32[48,256]{1,0:T(8,128)}, u32[]{:S(2)}) copy-start(f32[48,256]{1,0:T(8,128)} %copy-done.18) | copy-start | bytes 147460
  908.7 3.4 copy-start.31
  908.8 3.4 copy-start.65
  908.8 3.4 copy-start.67
  908.8 3.4 copy-start.68
  908.8 3.4 copy-start.69
  908.8 5.1 copy-start.20
  908.8 5.1 copy-start.22
  913.9 19.8 %copy-start.52 = (bf16[384]{0:T(512)(128)(2,1)S(1)}, bf16[384]{0:T(512)(128)(2,1)}, u32[]{:S(2)}) copy-start(bf16[384]{0:T(512)(128)(2,1)} %copy-done.51) | copy-start | bytes 2308
  913.9 19.8 %copy-start.57 = (f32[384]{0:T(512)S(1)}, f32[384]{0:T(512)}, u32[]{:S(2)}) copy-start(f32[384]{0:T(512)} %copy-done.56) | copy-start | bytes 4612
  968.6 42.5 %collective-permute-start = (f32[8,1536]{1,0:T(8,128)S(1)}, f32[8,1536]{1,0:T(8,128)S(1)}, u32[]{:S(2)}, u32[]{:S(2)}) collective-permute-start(f32[8,1536]{1,0:T(8,128)S(1)} %copy.148), channel_id=1, source_target_pairs={{1,0},{2,1},{3,2},{5,4},{6,5},{7,6},{9,8},{10,9},{11,10},{13,12},{... | collective-permute-start | bytes 147464 | tf_op jit(solution)/shard_map/ppermute | solution.py:23
  970.4 21.7 %copy-start.54 = (f32[256]{0:T(256)}, f32[256]{0:T(256)S(1)}, u32[]{:S(2)}) copy-start(f32[256]{0:T(256)S(1)} %fusion.15) | copy-start | bytes 3076
  970.4 8.3 copy-start.37
  987.5 7.0 copy-start.42
  987.5 7.1 copy-start.47
  996.9 6.7 copy-start.66
  997.0 7.3 copy-start.9
  1004.4 3.9 copy-start.50
  1016.3 223.7 %copy-start.55 = (f32[256]{0:T(256)S(1)}, f32[256]{0:T(256)}, u32[]{:S(2)}) copy-start(f32[256]{0:T(256)} %copy-done.54) | copy-start | bytes 3076
  1016.3 223.7 %copy-start.5 = (f32[256,1536]{0,1:T(8,128)S(1)}, f32[256,1536]{0,1:T(8,128)}, u32[]{:S(2)}) copy-start(f32[256,1536]{0,1:T(8,128)} %copy-done.4) | copy-start | bytes 4718596
  1016.3 223.7 %copy-start.53 = (f32[256]{0:T(256)S(1)}, f32[256]{0:T(256)}, u32[]{:S(2)}) copy-start(f32[256]{0:T(256)} %fusion.52) | copy-start | bytes 3076
  1241.8 4.6 copy-start.38
  1241.8 5.4 copy-start.27
  1241.8 5.4 copy-start.34
  1252.5 3.9 copy-start.29
  (27 other events, 62.7 us)

commit v3 on v2

--- a/solution.py
+++ b/solution.py
@@ -4,6 +4,7 @@
 import jax.numpy as jnp
 from jax import lax
 from jax.experimental import pallas as pl
+from jax.experimental.layout import Layout, with_layout_constraint
 from jax.experimental.pallas import tpu as pltpu
 from jax.sharding import PartitionSpec as P
 
@@ -564,7 +565,7 @@
     return value.astype(jnp.bfloat16)
 
 
-def call_steps(kernel, steps, ins, in_specs, outs, out_specs, scratch=(), name_id=None):
+def call_steps(kernel, steps, ins, in_specs, outs, out_specs, scratch=(), name_id=None, micros=0):
     return pl.pallas_call(
         kernel,
         grid=(steps,),
@@ -572,7 +573,7 @@
         out_specs=out_specs,
         out_shape=outs,
         scratch_shapes=list(scratch),
-        cost_estimate=BRIEF,
+        cost_estimate=pl.CostEstimate(flops=1024 + micros * 10**9, bytes_accessed=1024, transcendentals=0),
         compiler_params=pltpu.CompilerParams(
             vmem_limit_bytes=VMEM_MOST,
             dimension_semantics=("arbitrary",),
@@ -808,7 +809,7 @@
         [wide, wide, wide, block((WIDE, 8), lambda i: (i, 0)), whole(gate_rows), whole(bc_pre),
          block((GROUP, tokens), lambda i: (i, 0)), whole(flags)],
         [f32_out(DI, tokens), bf16_out(DI, tokens), bf16_out(DI, STATE)],
-        [wide, wide, block((WIDE, STATE), lambda i: (i, 0))],
+        [wide, wide, block((WIDE, STATE), lambda i: (i, 0))], micros=9,
     )
 
 
@@ -825,7 +826,7 @@
         [f32_out(DI, tokens), bf16_out(DI, STATE), f32_out(HEADS, tokens), f32_out(HEADS, tokens),
          f32_out(2 * STATE, tokens)],
         [wide, states, rows, rows, block((2 * STATE, tokens), lambda i: (0, 0))],
-        (square, square, square) + chain_room(groups), name_id=name_id,
+        (square, square, square) + chain_room(groups), name_id=name_id, micros=35,
     )
 
 
@@ -845,7 +846,7 @@
         [bf16_out(DI, proj.shape[1]), f32_out(DI, 8), f32_out(HEADS, tokens), f32_out(HEADS, tokens),
          f32_out(HEADS, 128), f32_out(2 * STATE, tokens)],
         [longer, narrow, rows, rows, block((GROUP, 128), lambda i: (i, 0)),
-         block((2 * STATE, tokens), lambda i: (0, 0))],
+         block((2 * STATE, tokens), lambda i: (0, 0))], micros=19,
     )
 
 
@@ -888,6 +889,7 @@
     for away in line:
         others[away] = (dp, lax.rem(z + away, 4))
     others["beside"] = (dp, flipped(z, 1))
+    others["across"] = (dp, 3 - z)
     return y, x, core, z, others
 
 
@@ -937,6 +939,7 @@
     y, x, core, z, others = places(line)
     deep = len(line) + 1
     slot = z if deep == 4 else lax.div(z, 2)
+    inner = jnp.logical_and(z > 0, z < 3)
     greet(others)
     sems = (sent, came)
 
@@ -958,6 +961,9 @@
         own = ins[array].at[area]
         mine = out.at[(y, x, core) + ((slot,) if line else ()) + area]
         lane = out.at[(y, x, core) + rest]
+        at_pair = lax.div(z, 2)
+        pair = out.at[(y, x, core, pl.ds(2 * at_pair, 2)) + area] if deep == 4 else None
+        rest_pair = out.at[(y, x, core, pl.ds(2 - 2 * at_pair, 2)) + area] if deep == 4 else None
         if first == "x":
             plane = out.at[(y, slice(None), core) + rest]
         else:
@@ -965,10 +971,9 @@
         every = out.at[(slice(None), slice(None), core) + rest]
         return {
             "keep": lambda: pltpu.make_async_copy(own, mine, kept.at[number]),
-            "line": lambda: [
-                send(own, mine, sems, number, away - 1, others[away])
-                for away in line
-            ],
+            "line": lambda: [send(own, mine, sems, number, 0, others["beside" if deep == 4 else 2])],
+            "across": lambda: send(pair, pair, sems, number, 1, others["across"]),
+            "outward": lambda: send(rest_pair, rest_pair, sems, number, 2, others["beside"]),
             "first": lambda: send(lane if line else own, lane, sems, number, 3, others[first]),
             "second": lambda: send(plane, plane, sems, number, 4, others[second]),
             "core": lambda: send(every, every, sems, number, 5, others["core"]),
@@ -985,15 +990,35 @@
         if not 0 <= number < len(pieces):
             return
         leg = legs(number)
+        if stage < 2 and deep < 4:
+            return
         if stage == 0:
             leg["keep"]().wait()
-            for copy in leg["line"]():
-                copy.wait_recv()
+            leg["line"]()[0].wait_recv()
+
+            @pl.when(inner)
+            def _():
+                leg["across"]().start()
+        elif stage == 1:
+
+            @pl.when(inner)
+            def _():
+                leg["across"]().wait_recv()
+                leg["outward"]().start()
+        elif stage == 2:
+            if deep == 4:
+
+                @pl.when(jnp.logical_not(inner))
+                def _():
+                    leg["outward"]().wait_recv()
+            else:
+                leg["keep"]().wait()
+                leg["line"]()[0].wait_recv()
             leg["first"]().start()
-        elif stage == 1:
+        elif stage == 3:
             leg["first"]().wait_recv()
             leg["second"]().start()
-        elif stage == 2:
+        elif stage == 4:
             leg["second"]().wait_recv()
             leg["core"]().start()
         else:
@@ -1002,17 +1027,24 @@
     for number in range(2 * ahead):
         begin(number)
     pairs = -(-len(pieces) // 2)
-    for turn in range(pairs + 3):
+    early = 0 if deep == 4 else 2
+    for turn in range(pairs + 5 - early):
         extra_turn(turn, pairs)
-        for stage in range(4):
-            for number in (2 * (turn - stage), 2 * (turn - stage) + 1):
+        for stage in range(early, 6):
+            for number in (2 * (turn - stage + early), 2 * (turn - stage + early) + 1):
                 advance(number, stage)
-                if stage == 0 and number < len(pieces):
+                if stage == early and number < len(pieces):
                     begin(number + 2 * ahead)
     for number in range(len(pieces)):
         leg = legs(number)
         for copy in leg["line"]() + [leg["first"](), leg["second"](), leg["core"]()]:
             copy.wait_send()
+        if deep == 4:
+
+            @pl.when(inner)
+            def _():
+                leg["across"]().wait_send()
+                leg["outward"]().wait_send()
     for copy in extra():
         copy.wait()
 
@@ -1190,7 +1222,7 @@
         copy.wait()
 
 
-def pallas_reduce(parts, steps, name_id, lines=None, ahead=2, more=(), more_shapes=(), moves=()):
+def pallas_reduce(parts, steps, name_id, lines=None, ahead=2, more=(), more_shapes=(), moves=(), same=()):
     lines = lines or [(1, 2, 3)] * len(parts)
     shapes = [part.shape[1:] for part in parts]
     pieces = []
@@ -1219,6 +1251,7 @@
         ]
         + move_room(moves)
         + room,
+        input_output_aliases={count + at: count + at for at in same},
         cost_estimate=BRIEF,
         compiler_params=pltpu.CompilerParams(
             collective_id=name_id, has_side_effects=True, vmem_limit_bytes=VMEM_MOST
@@ -1226,38 +1259,66 @@
         )(*[part.reshape((2, 2, 2) + ((len(line) + 1,) if line else ()) + shape) for part, shape, line in zip(parts, shapes, lines)], *more)
 
 
-def proj_back_kernel(normed_ref, weight_ref, grad_ref, grad_weight_ref, grad_normed_ref):
-    step, width = pl.program_id(0), weight_ref.shape[1]
-    last = pl.num_programs(0) - 1
-    grad = grad_ref[...]
-    grad_weight_ref[...] = half(mul_nt(normed_ref[...], grad))
+def proj_back_kernel(
+    normed_ref, weight_ref, grad_z_ref, grad_x_ref, grad_rest_ref, rows_ref,
+    grad_weight_ref, grad_normed_ref, came_ref, sent, came,
+):
+    step, groups = pl.program_id(0), DI // WIDE
+    tokens = grad_z_ref.shape[1]
+    dp, z = lax.axis_index("dp"), lax.axis_index("ctx")
+    far = (dp, lax.rem(z + 2, 4))
+
+    def exchange():
+        return pltpu.make_async_remote_copy(
+            src_ref=rows_ref,
+            dst_ref=came_ref,
+            send_sem=sent,
+            recv_sem=came,
+            device_id=far,
+            device_id_type=pl.DeviceIdType.MESH,
+        )
 
     @pl.when(step == 0)
     def _():
         grad_normed_ref[...] = jnp.zeros_like(grad_normed_ref)
-
-    @pl.when(step < last)
+        greet({"far": far})
+        exchange().start()
+
+    @pl.when(step == 2 * groups)
     def _():
-        grad_normed_ref[...] += mul_nn(weight_ref[...], grad)
-
-    @pl.when(step == last)
+        exchange().wait()
+
+    @pl.when(step < groups)
     def _():
-        left = PROJ - last * width
+        grad_weight_ref[...] = half(mul_nt(normed_ref[:, :tokens], grad_z_ref[...]))
+        grad_normed_ref[:, :tokens] += mul_nn(weight_ref[...], grad_z_ref[...])
+
+    @pl.when(jnp.logical_and(step >= groups, step < 2 * groups))
+    def _():
+        grad_weight_ref[...] = half(mul_nt(normed_ref[...], grad_x_ref[...]))
+        grad_normed_ref[...] += mul_nn(weight_ref[...], grad_x_ref[...])
+
+    @pl.when(step == 2 * groups)
+    def _():
         lane = lax.broadcasted_iota(jnp.int32, weight_ref.shape, 1)
-        row = lax.broadcasted_iota(jnp.int32, grad.shape, 0)
-        weight = jnp.where(lane < left, weight_ref[...], jnp.zeros_like(weight_ref))
-        grad_normed_ref[...] += mul_nn(weight, jnp.where(row < left, grad, jnp.zeros_like(grad)))
-
-
-def proj_back(normed_t, weight, grad_t):
+        weight = jnp.where(lane < PROJ - 2 * DI, weight_ref[...], jnp.zeros_like(weight_ref))
+        grad_weight_ref[...] = half(mul_nt(normed_ref[...], grad_rest_ref[...]))
+        grad_normed_ref[...] += mul_nn(weight, grad_rest_ref[...])
+
+
+def proj_back(normed_t, weight, grad_z, grad_x, grad_rest, rows, name_id):
     features, tokens = normed_t.shape
-    width = 512
+    groups = DI // WIDE
     return call_steps(
-        proj_back_kernel, -(-PROJ // width), (normed_t, weight, grad_t),
-        [whole(normed_t), block((features, width), lambda i: (0, i)), block((width, tokens), lambda i: (i, 0))],
-        [bf16_out(features, PROJ), f32_out(features, tokens)],
-        [block((features, width), lambda i: (0, i)), block((features, tokens), lambda i: (0, 0))],
-
+        proj_back_kernel, 2 * groups + 1, (normed_t, weight, grad_z, grad_x, grad_rest, rows),
+        [whole(normed_t), block((features, WIDE), lambda i: (0, i)),
+         block((WIDE, grad_z.shape[1]), lambda i: (jnp.minimum(i, groups - 1), 0)),
+         block((WIDE, tokens), lambda i: (jnp.clip(i - groups, 0, groups - 1), 0)), whole(grad_rest),
+         pl.BlockSpec(memory_space=pl.ANY)],
+        [bf16_out(features, PROJ), f32_out(features, tokens), bf16_out(*rows.shape)],
+        [block((features, WIDE), lambda i: (0, i)), block((features, tokens), lambda i: (0, 0)),
+         pl.BlockSpec(memory_space=pl.ANY)],
+        (pltpu.SemaphoreType.DMA, pltpu.SemaphoreType.DMA), name_id=name_id, micros=27,
     )
 
 
@@ -1414,6 +1475,18 @@
     return lax.ppermute(value, "ctx", [(source, source ^ bits) for source in range(count)])
 
 
+def other_strip(start):
+    def at(z):
+        first = EXP_DEV // 2 * (1 - lax.div(z, 2))
+        return (pl.ds(first, EXP_DEV // 2), pl.ds(start, STRIP))
+
+    return at
+
+
+def columns(place, start, size):
+    return lambda z: place(z) + (pl.ds(start, size),)
+
+
 def held_experts(shard, other):
     held = EXP_DEV // 2
     half_at = lax.div(lax.axis_index("ctx"), 2)
@@ -1451,8 +1524,8 @@
     return lax.dynamic_slice_in_dim(whole, flipped(lax.axis_index("ctx"), bits) * width, width, axis)
 
 
-def expert_owners(near, far):
-    far = far.astype(jnp.float32)
+def expert_owners(near, far, late):
+    far = far.astype(jnp.float32) + late
     low = lax.div(lax.axis_index("ctx"), 2) == 0
     return jnp.concatenate([jnp.where(low, near, far), jnp.where(low, far, near)], axis=0)
 
@@ -1624,29 +1697,30 @@
     small_flat = jnp.concatenate([part.reshape(-1) for part in small_parts])
     small_flat = jnp.pad(small_flat, (0, 4096 - small_flat.shape[0])).reshape(32, 128)
     edge_rows = layer_in[0, row_count - halo :].reshape(-1, 128)
-    gate_up = jnp.concatenate([e_gate, e_up], axis=2)
     width, hidden = e_gate.shape[1:]
     first_strips, down_strips = strips(width), strips(hidden)
-    w_in_all, w_out_all, shared_all, sdown_all, small_all, expert_first, expert_down = pallas_gather(
-        [
-            w_in,
-            w_out,
-            jnp.concatenate([w_sgate, w_sup], axis=1),
-            w_sdown,
-            jnp.concatenate([small_flat, edge_rows]),
-        ],
-        [(16, 1664), (16, 1536), (16, 1024), (16, 1536), (128, 128)],
+    w_in_all, w_out_all, small_all, expert_first, expert_down = pallas_gather(
+        [w_in, w_out, jnp.concatenate([small_flat, edge_rows])],
+        [(16, 1664), (16, 1536), (128, 128)],
         1,
-        ahead=3,
-        more=[held_experts(gate_up, True), held_experts(e_down, True)],
+        ahead=6,
+        more=[e_gate, e_up, e_down],
         more_shapes=[(held, d_model, 2 * hidden), (held, hidden, d_model)],
         moves=[
-            (part, part, strip(start), quarter(axis, width, 0, start), 2)
-            for part, axis, starts in ((0, 1, first_strips), (1, 2, down_strips))
-            for start in starts
-        ],
-    )
-    expert_first = with_quarter(expert_first, held_experts(gate_up, False), 1)
+            (part, 0, other_strip(start), columns(quarter(1, width, 0, start), part * hidden, hidden), 2)
+            for start in first_strips
+            for part in range(2)
+        ]
+        + [(2, 1, other_strip(start), quarter(2, width, 0, start), 2) for start in down_strips],
+    )
+    pair_at = lax.div(ctx_place, 2)
+    sent = nothing(w_in_all)
+    shared_all = lax.all_gather(
+        (jnp.concatenate([w_sgate, w_sup], axis=1).astype(f32) + sent).astype(bf16), BOTH, axis=0
+    )
+    sdown_all = lax.all_gather((w_sdown.astype(f32) + sent).astype(bf16), BOTH, axis=0)
+    own_first = jnp.concatenate([held_experts(e_gate, False), held_experts(e_up, False)], axis=2)
+    expert_first = with_quarter(expert_first, own_first, 1)
     expert_down = with_quarter(expert_down, held_experts(e_down, False), 2)
     edge_all = small_all[:, small_flat.shape[0] :].reshape(devices, halo, d_model)
     small_all = small_all[:, : small_flat.shape[0]].reshape(devices, 4096)
@@ -1722,7 +1796,8 @@
             for start in starts
         ],
     )
-    shared_hidden = jnp.dot(normed_mid, shared_weight, preferred_element_type=f32)
+    normed_later = (normed_mid.astype(f32) + nothing(token_rows)).astype(bf16)
+    shared_hidden = jnp.dot(normed_later, shared_weight, preferred_element_type=f32)
     shared_gate, shared_up = jnp.split(shared_hidden, 2, axis=1)
     shared_act = (jax.nn.silu(shared_gate) * shared_up).astype(bf16)
     shared_out = jnp.dot(shared_act, sdown_weight, preferred_element_type=f32)
@@ -1749,13 +1824,19 @@
     )
     grad_shared_out = out_grad[0]
     grad_w_sdown = times_rows(shared_act, grad_shared_out)
-    back_rows, routed, back_side, sum_sdown, beside_first, beside_down = pallas_reduce(
-        [grad_slot_rows, routed_rows, back_side, owned(grad_w_sdown)],
-        [(16, 1536), (16, 1536), (128, 128), (16, 1536)],
+    grad_shared_act = times_back(grad_shared_out, sdown_weight)
+    grad_sgate = (grad_shared_act * shared_up * silu_slope(shared_gate)).astype(bf16)
+    grad_sup = (grad_shared_act * jax.nn.silu(shared_gate)).astype(bf16)
+    grad_shared = jnp.concatenate([grad_sgate, grad_sup], axis=1)
+    grad_w_shared = times_rows(normed_mid, grad_shared)
+    back_rows, back_side, sum_sdown, sum_shared, beside_first, beside_down, routed_rows = pallas_reduce(
+        [grad_slot_rows, back_side, owned(grad_w_sdown), owned(grad_w_shared)],
+        [(16, 1536), (128, 128), (16, 1536), (16, 1024)],
         4,
-        lines=[(2,), (2,), (2,), (1, 2, 3)],
-        more=[grad_first, grad_down],
-        more_shapes=[(2, held, width, 2 * hidden), (2, held, hidden, width)],
+        lines=[(2,), (2,), (1, 2, 3), (1, 2, 3)],
+        more=[grad_first, grad_down, routed_rows],
+        more_shapes=[(2, held, width, 2 * hidden), (2, held, hidden, width), routed_rows.shape],
+        same=(2,),
         moves=[
             (part, part, quarter(axis, width, 2 * far + 1, start), strip(start, far), 1)
             for far in (1, 0)
@@ -1763,21 +1844,18 @@
             for start in starts
         ],
     )
-    far_first, far_down = (
-        half(own_quarter(whole, axis, 2).astype(f32) + beside[1].astype(f32))
-        for whole, beside, axis in ((grad_first, beside_first, 1), (grad_down, beside_down, 2))
-    )
+    routed = lax.psum_scatter(
+        routed_rows.reshape(-1, 2, row_count, d_model), "dp", scatter_dimension=0
+    )
+    routed = with_layout_constraint(routed, Layout(major_to_minor=(0, 1, 2)))
+    routed_own = lax.dynamic_index_in_dim(routed, pair_at, 0, keepdims=False)
+    routed_far = lax.dynamic_index_in_dim(routed, 1 - pair_at, 0, keepdims=False)
     near_first, near_down = (
         own_quarter(whole, axis, 0).astype(f32) + beside[0].astype(f32)
         for whole, beside, axis in ((grad_first, beside_first, 1), (grad_down, beside_down, 2))
     )
 
     grad_top = out_grad[0].astype(f32)
-    grad_shared_act = times_back(grad_shared_out, sdown_weight)
-    grad_sgate = (grad_shared_act * shared_up * silu_slope(shared_gate)).astype(bf16)
-    grad_sup = (grad_shared_act * jax.nn.silu(shared_gate)).astype(bf16)
-    grad_shared = jnp.concatenate([grad_sgate, grad_sup], axis=1)
-    grad_w_shared = times_rows(normed_mid, grad_shared)
     grad_mid_shared = times_back(grad_shared, shared_weight)
     grad_gates = back_side[:, :expert_count] + back_side[:, expert_count : 2 * expert_count]
     grad_pick = gates * (grad_gates - jnp.sum(gates * grad_gates, axis=-1, keepdims=True))
@@ -1804,6 +1882,10 @@
     )
     grad_scaled, grad_state_out, grad_cum_inner, grad_skip, grad_bc_inner = mixer_back_inner(
         grad_state_local, passed, pre, grad_y, bc_pre, dt_pos, cumul, cumul_col, flags, seg_col, 8
+    )
+    far_first, far_down = (
+        half(own_quarter(whole, axis, 2).astype(f32) + beside[1].astype(f32))
+        for whole, beside, axis in ((grad_first, beside_first, 1), (grad_down, beside_down, 2))
     )
     grad_x, grad_taps_x, grad_dt, grad_cum_join, grad_last, grad_bc_join = mixer_back_join(
         grad_scaled, grad_y, pre, projected, taps, masks, state_in, grad_state_out,
@@ -1823,16 +1905,16 @@
     head_sums_all = jnp.concatenate(
         [jnp.sum(grad_raw, axis=1), jnp.sum(decay * grad_decay, axis=1), jnp.sum(grad_skip, axis=1)]
     )
-    grad_proj = jnp.concatenate(
+    grad_rest = jnp.concatenate(
         [
-            jnp.pad(grad_z, ((0, 0), (0, 128))),
-            grad_x,
             grad_bc,
-            jnp.pad(grad_raw.astype(bf16), ((0, 0), (0, 128))),
+            jnp.pad(grad_raw.astype(bf16), ((0, WIDE - 2 * STATE - HEADS), (0, 128))),
         ]
     )
     normed_t = normed.T
-    grad_w_in, grad_normed = proj_back(normed_t, weight_in, grad_proj)
+    grad_w_in, grad_normed, routed_far = proj_back(
+        normed_t, weight_in, grad_z, grad_x, grad_rest, routed_far, 9
+    )
     grad_normed = grad_normed.T
     edge_grad = from_behind(grad_normed[row_count + 128 - halo :], "ctx", -1)
     grad_normed = jnp.concatenate(
@@ -1856,9 +1938,9 @@
         axis=1,
     )
     small_grads = jnp.pad(small_grads, ((0, 0), (0, 3072 - small_grads.shape[1])))
-    sum_in, sum_out, sum_shared, sum_small, far_first, far_down = pallas_reduce(
-        [owned(grad_w_in), owned(grad_w_out), owned(grad_w_shared), small_grads.reshape(devices, 24, 128)],
-        [(16, 1664), (16, 1536), (16, 1024), (24, 128)],
+    sum_in, sum_out, sum_small, far_first, far_down = pallas_reduce(
+        [owned(grad_w_in), owned(grad_w_out), small_grads.reshape(devices, 24, 128)],
+        [(16, 1664), (16, 1536), (24, 128)],
         6,
         ahead=3,
         more=[far_first, far_down],
@@ -1869,11 +1951,12 @@
             for start in starts
         ],
     )
-    layer_out = (resid_mid + shared_out + routed).astype(bf16)[None]
+    summed = nothing(sum_small)
+    layer_out = (resid_mid + shared_out + routed_own.astype(f32) + routed_far.astype(f32) + summed).astype(bf16)[None]
     sum_sgate, sum_sup = jnp.split(sum_shared, 2, axis=1)
-    grad_e_gate = expert_owners(near_first[..., :hidden], far_first[..., :hidden])
-    grad_e_up = expert_owners(near_first[..., hidden:], far_first[..., hidden:])
-    grad_e_down = expert_owners(near_down, far_down)
+    grad_e_gate = expert_owners(near_first[..., :hidden], far_first[..., :hidden], summed)
+    grad_e_up = expert_owners(near_first[..., hidden:], far_first[..., hidden:], summed)
+    grad_e_down = expert_owners(near_down, far_down, summed)
     sum_small = sum_small.reshape(-1)
     taken, mine = 0, []
     for part in small_parts:

time: 1270 us -> 1210 us (0.953)
  Pallas kernels: 1040 us -> 987 us
  other arithmetic: 62.1 us -> 43.8 us
  between operations: 3.19 us -> 18.6 us
    pallas_call x2, Pallas kernels: 392 us -> 355 us  [pallas_gather(): pl.pallas_call(partial(gather_kernel, pieces, ahead, count, line, moves,...]
    pallas_call x2, Pallas kernels: 401 us -> 368 us  [pallas_reduce(): pl.pallas_call(partial(reduce_kernel, pieces, ahead, count, lines, moves,...]
    concatenate x2 -> x1, other arithmetic: 20.5 us -> 0.78 us  [on_device(): jnp.concatenate([grad_bc, jnp.pad(grad_raw.astype(bf16), ((0, WIDE - 2 *...]
    pallas_call x8, Pallas kernels: 135 us -> 150 us  [call_steps(): pl.pallas_call(kernel, grid=(steps,), in_specs=in_specs, out_specs=out_sp...]
  transfers between devices with their start and end apart: 1 -> 4, of which waited for: 0 -> 0; matrix products, arithmetic and copies ran while one was open for 3% -> 10% of each run, Pallas kernels for 0% -> 33%
where the time goes in v3:
time: 1210 us; the launch traced here: 1200 us
  Pallas kernels  987 us (82%)
  local copies, waits for them, and re-layouts  84.9 us (7%)
  matrix products  67.5 us (6%)
  other arithmetic  43.8 us (4%)
  between operations  18.6 us (2%)
    pallas_call x2, Pallas kernels, pallas_reduce(): pl.pallas_call(partial(reduce_kernel, pieces, ahead, count, lines, moves,...  368 us
    pallas_call x2, Pallas kernels, pallas_gather(): pl.pallas_call(partial(gather_kernel, pieces, ahead, count, line, moves,...  355 us
    pallas_call x8, Pallas kernels, call_steps(): pl.pallas_call(kernel, grid=(steps,), in_specs=in_specs, out_specs=out_sp...  150 us
    pallas_call x1, Pallas kernels, routed_experts(): pl.pallas_call(experts_kernel, grid=(blocks // TILE, held), in_specs=[tab...  114 us
    unnamed x159, local copies, waits for them, and re-layouts  24.7 us
  transfers between devices with their start and end apart: 4, of which 0 were waited for; matrix products, arithmetic and copies ran while one was open for 10% of the time, Pallas kernels for 33%

profile of v3, /device:TPU:0, one launch (start us, length us, event | category | flops | bytes accessed | tf_op | source)
XLA Modules:
  0.0 1203.1 jit_solution(11193799717906507462)
XLA Ops:
  8.9 2.8 concatenate.72
  13.1 188.3 %shard_map.348 = (bf16[2,2,2,4,48,6448]{5,4,3,2,1,0:T(8,128)(2,1)}, bf16[2,2,2,4,96,1536]{5,4,3,2,1,0:T(8,128)(2,1)}, bf16[2,2,2,4,128,128]{5,4,3,2,1,0:T(8,128)...) custom-call(bf16[48,6448]{1,0:T(8,128)(2,1)} %refs_0_.1, bf16[96,1536]{1,0:T(8,128)(2,1)} %refs_1_.1, ...), custom_call_target="tpu_custom_call" | custom-call | flops 1024 | bytes 1024 | tf_op jit(solution)/shard_map/pallas_call | solution.py:1066
  210.8 1.7 copy.131.taps_ref
  212.5 14.7 %fusion.71.x_ref.z_ref = f32[6448,384]{1,0:T(8,128)S(1)} fusion(bf16[1536,6448]{1,0:T(8,128)(2,1)} %bitcast.181, f32[1536]{0:T(1024)S(1)} %reshape.333, f32[384]{0:T(512)S(1)} %add_rsqrt_fusion, bf16[8,1536]{0,1:T(8,128)(2,1)S(1)} %select_bitcast_fusion, bf16[256,1536]{0,1:T(8,128)(2,1)S(1)} %bitcast.131, bf16[384]{0:T(512)(128)(2,1)S(1)} %pad.64.clone), kind=kOutput, calls=%fused_computation.182 | convolution fusion | flops 7611678720 | bytes 30531840 | tf_op jit(solution)/shard_map/dot_general | solution.py:1751
  227.2 3.9 copy-done
  233.4 2.4 shard_map.349.bc_ref.pre_ref
  235.7 10.0 shard_map.350
  253.5 34.7 %shard_map.351 = (f32[3072,256]{1,0:T(8,128)}, bf16[3072,128]{1,0:T(8,128)(2,1)}, bf16[3072,256]{1,0:T(8,128)(2,1)}, f32[8,256]{1,0:T(8,128)}) custom-call(bf16[3072,128]{1,0:T(8,128)(2,1)} %get-tuple-element.73.local_ref, f32[3072,8]{1,0:T(8,128)} %broadcast_in_dim.118.passed_ref, f32[3072,256]{1,0:T(8,128)} %get-tuple-element.74.pre_ref, ...), custom_call_target="tpu_custom_call" | custom-call | flops 1024 | bytes 1024 | tf_op jit(solution)/shard_map/pallas_call | solution.py:569
  288.8 7.1 multiply_reduce_fusion.4
  299.1 2.2 dynamic-slice_dynamic-update-slice_fusion.refs_4_
  305.9 166.3 %shard_map.352 = (bf16[2,2,2,2,256,1536]{5,4,3,2,1,0:T(8,128)(2,1)}, bf16[2,2,2,2,256,1536]{5,4,3,2,1,0:T(8,128)(2,1)}, bf16[2,2,2,2,256,128]{5,4,3,2,1,0:T(8,12...) custom-call(bf16[256,1536]{1,0:T(8,128)(2,1)} %copy.140.refs_0_, ...), custom_call_target="tpu_custom_call", output_to_operand_aliasing={{3}: (3, {}), {4}: (4, {})} | custom-call | flops 1024 | bytes 1024 | tf_op jit(solution)/shard_map/pallas_call | solution.py:1066
  475.0 114.5 %shard_map.353 = (bf16[16,256,1536]{2,1,0:T(8,128)(2,1)}, bf16[16,256,1536]{2,1,0:T(8,128)(2,1)}, f32[16,2,256]{2,1,0:T(2,128)}, bf16[2,1536,1024]{2,1,0:T(8,128)(2,1)}, bf16[2,512,1536]{2,1,0:T(8,128)(2,1)}) custom-call(f32[16,2,256]{2,1,0:T(2,128)} %convert_bitcast_fusion.rank_ref, f32[16,2,256]{2,1,0:T(2,128)} %add_bitcast_fusion.gate_ref, ...), custom_call_target="tpu_custom_call" | custom-call | flops 1024 | bytes 1024 | tf_op jit(solution)/shard_map/pallas_call | solution.py:1626
  592.4 1.9 copy.144
  594.4 2.7 subtract_convert_fusion
  597.0 1.6 maximum_maximum_fusion.refs_1_
  598.7 6.0 fusion.25
  604.7 3.7 multiply_convert_fusion.2
  608.4 2.7 convolution_convert_fusion.2
  611.1 4.4 convolution_convert_fusion.1
  615.6 171.5 %shard_map.354 = (f32[256,1536]{1,0:T(8,128)}, f32[256,128]{1,0:T(8,128)}, f32[32,1536]{1,0:T(8,128)}, f32[48,2048]{1,0:T(8,128)}, bf16[2,2,384,1024]{3,2,1,0:T(...) custom-call(bf16[2,2,2,2,256,1536]{5,4,3,2,1,0:T(8,128)(2,1)} %bitca, ...), custom_call_target="tpu_custom_call", output_to_operand_aliasing={{6}: (6, {})} | custom-call | flops 1024 | bytes 1024 | tf_op jit(solution)/shard_map/pallas_call | solution.py:1240
  791.5 3.6 copy.147
  795.5 7.2 convolution_add_fusion.2
  806.6 1.7 copy-done.59
  808.4 6.9 multiply_reduce_fusion
  816.6 8.6 shard_map.355
  825.2 35.1 %shard_map.356 = (f32[3072,256]{1,0:T(8,128)}, bf16[3072,128]{1,0:T(8,128)(2,1)}, f32[48,256]{1,0:T(8,128)}, f32[48,256]{1,0:T(8,128)}, f32[256,256]{1,0:T(8,128)}) custom-call(bf16[3072,128]{1,0:T(8,128)(2,1)} %get-tuple-element.95.local_ref, f32[3072,8]{1,0:T(8,128)} %broadcast_in_dim.118.passed_ref, f32[3072,256]{1,0:T(8,128)} %get-tuple-element.74.pre_ref, ...), custom_call_target="tpu_custom_call" | custom-call | flops 35000000512 | bytes 1024 | tf_op jit(solution)/shard_map/pallas_call | solution.py:569
  860.4 18.7 %shard_map.357 = (bf16[3072,384]{1,0:T(8,128)(2,1)}, f32[3072,8]{1,0:T(8,128)}, f32[48,256]{1,0:T(8,128)}, f32[48,256]{1,0:T(8,128)}, f32[48,128]{1,0:T(8,128)}, /*index=5*/f32[256,256]{1,0:T(8,128)}) custom-call(f32[3072,256]{1,0:T(8,128)} %get-tuple-element.97.grad_in_ref, f32[3072,256]{1,0:T(8,128)} %get-tuple-element.96.grad_y_ref, ...), custom_call_target="tpu_custom_call" | custom-call | flops 19000000512 | bytes 1024 | tf_op jit(solution)/shard_map/pallas_call | solution.py:569
  879.0 1.7 add.311.grad_ref
  880.7 3.2 shard_map.358
  885.3 1.8 copy.156
  890.3 2.3 fusion.16.refs_4_
  893.8 5.7 convert_add_fusion
  899.5 5.1 convolution_convert_fusion
  904.6 2.4 constant_dynamic-slice_fusion
  907.0 37.2 %shard_map.359 = (bf16[1536,6448]{1,0:T(8,128)(2,1)}, f32[1536,384]{1,0:T(8,128)}, bf16[256,1536]{1,0:T(8,128)(2,1)}) custom-call(bf16[1536,384]{1,0:T(8,128)(2,1)} %fusion.70.normed_ref, bf16[1536,6448]{1,0:T(8,128)(2,1)} %bitcast.182, bf16[3072,256]{1,0:T(8,128)(2,1)} %get-tuple-element.94.grad_z_ref, bf16[3072,384]{1,0:T(8,128)(2,1)} %get-tuple-element.100.grad_x_ref, ...), custom_call_target="tpu_custom_call" | custom-call | flops 27000000512 | bytes 1024 | tf_op jit(solution)/shard_map/pallas_call | solution.py:569
  944.2 3.0 fusion.75
  949.9 2.1 reshape.329
  953.8 2.7 slice.208
  957.6 2.4 copy.152
  960.5 2.3 fusion.15
  966.1 196.4 %shard_map.360 = (f32[48,6448]{1,0:T(8,128)}, f32[96,1536]{1,0:T(8,128)}, f32[24,128]{1,0:T(8,128)}, bf16[2,384,1024]{2,1,0:T(8,128)(2,1)}, bf16[2,512,384]{2,1,0:T(8,128)(2,1)}) custom-call(bf16[2,2,2,4,48,6448]{5,4,3,2,1,0:T(8,128)(2,1)} %bitcast.135, bf16[2,2,2,4,96,1536]{5,4,3,2,1,0:T(8,128)(2,1)} %bitcast.127, f32[2,2,2,4,24,128]{5,4,3,2,1,0:T(8,128)} %bitcast.147, ...), custom_call_target="tpu_custom_call" | custom-call | flops 1024 | bytes 1024 | tf_op jit(solution)/shard_map/pallas_call | solution.py:1240
  1169.1 1.7 fusion.11
  1170.8 3.2 copy.161
  1174.7 4.7 fusion.5
  1179.3 2.4 copy.160
  1184.7 1.9 pad_maximum_fusion.2
  1189.2 2.0 pad_maximum_fusion.1
  1191.2 2.0 pad_maximum_fusion
  (294 shorter events, 73.5 us)
Async XLA Ops:
  7.2 591.5 %all-gather.4.cloned.1.call-start = ((), (), s32[]{:S(2)}) async-start(), calls=%async_computation.1 | async-start | bytes 6488064 | tf_op jit(solution)/shard_map/all_gather | solution.py:1718
  13.1 190.3 %copy-start.42 = (bf16[48,1024]{1,0:T(8,128)(2,1)S(1)}, bf16[48,1024]{1,0:T(8,128)(2,1)}, u32[]{:S(2)}) copy-start(bf16[48,1024]{1,0:T(8,128)(2,1)} %param.37) | copy-start | bytes 294916
  13.1 190.3 %copy-start.43 = (bf16[48,1024]{1,0:T(8,128)(2,1)S(1)}, bf16[48,1024]{1,0:T(8,128)(2,1)}, u32[]{:S(2)}) copy-start(bf16[48,1024]{1,0:T(8,128)(2,1)} %param.36) | copy-start | bytes 294916
  13.1 191.1 %copy-start.40 = (bf16[32,1536]{1,0:T(8,128)(2,1)S(1)}, bf16[32,1536]{1,0:T(8,128)(2,1)}, u32[]{:S(2)}) copy-start(bf16[32,1536]{1,0:T(8,128)(2,1)} %param.38) | copy-start | bytes 294916
  13.1 191.8 %copy-start.55 = (s32[1,1024]{1,0:T(1,128)S(1)}, s32[1,1024]{1,0:T(1,128)}, u32[]{:S(2)}) copy-start(s32[1,1024]{1,0:T(1,128)} %param.22) | copy-start | bytes 12292
  13.1 192.6 %copy-start.25 = (bf16[1,256,1536]{2,1,0:T(8,128)(2,1)S(1)}, bf16[1,256,1536]{2,1,0:T(8,128)(2,1)}, u32[]{:S(2)}) copy-start(bf16[1,256,1536]{2,1,0:T(8,128)(2,1)} %param.21) | copy-start | bytes 2359300
  201.4 4.6 copy-start.24
  204.1 400.6 %all-gather.6.cloned.1.call-start = ((), (), s32[]{:S(2)}) async-start(), calls=%async_computation.3 | async-start | bytes 3244032 | tf_op jit(solution)/shard_map/all_gather | solution.py:1721
  204.8 699.8 %reduce-scatter.2.cloned.1.call-start = ((), (), s32[]{:S(2)}) async-start(), calls=%async_computation.2 | async-start | bytes 14155776 | tf_op jit(solution)/shard_map/reduce_scatter | solution.py:1847
  204.9 26.8 %copy-start.64 = (s32[256]{0:T(256)}, s32[256]{0:T(256)S(1)}, u32[]{:S(2)}) copy-start(s32[256]{0:T(256)S(1)} %iota_add_fusion) | copy-start | bytes 3076
  210.7 16.5 %copy-start.50 = (f32[384]{0:T(512)}, f32[384]{0:T(512)S(1)}, u32[]{:S(2)}) copy-start(f32[384]{0:T(512)S(1)} %add_rsqrt_fusion) | copy-start | bytes 4612
  212.5 18.6 %copy-start.57 = (f32[48]{0:T(128)S(1)}, f32[48]{0:T(128)}, u32[]{:S(2)}) copy-start(f32[48]{0:T(128)} %param.29) | copy-start | bytes 580
  212.5 18.7 %copy-start.60 = (f32[48]{0:T(128)S(1)}, f32[48]{0:T(128)}, u32[]{:S(2)}) copy-start(f32[48]{0:T(128)} %param.30) | copy-start | bytes 580
  227.2 3.9 copy-start
  231.2 4.6 copy-start.34
  235.7 11.5 copy-start.26
  235.7 13.0 %copy-start.56 = (f32[48]{0:T(128)S(1)}, f32[48]{0:T(128)}, u32[]{:S(2)}) copy-start(f32[48]{0:T(128)} %param.31) | copy-start | bytes 580
  247.2 6.2 copy-start.44
  253.5 34.9 %copy-start.52 = (s32[1,256,6]{1,0,2:T(1,128)S(1)}, s32[1,256,6]{1,0,2:T(1,128)}, u32[]{:S(2)}) copy-start(s32[1,256,6]{1,0,2:T(1,128)} %param.23) | copy-start | bytes 18436
  288.8 9.8 copy-start.9
  598.7 6.0 copy-start.8
  789.3 5.8 copy-start.48
  791.5 3.6 copy-start.16
  791.5 3.6 copy-start.23
  791.5 3.9 copy-start.31
  791.5 4.0 copy-start.33
  795.5 7.3 copy-start.5
  795.5 7.3 copy-start.10
  795.5 10.5 slice-start
  795.5 10.6 slice-start.1
  802.8 3.8 slice-start.2
  806.0 9.2 copy-start.1
  860.3 18.7 %copy-start.37 = (f32[256,256]{1,0:T(8,128)S(1)}, f32[256,256]{1,0:T(8,128)}, u32[]{:S(2)}) copy-start(f32[256,256]{1,0:T(8,128)} %get-tuple-element.101) | copy-start | bytes 786436
  883.9 3.4 copy-start.58
  883.9 3.4 copy-start.61
  884.0 4.7 copy-start.39
  884.0 5.5 copy-start.36
  890.3 3.6 copy-start.15
  893.8 5.7 copy-start.2
  893.8 5.7 copy-start.12
  948.6 11.6 collective-permute-start
  966.1 203.0 %copy-start.49 = (f32[256]{0:T(256)S(1)}, f32[256]{0:T(256)}, u32[]{:S(2)}) copy-start(f32[256]{0:T(256)} %copy-done.48) | copy-start | bytes 3076
  966.1 203.0 %copy-start.3 = (f32[248,1536]{0,1:T(8,128)S(1)}, f32[248,1536]{0,1:T(8,128)}, u32[]{:S(2)}) copy-start(f32[248,1536]{0,1:T(8,128)} %slice.208) | copy-start | bytes 4571140
  1170.8 3.8 copy-start.6
  1170.8 3.8 copy-start.22
  1174.6 8.5 copy-start.28
  1179.3 3.8 copy-start.18
  1184.7 3.5 copy-start.19
  (28 other events, 71.6 us)
Sparse Core Ops, SparseCore 0:
  204.2 74.8 all-gather.3
  282.6 75.5 all-gather.5
  787.2 91.7 reduce-scatter.1

commit v4 on v3

--- a/solution.py
+++ b/solution.py
@@ -1475,9 +1475,10 @@
     return lax.ppermute(value, "ctx", [(source, source ^ bits) for source in range(count)])
 
 
-def other_strip(start):
+def half_strip(other, start):
     def at(z):
-        first = EXP_DEV // 2 * (1 - lax.div(z, 2))
+        own = lax.div(z, 2)
+        first = EXP_DEV // 2 * (1 - own if other else own)
         return (pl.ds(first, EXP_DEV // 2), pl.ds(start, STRIP))
 
     return at
@@ -1524,8 +1525,8 @@
     return lax.dynamic_slice_in_dim(whole, flipped(lax.axis_index("ctx"), bits) * width, width, axis)
 
 
-def expert_owners(near, far, late):
-    far = far.astype(jnp.float32) + late
+def expert_owners(near, far):
+    far = far.astype(jnp.float32)
     low = lax.div(lax.axis_index("ctx"), 2) == 0
     return jnp.concatenate([jnp.where(low, near, far), jnp.where(low, far, near)], axis=0)
 
@@ -1536,7 +1537,7 @@
 def experts_kernel(
     rank_ref, gate_ref, rows_ref, grads_ref, first_ref, down_ref,
     routed_ref, back_ref, dgate_ref, grad_first_ref, grad_down_ref,
-    x_s, g_s, sum_first_s, sum_down_s, ready_s, sem,
+    x_s, g_s, sum_first_s, sum_down_s, ready_s, pick_s, routed_s, back_s, sem,
 ):
     tile, expert = pl.program_id(0), pl.program_id(1)
     last = pl.num_programs(0) - 1
@@ -1583,22 +1584,19 @@
     sum_down_s[expert] += mul_tn(act, grad_out)
     for at in range(TILE):
         rows = slice(at * slots, (at + 1) * slots)
-        picker = half(chosen[at].astype(jnp.float32))
-        routed_part, back_part = half(mul_tn(picker, routed[rows])), half(mul_tn(picker, back[rows]))
-
-        @pl.when(expert == 0)
-        def _():
-            routed_ref[at] = routed_part
-            back_ref[at] = back_part
-
-        @pl.when(expert > 0)
-        def _():
-            routed_ref[at] = routed_ref[at] + routed_part
-            back_ref[at] = back_ref[at] + back_part
-
+        some = pl.ds(pl.multiple_of(expert * slots, slots), slots)
+        pick_s[at, some, :] = half(chosen[at].astype(jnp.float32))
+        routed_s[at, some, :] = routed[rows]
+        back_s[at, some, :] = back[rows]
         dgate_ref[at, pl.ds(expert, 1), :] = jnp.sum(
             jnp.where(chosen[at], dgate[rows], 0.0), axis=0, keepdims=True
         )
+
+    @pl.when(expert == pl.num_programs(1) - 1)
+    def _():
+        for at in range(TILE):
+            routed_ref[at] = half(mul_tn(pick_s[at], routed_s[at]))
+            back_ref[at] = half(mul_tn(pick_s[at], back_s[at]))
 
     @pl.when(tile == last)
     def _():
@@ -1648,6 +1646,9 @@
             pltpu.VMEM((held, features, 2 * hidden), jnp.float32),
             pltpu.VMEM((held, hidden, features), jnp.float32),
             pltpu.VMEM((256, features), jnp.bfloat16),
+            pltpu.VMEM((TILE, held * slots, tokens), jnp.bfloat16),
+            pltpu.VMEM((TILE, held * slots, features), jnp.bfloat16),
+            pltpu.VMEM((TILE, held * slots, features), jnp.bfloat16),
             pltpu.SemaphoreType.DMA,
         ],
         cost_estimate=BRIEF,
@@ -1707,11 +1708,11 @@
         more=[e_gate, e_up, e_down],
         more_shapes=[(held, d_model, 2 * hidden), (held, hidden, d_model)],
         moves=[
-            (part, 0, other_strip(start), columns(quarter(1, width, 0, start), part * hidden, hidden), 2)
+            (part, 0, half_strip(True, start), columns(quarter(1, width, 0, start), part * hidden, hidden), 2)
             for start in first_strips
             for part in range(2)
         ]
-        + [(2, 1, other_strip(start), quarter(2, width, 0, start), 2) for start in down_strips],
+        + [(2, 1, half_strip(True, start), quarter(2, width, 0, start), 2) for start in down_strips],
     )
     pair_at = lax.div(ctx_place, 2)
     sent = nothing(w_in_all)
@@ -1790,8 +1791,8 @@
         ahead=4,
         more=[expert_first, expert_down],
         moves=[
-            (part, part, quarter(axis, width, 2 * far, start), quarter(axis, width, 2 * far, start), 1)
-            for far in (0, 1)
+            (part, part, quarter(axis, width, bits, start), quarter(axis, width, bits, start), 1)
+            for bits in (0, 2)
             for part, axis, starts in ((0, 1, first_strips), (1, 2, down_strips))
             for start in starts
         ],
@@ -1835,11 +1836,10 @@
         4,
         lines=[(2,), (2,), (1, 2, 3), (1, 2, 3)],
         more=[grad_first, grad_down, routed_rows],
-        more_shapes=[(2, held, width, 2 * hidden), (2, held, hidden, width), routed_rows.shape],
+        more_shapes=[(held, width, 2 * hidden), (held, hidden, width), routed_rows.shape],
         same=(2,),
         moves=[
-            (part, part, quarter(axis, width, 2 * far + 1, start), strip(start, far), 1)
-            for far in (1, 0)
+            (part, part, quarter(axis, width, 3, start), strip(start), 1)
             for part, axis, starts in ((0, 1, first_strips), (1, 2, down_strips))
             for start in starts
         ],
@@ -1850,11 +1850,6 @@
     routed = with_layout_constraint(routed, Layout(major_to_minor=(0, 1, 2)))
     routed_own = lax.dynamic_index_in_dim(routed, pair_at, 0, keepdims=False)
     routed_far = lax.dynamic_index_in_dim(routed, 1 - pair_at, 0, keepdims=False)
-    near_first, near_down = (
-        own_quarter(whole, axis, 0).astype(f32) + beside[0].astype(f32)
-        for whole, beside, axis in ((grad_first, beside_first, 1), (grad_down, beside_down, 2))
-    )
-
     grad_top = out_grad[0].astype(f32)
     grad_mid_shared = times_back(grad_shared, shared_weight)
     grad_gates = back_side[:, :expert_count] + back_side[:, expert_count : 2 * expert_count]
@@ -1884,7 +1879,7 @@
         grad_state_local, passed, pre, grad_y, bc_pre, dt_pos, cumul, cumul_col, flags, seg_col, 8
     )
     far_first, far_down = (
-        half(own_quarter(whole, axis, 2).astype(f32) + beside[1].astype(f32))
+        half(own_quarter(whole, axis, 2).astype(f32) + beside.astype(f32))
         for whole, beside, axis in ((grad_first, beside_first, 1), (grad_down, beside_down, 2))
     )
     grad_x, grad_taps_x, grad_dt, grad_cum_join, grad_last, grad_bc_join = mixer_back_join(
@@ -1938,25 +1933,32 @@
         axis=1,
     )
     small_grads = jnp.pad(small_grads, ((0, 0), (0, 3072 - small_grads.shape[1])))
-    sum_in, sum_out, sum_small, far_first, far_down = pallas_reduce(
+    sum_in, sum_out, sum_small, far_first, far_down, beside_first, beside_down = pallas_reduce(
         [owned(grad_w_in), owned(grad_w_out), small_grads.reshape(devices, 24, 128)],
         [(16, 1664), (16, 1536), (24, 128)],
         6,
         ahead=3,
-        more=[far_first, far_down],
-        more_shapes=[far_first.shape, far_down.shape],
+        more=[far_first, far_down, grad_first, grad_down],
+        more_shapes=[far_first.shape, far_down.shape] * 2,
         moves=[
-            (part, part, strip(start), strip(start), 2)
-            for part, starts in ((0, first_strips), (1, down_strips))
+            move
+            for part, axis, starts in ((0, 1, first_strips), (1, 2, down_strips))
             for start in starts
+            for move in (
+                (part, part, strip(start), strip(start), 2),
+                (2 + part, 2 + part, quarter(axis, width, 1, start), strip(start), 1),
+            )
         ],
     )
-    summed = nothing(sum_small)
-    layer_out = (resid_mid + shared_out + routed_own.astype(f32) + routed_far.astype(f32) + summed).astype(bf16)[None]
+    near_first, near_down = (
+        own_quarter(whole, axis, 0).astype(f32) + beside.astype(f32)
+        for whole, beside, axis in ((grad_first, beside_first, 1), (grad_down, beside_down, 2))
+    )
+    layer_out = (resid_mid + shared_out + routed_own.astype(f32) + routed_far.astype(f32)).astype(bf16)[None]
     sum_sgate, sum_sup = jnp.split(sum_shared, 2, axis=1)
-    grad_e_gate = expert_owners(near_first[..., :hidden], far_first[..., :hidden], summed)
-    grad_e_up = expert_owners(near_first[..., hidden:], far_first[..., hidden:], summed)
-    grad_e_down = expert_owners(near_down, far_down, summed)
+    grad_e_gate = expert_owners(near_first[..., :hidden], far_first[..., :hidden])
+    grad_e_up = expert_owners(near_first[..., hidden:], far_first[..., hidden:])
+    grad_e_down = expert_owners(near_down, far_down)
     sum_small = sum_small.reshape(-1)
     taken, mine = 0, []
     for part in small_parts:

time: 1210 us -> 1150 us (0.950)
  Pallas kernels: 987 us -> 932 us
    pallas_call x2, Pallas kernels: 368 us -> 329 us  [pallas_reduce(): pl.pallas_call(partial(reduce_kernel, pieces, ahead, count, lines, moves,...]
    pallas_call x1, Pallas kernels: 114 us -> 99.2 us  [routed_experts(): pl.pallas_call(experts_kernel, grid=(blocks // TILE, held), in_specs=[tab...]
    unnamed x159 -> x147, local copies, waits for them, and re-layouts: 24.7 us -> 23.2 us
  transfers between devices with their start and end apart: 4 -> 4, of which waited for: 0 -> 0; matrix products, arithmetic and copies ran while one was open for 10% -> 11% of each run, Pallas kernels for 33% -> 33%
where the time goes in v4:
time: 1150 us; the launch traced here: 1140 us
  Pallas kernels  932 us (81%)
  local copies, waits for them, and re-layouts  79.4 us (7%)
  matrix products  68.2 us (6%)
  other arithmetic  42.2 us (4%)
  between operations  17.5 us (2%)
    pallas_call x2, Pallas kernels, pallas_gather(): pl.pallas_call(partial(gather_kernel, pieces, ahead, count, line, moves,...  355 us
    pallas_call x2, Pallas kernels, pallas_reduce(): pl.pallas_call(partial(reduce_kernel, pieces, ahead, count, lines, moves,...  329 us
    pallas_call x8, Pallas kernels, call_steps(): pl.pallas_call(kernel, grid=(steps,), in_specs=in_specs, out_specs=out_sp...  149 us
    pallas_call x1, Pallas kernels, routed_experts(): pl.pallas_call(experts_kernel, grid=(blocks // TILE, held), in_specs=[tab...  99.2 us
    unnamed x147, local copies, waits for them, and re-layouts  23.2 us
  transfers between devices with their start and end apart: 4, of which 0 were waited for; matrix products, arithmetic and copies ran while one was open for 11% of the time, Pallas kernels for 33%

profile of v4, /device:TPU:0, one launch (start us, length us, event | category | flops | bytes accessed | tf_op | source)
XLA Modules:
  0.0 1140.6 jit_solution(5994958872770219199)
XLA Ops:
  8.9 2.8 concatenate.72
  13.1 188.3 %shard_map.348 = (bf16[2,2,2,4,48,6448]{5,4,3,2,1,0:T(8,128)(2,1)}, bf16[2,2,2,4,96,1536]{5,4,3,2,1,0:T(8,128)(2,1)}, bf16[2,2,2,4,128,128]{5,4,3,2,1,0:T(8,128)...) custom-call(bf16[48,6448]{1,0:T(8,128)(2,1)} %refs_0_.1, bf16[96,1536]{1,0:T(8,128)(2,1)} %refs_1_.1, ...), custom_call_target="tpu_custom_call" | custom-call | flops 1024 | bytes 1024 | tf_op jit(solution)/shard_map/pallas_call | solution.py:1066
  210.7 1.7 copy.131.taps_ref
  212.5 14.9 %fusion.62.x_ref.z_ref = f32[6448,384]{1,0:T(8,128)S(1)} fusion(bf16[1536,6448]{1,0:T(8,128)(2,1)} %bitcast.167, f32[1536]{0:T(1024)S(1)} %reshape.322, f32[384]{0:T(512)S(1)} %add_rsqrt_fusion, bf16[8,1536]{0,1:T(8,128)(2,1)S(1)} %select_bitcast_fusion, bf16[256,1536]{0,1:T(8,128)(2,1)S(1)} %bitcast.117, bf16[384]{0:T(512)(128)(2,1)S(1)} %pad.64.clone), kind=kOutput, calls=%fused_computation.176 | convolution fusion | flops 7611678720 | bytes 30531840 | tf_op jit(solution)/shard_map/dot_general | solution.py:1752
  227.4 3.9 copy-done
  233.6 2.4 shard_map.349.bc_ref.pre_ref
  235.9 10.0 shard_map.350
  250.4 1.6 broadcast_in_dim.121.gain_ref
  252.0 1.6 broadcast_in_dim.118.passed_ref
  253.6 34.5 %shard_map.351 = (f32[3072,256]{1,0:T(8,128)}, bf16[3072,128]{1,0:T(8,128)(2,1)}, bf16[3072,256]{1,0:T(8,128)(2,1)}, f32[8,256]{1,0:T(8,128)}) custom-call(bf16[3072,128]{1,0:T(8,128)(2,1)} %get-tuple-element.75.local_ref, f32[3072,8]{1,0:T(8,128)} %broadcast_in_dim.118.passed_ref, f32[3072,256]{1,0:T(8,128)} %get-tuple-element.76.pre_ref, ...), custom_call_target="tpu_custom_call" | custom-call | flops 1024 | bytes 1024 | tf_op jit(solution)/shard_map/pallas_call | solution.py:569
  288.8 7.4 multiply_reduce_fusion.4
  299.4 2.3 dynamic-slice_dynamic-update-slice_fusion.refs_4_
  306.1 166.3 %shard_map.352 = (bf16[2,2,2,2,256,1536]{5,4,3,2,1,0:T(8,128)(2,1)}, bf16[2,2,2,2,256,1536]{5,4,3,2,1,0:T(8,128)(2,1)}, bf16[2,2,2,2,256,128]{5,4,3,2,1,0:T(8,12...) custom-call(bf16[256,1536]{1,0:T(8,128)(2,1)} %copy.140.refs_0_, ...), custom_call_target="tpu_custom_call", output_to_operand_aliasing={{3}: (3, {}), {4}: (4, {})} | custom-call | flops 1024 | bytes 1024 | tf_op jit(solution)/shard_map/pallas_call | solution.py:1066
  475.3 99.2 %shard_map.353 = (bf16[16,256,1536]{2,1,0:T(8,128)(2,1)}, bf16[16,256,1536]{2,1,0:T(8,128)(2,1)}, f32[16,2,256]{2,1,0:T(2,128)}, bf16[2,1536,1024]{2,1,0:T(8,128)(2,1)}, bf16[2,512,1536]{2,1,0:T(8,128)(2,1)}) custom-call(f32[16,2,256]{2,1,0:T(2,128)} %convert_bitcast_fusion.rank_ref, f32[16,2,256]{2,1,0:T(2,128)} %add_bitcast_fusion.gate_ref, ...), custom_call_target="tpu_custom_call" | custom-call | flops 1024 | bytes 1024 | tf_op jit(solution)/shard_map/pallas_call | solution.py:1624
  577.4 1.9 copy.144
  579.4 2.7 subtract_convert_fusion
  582.0 1.6 maximum_maximum_fusion.refs_1_
  583.6 6.0 fusion.16
  589.6 3.7 multiply_convert_fusion.2
  593.4 2.7 convolution_convert_fusion.2
  596.1 4.4 convolution_convert_fusion.1
  600.6 135.3 %shard_map.354 = (f32[256,1536]{1,0:T(8,128)}, f32[256,128]{1,0:T(8,128)}, f32[32,1536]{1,0:T(8,128)}, f32[48,2048]{1,0:T(8,128)}, bf16[2,384,1024]{2,1,0:T(8,12...) custom-call(bf16[2,2,2,2,256,1536]{5,4,3,2,1,0:T(8,128)(2,1)} %bitcast.126,, ...), custom_call_target="tpu_custom_call", output_to_operand_aliasing={{6}: (6, {})} | custom-call | flops 1024 | bytes 1024 | tf_op jit(solution)/shard_map/pallas_call | solution.py:1240
  740.2 3.3 copy.147
  743.9 7.7 convolution_add_fusion.2
  755.7 1.7 copy-done.57
  757.4 6.9 multiply_reduce_fusion
  765.6 8.5 shard_map.355
  774.2 34.4 %shard_map.356 = (f32[3072,256]{1,0:T(8,128)}, bf16[3072,128]{1,0:T(8,128)(2,1)}, f32[48,256]{1,0:T(8,128)}, f32[48,256]{1,0:T(8,128)}, f32[256,256]{1,0:T(8,128)}) custom-call(bf16[3072,128]{1,0:T(8,128)(2,1)} %get-tuple-element.97.local_ref, f32[3072,8]{1,0:T(8,128)} %broadcast_in_dim.118.passed_ref, f32[3072,256]{1,0:T(8,128)} %get-tuple-element.76.pre_ref, ...), custom_call_target="tpu_custom_call" | custom-call | flops 35000000512 | bytes 1024 | tf_op jit(solution)/shard_map/pallas_call | solution.py:569
  808.6 18.7 %shard_map.357 = (bf16[3072,384]{1,0:T(8,128)(2,1)}, f32[3072,8]{1,0:T(8,128)}, f32[48,256]{1,0:T(8,128)}, f32[48,256]{1,0:T(8,128)}, f32[48,128]{1,0:T(8,128)}, /*index=5*/f32[256,256]{1,0:T(8,128)}) custom-call(f32[3072,256]{1,0:T(8,128)} %get-tuple-element.99.grad_in_ref, f32[3072,256]{1,0:T(8,128)} %get-tuple-element.98.grad_y_ref, ...), custom_call_target="tpu_custom_call" | custom-call | flops 19000000512 | bytes 1024 | tf_op jit(solution)/shard_map/pallas_call | solution.py:569
  827.3 1.7 add.289.grad_ref
  829.0 3.2 shard_map.358
  833.4 2.1 reshape.318
  836.5 1.9 copy.156
  842.6 2.5 add_convert_fusion.1.refs_4_
  845.0 3.4 add_convert_fusion.refs_3_
  848.4 5.0 convolution_convert_fusion
  853.5 2.4 constant_dynamic-slice_fusion
  857.0 37.5 %shard_map.359 = (bf16[1536,6448]{1,0:T(8,128)(2,1)}, f32[1536,384]{1,0:T(8,128)}, bf16[256,1536]{1,0:T(8,128)(2,1)}) custom-call(bf16[1536,384]{1,0:T(8,128)(2,1)} %fusion.61.normed_ref, bf16[1536,6448]{1,0:T(8,128)(2,1)} %bitcast.168, bf16[3072,256]{1,0:T(8,128)(2,1)} %get-tuple-element.96.grad_z_ref, bf16[3072,384]{1,0:T(8,128)(2,1)} %get-tuple-element.102.grad_x_ref, ...), custom_call_target="tpu_custom_call" | custom-call | flops 27000000512 | bytes 1024 | tf_op jit(solution)/shard_map/pallas_call | solution.py:569
  894.5 2.3 copy.152
  896.8 3.1 fusion.66
  902.6 4.6 fusion.3
  915.4 193.4 %shard_map.360 = (f32[48,6448]{1,0:T(8,128)}, f32[96,1536]{1,0:T(8,128)}, f32[24,128]{1,0:T(8,128)}, bf16[2,384,1024]{2,1,0:T(8,128)(2,1)}, bf16[2,512,384]{2,1,...) custom-call(bf16[2,2,2,4,48,6448]{5,4,3,2,1,0:T(8,128)(2,1)} %bitcast.121, ...), custom_call_target="tpu_custom_call" | custom-call | flops 1024 | bytes 1024 | tf_op jit(solution)/shard_map/pallas_call | solution.py:1240
  1114.2 1.7 fusion.9
  1115.9 3.1 copy.161
  1120.5 2.2 convert_add_fusion
  1124.2 1.9 pad_maximum_fusion.2
  1127.0 2.0 pad_maximum_fusion.1
  1129.0 2.0 pad_maximum_fusion
  (282 shorter events, 70.9 us)
Async XLA Ops:
  7.2 576.5 %all-gather.4.cloned.1.call-start = ((), (), s32[]{:S(2)}) async-start(), calls=%async_computation.1 | async-start | bytes 6488064 | tf_op jit(solution)/shard_map/all_gather | solution.py:1719
  13.1 190.3 %copy-start.40 = (bf16[48,1024]{1,0:T(8,128)(2,1)S(1)}, bf16[48,1024]{1,0:T(8,128)(2,1)}, u32[]{:S(2)}) copy-start(bf16[48,1024]{1,0:T(8,128)(2,1)} %param.37) | copy-start | bytes 294916
  13.1 190.3 %copy-start.41 = (bf16[48,1024]{1,0:T(8,128)(2,1)S(1)}, bf16[48,1024]{1,0:T(8,128)(2,1)}, u32[]{:S(2)}) copy-start(bf16[48,1024]{1,0:T(8,128)(2,1)} %param.36) | copy-start | bytes 294916
  13.1 191.1 %copy-start.38 = (bf16[32,1536]{1,0:T(8,128)(2,1)S(1)}, bf16[32,1536]{1,0:T(8,128)(2,1)}, u32[]{:S(2)}) copy-start(bf16[32,1536]{1,0:T(8,128)(2,1)} %param.38) | copy-start | bytes 294916
  13.1 191.8 %copy-start.53 = (s32[1,1024]{1,0:T(1,128)S(1)}, s32[1,1024]{1,0:T(1,128)}, u32[]{:S(2)}) copy-start(s32[1,1024]{1,0:T(1,128)} %param.22) | copy-start | bytes 12292
  13.1 192.6 %copy-start.23 = (bf16[1,256,1536]{2,1,0:T(8,128)(2,1)S(1)}, bf16[1,256,1536]{2,1,0:T(8,128)(2,1)}, u32[]{:S(2)}) copy-start(bf16[1,256,1536]{2,1,0:T(8,128)(2,1)} %param.21) | copy-start | bytes 2359300
  201.4 4.6 copy-start.22
  204.1 385.6 %all-gather.6.cloned.1.call-start = ((), (), s32[]{:S(2)}) async-start(), calls=%async_computation.3 | async-start | bytes 3244032 | tf_op jit(solution)/shard_map/all_gather | solution.py:1722
  204.8 648.6 %reduce-scatter.2.cloned.1.call-start = ((), (), s32[]{:S(2)}) async-start(), calls=%async_computation.2 | async-start | bytes 14155776 | tf_op jit(solution)/shard_map/reduce_scatter | solution.py:1847
  210.7 16.7 %copy-start.48 = (f32[384]{0:T(512)}, f32[384]{0:T(512)S(1)}, u32[]{:S(2)}) copy-start(f32[384]{0:T(512)S(1)} %add_rsqrt_fusion) | copy-start | bytes 4612
  212.5 18.8 %copy-start.55 = (f32[48]{0:T(128)S(1)}, f32[48]{0:T(128)}, u32[]{:S(2)}) copy-start(f32[48]{0:T(128)} %param.29) | copy-start | bytes 580
  212.5 18.9 %copy-start.58 = (f32[48]{0:T(128)S(1)}, f32[48]{0:T(128)}, u32[]{:S(2)}) copy-start(f32[48]{0:T(128)} %param.30) | copy-start | bytes 580
  227.4 3.9 copy-start
  231.4 4.5 copy-start.31
  235.9 11.5 %copy-start.24 = (f32[48,256]{1,0:T(8,128)S(1)}, f32[48,256]{1,0:T(8,128)}, u32[]{:S(2)}) copy-start(f32[48,256]{1,0:T(8,128)} %fusion.24.cum_ref) | copy-start | bytes 147460
  235.9 13.0 %copy-start.54 = (f32[48]{0:T(128)S(1)}, f32[48]{0:T(128)}, u32[]{:S(2)}) copy-start(f32[48]{0:T(128)} %param.31) | copy-start | bytes 580
  247.4 6.2 copy-start.42
  253.6 34.7 %copy-start.50 = (s32[1,256,6]{1,0,2:T(1,128)S(1)}, s32[1,256,6]{1,0,2:T(1,128)}, u32[]{:S(2)}) copy-start(s32[1,256,6]{1,0,2:T(1,128)} %param.23) | copy-start | bytes 18436
  288.8 10.1 copy-start.8
  583.6 6.0 copy-start.6
  738.1 5.4 copy-start.46
  740.2 3.3 copy-start.21
  743.8 7.8 copy-start.2
  743.8 7.8 copy-start.9
  743.9 11.2 slice-start
  743.9 11.3 slice-start.1
  751.6 4.1 slice-start.2
  755.0 9.2 copy-start.3
  808.6 18.7 %copy-start.34 = (f32[256,256]{1,0:T(8,128)S(1)}, f32[256,256]{1,0:T(8,128)}, u32[]{:S(2)}) copy-start(f32[256,256]{1,0:T(8,128)} %get-tuple-element.103) | copy-start | bytes 786436
  832.2 4.1 copy-start.44
  832.2 4.2 copy-start.37
  833.4 6.0 copy-start.25
  833.4 6.0 copy-start.39
  835.5 4.1 copy-start.32
  835.5 4.1 copy-start.56
  835.5 4.1 copy-start.59
  835.5 4.1 copy-start.61
  835.6 4.1 copy-start.62
  836.4 4.6 copy-start.36
  836.5 5.3 copy-start.33
  845.0 3.4 copy-start.4
  845.0 3.4 copy-start.13
  896.8 5.8 copy-start.12
  901.2 6.0 copy-start.7
  901.2 9.7 collective-permute-start
  915.4 198.8 %copy-start.47 = (f32[256]{0:T(256)S(1)}, f32[256]{0:T(256)}, u32[]{:S(2)}) copy-start(f32[256]{0:T(256)} %copy-done.46) | copy-start | bytes 3076
  915.4 198.9 %copy-start.5 = (f32[256,1536]{0,1:T(8,128)S(1)}, f32[256,1536]{0,1:T(8,128)}, u32[]{:S(2)}) copy-start(f32[256,1536]{0,1:T(8,128)} %copy-done.3) | copy-start | bytes 4718596
  1115.9 4.6 copy-start.18
  (22 other events, 49.1 us)
Sparse Core Ops, SparseCore 0:
  204.2 74.8 all-gather.3
  282.5 76.0 all-gather.5
  736.0 92.4 reduce-scatter.1

commit v5 on v4

--- a/solution.py
+++ b/solution.py
@@ -1536,26 +1536,34 @@
 
 def experts_kernel(
     rank_ref, gate_ref, rows_ref, grads_ref, first_ref, down_ref,
-    routed_ref, back_ref, dgate_ref, grad_first_ref, grad_down_ref,
-    x_s, g_s, sum_first_s, sum_down_s, ready_s, pick_s, routed_s, back_s, sem,
+    routed_ref, back_ref, side_ref, grad_first_ref, grad_down_ref,
+    x_s, g_s, sum_first_s, sum_down_s, ready_s, pick_s, routed_s, back_s, side_s, sem,
 ):
     tile, expert = pl.program_id(0), pl.program_id(1)
     last = pl.num_programs(0) - 1
     hidden = down_ref.shape[1]
-    slots = x_s.shape[0] // TILE
+    held, slots = x_s.shape[0], x_s.shape[1] // TILE
     tokens = rank_ref.shape[2]
-    chosen, gates = [], []
+    gates = []
     number = lax.broadcasted_iota(jnp.int32, (slots, tokens), 0).astype(jnp.float32)
+    @pl.when(expert == 0)
+    def _():
+        for at in range(TILE):
+            rows = pl.ds(at * slots, slots)
+            for one in range(held):
+                own = rank_ref[at, one : one + 1, :] == number
+                pick_s[at, one * slots : (one + 1) * slots, :] = half(own.astype(jnp.float32))
+            x_rows = half(mul_nn(pick_s[at], rows_ref[at]))
+            g_rows = half(mul_nn(pick_s[at], grads_ref[at]))
+            for one in range(held):
+                x_s[one, rows, :] = x_rows[one * slots : (one + 1) * slots]
+                g_s[one, rows, :] = g_rows[one * slots : (one + 1) * slots]
+
     for at in range(TILE):
-        rows = pl.ds(at * slots, slots)
         own = rank_ref[at, pl.ds(expert, 1), :] == number
-        chosen.append(own)
         gates.append(jnp.sum(jnp.where(own, gate_ref[at, pl.ds(expert, 1), :], 0.0), axis=1, keepdims=True))
-        picker = half(own.astype(jnp.float32))
-        x_s[rows, :] = half(mul_nn(picker, rows_ref[at]))
-        g_s[rows, :] = half(mul_nn(picker, grads_ref[at]))
     gate = jnp.concatenate(gates, axis=0)
-    x, grad = x_s[...], g_s[...].astype(jnp.float32)
+    x, grad = x_s[expert], g_s[expert].astype(jnp.float32)
     both = mul_nn(x, first_ref[0])
     hg, hu = both[:, :hidden], both[:, hidden:]
     squashed = jax.nn.sigmoid(hg)
@@ -1576,20 +1584,23 @@
         sum_first_s[expert] = jnp.zeros(sum_first_s.shape[1:], jnp.float32)
         sum_down_s[expert] = jnp.zeros(sum_down_s.shape[1:], jnp.float32)
 
-    @pl.loop(0, x_s.shape[1] // 256)
+    @pl.loop(0, x_s.shape[2] // 256)
     def _(at):
         some = pl.ds(pl.multiple_of(at * 256, 256), 256)
-        sum_first_s[expert, some, :] += mul_tn(x_s[:, some], grad_both)
+        sum_first_s[expert, some, :] += mul_tn(x_s[expert, :, some], grad_both)
 
     sum_down_s[expert] += mul_tn(act, grad_out)
+    count = EXP_DEV * lax.axis_size("dp")
+    column = lax.axis_index("dp") * EXP_DEV + lax.div(lax.axis_index("ctx"), 2) * held + expert
+    lane = lax.broadcasted_iota(jnp.int32, (slots, side_s.shape[2]), 1)
+    high = half(dgate).astype(jnp.float32)
     for at in range(TILE):
         rows = slice(at * slots, (at + 1) * slots)
         some = pl.ds(pl.multiple_of(expert * slots, slots), slots)
-        pick_s[at, some, :] = half(chosen[at].astype(jnp.float32))
         routed_s[at, some, :] = routed[rows]
         back_s[at, some, :] = back[rows]
-        dgate_ref[at, pl.ds(expert, 1), :] = jnp.sum(
-            jnp.where(chosen[at], dgate[rows], 0.0), axis=0, keepdims=True
+        side_s[at, some, :] = half(
+            jnp.where(lane == column, high[rows], jnp.where(lane == column + count, dgate[rows] - high[rows], 0.0))
         )
 
     @pl.when(expert == pl.num_programs(1) - 1)
@@ -1597,6 +1608,7 @@
         for at in range(TILE):
             routed_ref[at] = half(mul_tn(pick_s[at], routed_s[at]))
             back_ref[at] = half(mul_tn(pick_s[at], back_s[at]))
+            side_ref[at] = half(mul_tn(pick_s[at], side_s[at]))
 
     @pl.when(tile == last)
     def _():
@@ -1632,23 +1644,24 @@
             pl.BlockSpec((1, features, 2 * hidden), lambda t, e: (e, 0, 0)),
             pl.BlockSpec((1, hidden, features), lambda t, e: (e, 0, 0)),
         ],
-        out_specs=[wide, wide, table, anywhere, anywhere],
+        out_specs=[wide, wide, pl.BlockSpec((TILE, tokens, 128), some), anywhere, anywhere],
         out_shape=[
             bf16_out(blocks, tokens, features),
             bf16_out(blocks, tokens, features),
-            f32_out(blocks, held, tokens),
+            bf16_out(blocks, tokens, 128),
             bf16_out(held, features, 2 * hidden),
             bf16_out(held, hidden, features),
         ],
         scratch_shapes=[
-            pltpu.VMEM((TILE * slots, features), jnp.bfloat16),
-            pltpu.VMEM((TILE * slots, features), jnp.bfloat16),
+            pltpu.VMEM((held, TILE * slots, features), jnp.bfloat16),
+            pltpu.VMEM((held, TILE * slots, features), jnp.bfloat16),
             pltpu.VMEM((held, features, 2 * hidden), jnp.float32),
             pltpu.VMEM((held, hidden, features), jnp.float32),
             pltpu.VMEM((256, features), jnp.bfloat16),
             pltpu.VMEM((TILE, held * slots, tokens), jnp.bfloat16),
             pltpu.VMEM((TILE, held * slots, features), jnp.bfloat16),
             pltpu.VMEM((TILE, held * slots, features), jnp.bfloat16),
+            pltpu.VMEM((TILE, held * slots, 128), jnp.bfloat16),
             pltpu.SemaphoreType.DMA,
         ],
         cost_estimate=BRIEF,
@@ -1812,16 +1825,8 @@
     ).astype(f32)
     my_rank = mine_of(side_all, first_expert + 2 * expert_count).astype(f32)
     my_gate, my_rank = jnp.swapaxes(my_gate, 1, 2), jnp.swapaxes(my_rank, 1, 2)
-    routed_rows, grad_slot_rows, token_dgate, grad_first, grad_down = routed_experts(
+    routed_rows, grad_slot_rows, back_side, grad_first, grad_down = routed_experts(
         my_rank, my_gate, token_rows, grad_rows, expert_first, expert_down, slots
-    )
-    experts = jnp.arange(held, dtype=jnp.int32)[:, None] + first_expert
-    dgate_table = jnp.sum(
-        token_dgate[..., None] * (jnp.arange(expert_count) == experts).astype(f32)[:, None, :], axis=1
-    )
-    dgate_high, dgate_low = two_parts(dgate_table)
-    back_side = jnp.concatenate(
-        [dgate_high, dgate_low, jnp.zeros((blocks, row_count, 128 - 2 * expert_count), bf16)], axis=-1
     )
     grad_shared_out = out_grad[0]
     grad_w_sdown = times_rows(shared_act, grad_shared_out)

time: 1150 us -> 1130 us (0.983)
    unnamed x147 -> x157, local copies, waits for them, and re-layouts: 23.2 us -> 19.8 us
  transfers between devices with their start and end apart: 4 -> 4, of which waited for: 0 -> 0; matrix products, arithmetic and copies ran while one was open for 11% -> 10% of each run, Pallas kernels for 33% -> 33%
where the time goes in v5:
time: 1130 us; the launch traced here: 1120 us
  Pallas kernels  924 us (82%)
  local copies, waits for them, and re-layouts  72.8 us (6%)
  matrix products  69.5 us (6%)
  other arithmetic  37.7 us (3%)
  between operations  17.7 us (2%)
    pallas_call x2, Pallas kernels, pallas_gather(): pl.pallas_call(partial(gather_kernel, pieces, ahead, count, line, moves,...  354 us
    pallas_call x2, Pallas kernels, pallas_reduce(): pl.pallas_call(partial(reduce_kernel, pieces, ahead, count, lines, moves,...  325 us
    pallas_call x8, Pallas kernels, call_steps(): pl.pallas_call(kernel, grid=(steps,), in_specs=in_specs, out_specs=out_sp...  150 us
    pallas_call x1, Pallas kernels, routed_experts(): pl.pallas_call(experts_kernel, grid=(blocks // TILE, held), in_specs=[tab...  95.4 us
  transfers between devices with their start and end apart: 4, of which 0 were waited for; matrix products, arithmetic and copies ran while one was open for 10% of the time, Pallas kernels for 33%

profile of v5, /device:TPU:0, one launch (start us, length us, event | category | flops | bytes accessed | tf_op | source)
XLA Modules:
  0.0 1123.4 jit_solution(15524937863077141317)
XLA Ops:
  8.9 2.8 concatenate.68
  13.1 188.3 %shard_map.348 = (bf16[2,2,2,4,48,6448]{5,4,3,2,1,0:T(8,128)(2,1)}, bf16[2,2,2,4,96,1536]{5,4,3,2,1,0:T(8,128)(2,1)}, bf16[2,2,2,4,128,128]{5,4,3,2,1,0:T(8,128)...) custom-call(bf16[48,6448]{1,0:T(8,128)(2,1)} %refs_0_.1, bf16[96,1536]{1,0:T(8,128)(2,1)} %refs_1_.1, ...), custom_call_target="tpu_custom_call" | custom-call | flops 1024 | bytes 1024 | tf_op jit(solution)/shard_map/pallas_call | solution.py:1066
  210.6 18.0 %fusion.62.x_ref.z_ref = f32[6448,384]{1,0:T(8,128)} fusion(bf16[1536,6448]{1,0:T(8,128)(2,1)} %bitcast.167, f32[1536]{0:T(1024)S(1)} %reshape.295, f32[384]{0:T(512)S(1)} %add_rsqrt_fusion, bf16[8,1536]{0,1:T(8,128)(2,1)S(1)} %select_bitcast_fusion, bf16[256,1536]{0,1:T(8,128)(2,1)S(1)} %bitcast.117, bf16[384]{0:T(512)(128)(2,1)S(1)} %pad.61.clone), kind=kOutput, calls=%fused_computation.171 | convolution fusion | flops 7611678720 | bytes 30531840 | tf_op jit(solution)/shard_map/dot_general | solution.py:1765
  228.8 1.7 copy.131.taps_ref
  233.6 2.4 shard_map.349.bc_ref.pre_ref
  236.0 10.0 shard_map.350
  250.5 1.6 broadcast_in_dim.115.gain_ref
  252.1 1.6 broadcast_in_dim.112.passed_ref
  253.7 34.5 %shard_map.351 = (f32[3072,256]{1,0:T(8,128)}, bf16[3072,128]{1,0:T(8,128)(2,1)}, bf16[3072,256]{1,0:T(8,128)(2,1)}, f32[8,256]{1,0:T(8,128)}) custom-call(bf16[3072,128]{1,0:T(8,128)(2,1)} %get-tuple-element.75.local_ref, f32[3072,8]{1,0:T(8,128)} %broadcast_in_dim.112.passed_ref, f32[3072,256]{1,0:T(8,128)} %get-tuple-element.76.pre_ref, ...), custom_call_target="tpu_custom_call" | custom-call | flops 1024 | bytes 1024 | tf_op jit(solution)/shard_map/pallas_call | solution.py:569
  288.8 7.0 multiply_reduce_fusion.4
  299.0 2.2 dynamic-slice_dynamic-update-slice_fusion.refs_4_
  302.5 1.4 maximum_dynamic-update-slice_fusion.refs_3_
  305.7 165.7 %shard_map.352 = (bf16[2,2,2,2,256,1536]{5,4,3,2,1,0:T(8,128)(2,1)}, bf16[2,2,2,2,256,1536]{5,4,3,2,1,0:T(8,128)(2,1)}, bf16[2,2,2,2,256,128]{5,4,3,2,1,0:T(8,12...) custom-call(bf16[256,1536]{1,0:T(8,128)(2,1)} %copy.140.refs_0_, ...), custom_call_target="tpu_custom_call", output_to_operand_aliasing={{3}: (3, {}), {4}: (4, {})} | custom-call | flops 1024 | bytes 1024 | tf_op jit(solution)/shard_map/pallas_call | solution.py:1066
  471.4 1.5 copy.143
  474.2 95.4 %shard_map.353 = (bf16[16,256,1536]{2,1,0:T(8,128)(2,1)}, bf16[16,256,1536]{2,1,0:T(8,128)(2,1)}, bf16[16,256,128]{2,1,0:T(8,128)(2,1)}, bf16[2,1536,1024]{2,1,0:T(8,128)(2,1)}, bf16[2,512,1536]{2,1,0:T(8,128)(2,1)}) custom-call(f32[16,2,256]{2,1,0:T(2,128)} %convert_bitcast_fusion.rank_ref, f32[16,2,256]{2,1,0:T(2,128)} %add_bitcast_fusion.gate_ref, ...), custom_call_target="tpu_custom_call" | custom-call | flops 1024 | bytes 1024 | tf_op jit(solution)/shard_map/pallas_call | solution.py:1636
  571.5 6.0 fusion.16
  577.4 3.7 multiply_convert_fusion.2
  581.2 2.7 convolution_convert_fusion.2
  583.9 4.4 convolution_convert_fusion.1
  588.4 134.7 %shard_map.354 = (f32[256,1536]{1,0:T(8,128)}, f32[256,128]{1,0:T(8,128)}, f32[32,1536]{1,0:T(8,128)}, f32[48,2048]{1,0:T(8,128)}, bf16[2,384,1024]{2,1,0:T(8,12...) custom-call(bf16[2,2,2,2,256,1536]{5,4,3,2,1,0:T(8,128)(2,1)} %bitcast.126,, ...), custom_call_target="tpu_custom_call", output_to_operand_aliasing={{6}: (6, {})} | custom-call | flops 1024 | bytes 1024 | tf_op jit(solution)/shard_map/pallas_call | solution.py:1240
  725.9 1.6 fusion.61.normed_ref
  727.5 3.1 copy.146
  731.0 7.2 convolution_add_fusion.2
  742.7 1.7 copy-done.60
  744.4 6.9 multiply_reduce_fusion
  752.7 8.8 shard_map.355
  761.5 35.5 %shard_map.356 = (f32[3072,256]{1,0:T(8,128)}, bf16[3072,128]{1,0:T(8,128)(2,1)}, f32[48,256]{1,0:T(8,128)}, f32[48,256]{1,0:T(8,128)}, f32[256,256]{1,0:T(8,128)}) custom-call(bf16[3072,128]{1,0:T(8,128)(2,1)} %get-tuple-element.97.local_ref, f32[3072,8]{1,0:T(8,128)} %broadcast_in_dim.112.passed_ref, f32[3072,256]{1,0:T(8,128)} %get-tuple-element.76.pre_ref, ...), custom_call_target="tpu_custom_call" | custom-call | flops 35000000512 | bytes 1024 | tf_op jit(solution)/shard_map/pallas_call | solution.py:569
  797.1 18.6 %shard_map.357 = (bf16[3072,384]{1,0:T(8,128)(2,1)}, f32[3072,8]{1,0:T(8,128)}, f32[48,256]{1,0:T(8,128)}, f32[48,256]{1,0:T(8,128)}, f32[48,128]{1,0:T(8,128)}, /*index=5*/f32[256,256]{1,0:T(8,128)}) custom-call(f32[3072,256]{1,0:T(8,128)} %get-tuple-element.99.grad_in_ref, f32[3072,256]{1,0:T(8,128)} %get-tuple-element.98.grad_y_ref, ...), custom_call_target="tpu_custom_call" | custom-call | flops 19000000512 | bytes 1024 | tf_op jit(solution)/shard_map/pallas_call | solution.py:569
  815.7 1.7 add.276.grad_ref
  817.4 3.2 shard_map.358
  822.9 1.9 copy.155
  829.0 2.2 add_convert_fusion.1.refs_4_
  831.2 3.4 add_convert_fusion.refs_3_
  834.6 5.1 convolution_convert_fusion
  839.6 2.4 constant_dynamic-slice_fusion
  843.2 37.2 %shard_map.359 = (bf16[1536,6448]{1,0:T(8,128)(2,1)}, f32[1536,384]{1,0:T(8,128)}, bf16[256,1536]{1,0:T(8,128)(2,1)}) custom-call(bf16[1536,384]{1,0:T(8,128)(2,1)} %fusion.61.normed_ref, bf16[1536,6448]{1,0:T(8,128)(2,1)} %bitcast.168, bf16[3072,256]{1,0:T(8,128)(2,1)} %get-tuple-element.96.grad_z_ref, bf16[3072,384]{1,0:T(8,128)(2,1)} %get-tuple-element.102.grad_x_ref, ...), custom_call_target="tpu_custom_call" | custom-call | flops 27000000512 | bytes 1024 | tf_op jit(solution)/shard_map/pallas_call | solution.py:569
  880.4 2.3 copy.151
  882.7 3.1 fusion.66
  887.2 1.4 collective-permute-start
  888.7 4.6 fusion.3
  901.4 189.8 %shard_map.360 = (f32[48,6448]{1,0:T(8,128)}, f32[96,1536]{1,0:T(8,128)}, f32[24,128]{1,0:T(8,128)}, bf16[2,384,1024]{2,1,0:T(8,128)(2,1)}, bf16[2,512,384]{2,1,...) custom-call(bf16[2,2,2,4,48,6448]{5,4,3,2,1,0:T(8,128)(2,1)} %bitcast.121, ...), custom_call_target="tpu_custom_call" | custom-call | flops 1024 | bytes 1024 | tf_op jit(solution)/shard_map/pallas_call | solution.py:1240
  1096.7 1.7 fusion.9
  1098.4 3.1 copy.160
  1103.0 2.2 convert_add_fusion
  1105.1 1.4 convert_select_fusion.1
  1106.6 1.9 pad_maximum_fusion.2
  1109.7 2.0 pad_maximum_fusion.1
  1111.7 2.0 pad_maximum_fusion
  (284 shorter events, 64.0 us)
Async XLA Ops:
  7.2 564.2 %all-gather.4.cloned.1.call-start = ((), (), s32[]{:S(2)}) async-start(), calls=%async_computation.1 | async-start | bytes 6488064 | tf_op jit(solution)/shard_map/all_gather | solution.py:1732
  13.1 190.2 %copy-start.43 = (bf16[48,1024]{1,0:T(8,128)(2,1)S(1)}, bf16[48,1024]{1,0:T(8,128)(2,1)}, u32[]{:S(2)}) copy-start(bf16[48,1024]{1,0:T(8,128)(2,1)} %param.37) | copy-start | bytes 294916
  13.1 190.3 %copy-start.44 = (bf16[48,1024]{1,0:T(8,128)(2,1)S(1)}, bf16[48,1024]{1,0:T(8,128)(2,1)}, u32[]{:S(2)}) copy-start(bf16[48,1024]{1,0:T(8,128)(2,1)} %param.36) | copy-start | bytes 294916
  13.1 191.0 %copy-start.41 = (bf16[32,1536]{1,0:T(8,128)(2,1)S(1)}, bf16[32,1536]{1,0:T(8,128)(2,1)}, u32[]{:S(2)}) copy-start(bf16[32,1536]{1,0:T(8,128)(2,1)} %param.38) | copy-start | bytes 294916
  13.1 191.8 %copy-start.23 = (bf16[1,256,1536]{2,1,0:T(8,128)(2,1)S(1)}, bf16[1,256,1536]{2,1,0:T(8,128)(2,1)}, u32[]{:S(2)}) copy-start(bf16[1,256,1536]{2,1,0:T(8,128)(2,1)} %param.21) | copy-start | bytes 2359300
  201.4 3.8 copy-start.22
  204.1 373.4 %all-gather.6.cloned.1.call-start = ((), (), s32[]{:S(2)}) async-start(), calls=%async_computation.3 | async-start | bytes 3244032 | tf_op jit(solution)/shard_map/all_gather | solution.py:1735
  204.8 634.8 %reduce-scatter.2.cloned.1.call-start = ((), (), s32[]{:S(2)}) async-start(), calls=%async_computation.2 | async-start | bytes 14155776 | tf_op jit(solution)/shard_map/reduce_scatter | solution.py:1852
  210.6 18.0 %copy-start.51 = (f32[384]{0:T(512)}, f32[384]{0:T(512)S(1)}, u32[]{:S(2)}) copy-start(f32[384]{0:T(512)S(1)} %add_rsqrt_fusion) | copy-start | bytes 4612
  232.0 4.0 copy-start.34
  236.0 11.5 %copy-start.24 = (f32[48,256]{1,0:T(8,128)S(1)}, f32[48,256]{1,0:T(8,128)}, u32[]{:S(2)}) copy-start(f32[48,256]{1,0:T(8,128)} %fusion.24.cum_ref) | copy-start | bytes 147460
  236.0 13.0 %copy-start.57 = (f32[48]{0:T(128)S(1)}, f32[48]{0:T(128)}, u32[]{:S(2)}) copy-start(f32[48]{0:T(128)} %param.31) | copy-start | bytes 580
  247.5 6.2 copy-start.45
  253.7 34.7 %copy-start.53 = (s32[1,256,6]{1,0,2:T(1,128)S(1)}, s32[1,256,6]{1,0,2:T(1,128)}, u32[]{:S(2)}) copy-start(s32[1,256,6]{1,0,2:T(1,128)} %param.23) | copy-start | bytes 18436
  288.8 9.6 copy-start.8
  571.4 6.0 copy-start.6
  725.3 5.3 copy-start.49
  727.5 3.5 copy-start.31
  727.5 3.5 copy-start.33
  731.0 7.3 copy-start.1
  731.0 7.3 copy-start.9
  731.0 10.5 slice-start
  731.0 10.9 slice-start.1
  738.3 4.4 slice-start.2
  741.1 3.3 copy-start.60
  741.5 9.8 copy-start.3
  797.1 18.6 %copy-start.37 = (f32[256,256]{1,0:T(8,128)S(1)}, f32[256,256]{1,0:T(8,128)}, u32[]{:S(2)}) copy-start(f32[256,256]{1,0:T(8,128)} %get-tuple-element.103) | copy-start | bytes 786436
  821.0 4.9 copy-start.25
  821.0 4.9 copy-start.42
  821.9 4.1 copy-start.35
  821.9 4.1 copy-start.59
  821.9 4.1 copy-start.62
  821.9 4.1 copy-start.64
  821.9 4.1 copy-start.65
  822.0 4.1 copy-start.66
  822.0 4.1 copy-start.67
  822.8 4.5 copy-start.39
  822.9 5.3 copy-start.36
  824.8 4.1 copy-start.26
  831.2 3.4 copy-start.4
  831.2 3.4 copy-start.13
  882.7 5.9 copy-start.2
  882.7 5.9 copy-start.12
  887.2 6.0 copy-start.7
  887.2 9.7 collective-permute-start
  901.4 195.2 %copy-start.50 = (f32[256]{0:T(256)S(1)}, f32[256]{0:T(256)}, u32[]{:S(2)}) copy-start(f32[256]{0:T(256)} %copy-done.49) | copy-start | bytes 3076
  901.4 195.3 %copy-start.5 = (f32[256,1536]{0,1:T(8,128)S(1)}, f32[256,1536]{0,1:T(8,128)}, u32[]{:S(2)}) copy-start(f32[256,1536]{0,1:T(8,128)} %copy-done.3) | copy-start | bytes 4718596
  1098.4 4.6 copy-start.18
  (27 other events, 59.7 us)
Sparse Core Ops, SparseCore 0:
  204.2 74.8 all-gather.3
  282.6 76.0 all-gather.5
  723.2 93.1 reduce-scatter.1
